TPU v7x, 32 devices: a whole 2x2x4 slice. The times are simulated.
32 devices in a mesh: dp: 8 (over z, core), head: 4 (over y, x).
Axes of the slice: x: 2, y: 2, z: 4, core: 2. Of those that a mesh axis runs over, the one named last changes fastest.
Arguments:
- tokens: bfloat16 [4, 4096, 2048], P(None, ('dp', 'head')), may hold values from -6 to 6
- cotangent: bfloat16 [4, 4096, 2048], P(None, ('dp', 'head')), may hold values from -6 to 6
- token_counts: int32 [4, 8], P(None, 'dp'), may hold values from 1 to 512, 3072 in all within a row
- doc_lengths: int32 [4, 8, 4], P(None, 'dp'), may hold values from 1 to 256, 512 in all within a row
- norm_in: float32 [2048], replicated, may hold values from 0.5 to 1.5
- w_query: bfloat16 [2048, 2048], P(None, 'head'), may hold values from -0.125 to 0.125
- w_key: bfloat16 [2048, 2048], P(None, 'head'), may hold values from -0.125 to 0.125
- w_value: bfloat16 [2048, 2048], P(None, 'head'), may hold values from -0.125 to 0.125
- w_outgate: bfloat16 [2048, 2048], P(None, 'head'), may hold values from -0.125 to 0.125
- w_decay: bfloat16 [2048, 16], P(None, 'head'), may hold values from -0.125 to 0.125
- w_beta: bfloat16 [2048, 16], P(None, 'head'), may hold values from -0.125 to 0.125
- conv_weight: float32 [3, 4, 2048], P(None, None, 'head'), may hold values from -3 to 3
- decay_log: float32 [16], P('head'), may hold values from -6.9 to -3
- dt_bias: float32 [16], P('head'), may hold values from -1 to 1
- gain_out: float32 [2048], P('head'), may hold values from 0.5 to 1.5
- w_out: bfloat16 [2048, 2048], P('head'), may hold values from -0.25 to 0.25
- norm_mid: float32 [2048], replicated, may hold values from 0.5 to 1.5
- w_gate: bfloat16 [2048, 5632], P('dp', 'head'), may hold values from -0.125 to 0.125
- w_up: bfloat16 [2048, 5632], P('dp', 'head'), may hold values from -0.125 to 0.125
- w_down: bfloat16 [2048, 5632], P('dp', 'head'), may hold values from -0.15625 to 0.15625
Outputs:
- block_out: bfloat16 [4, 4096, 2048], P(None, ('dp', 'head'))
- grad_tokens: bfloat16 [4, 4096, 2048], P(None, ('dp', 'head'))
- grad_norm_in: float32 [2048], replicated
- grad_query: float32 [2048, 2048], P('dp', 'head')
- grad_key: float32 [2048, 2048], P('dp', 'head')
- grad_value: float32 [2048, 2048], P('dp', 'head')
- grad_outgate: float32 [2048, 2048], P('dp', 'head')
- grad_decay: float32 [2048, 16], P('dp', 'head')
- grad_beta: float32 [2048, 16], P('dp', 'head')
- grad_conv: float32 [3, 4, 2048], P(None, None, 'head')
- grad_decay_log: float32 [16], P('head')
- grad_dt_bias: float32 [16], P('head')
- grad_gain_out: float32 [2048], P('head')
- grad_out_proj: float32 [2048, 2048], P('head', 'dp')
- grad_norm_mid: float32 [2048], replicated
- grad_gate: float32 [2048, 5632], P('dp', 'head')
- grad_up: float32 [2048, 5632], P('dp', 'head')
- grad_down: float32 [2048, 5632], P('dp', 'head')
Inputs may be any that keep to these rules, and one draw needn't show every extreme that they name: `token_counts`: the counts of one micro-batch sum to three quarters of its 4096 slots, and one of them equals 512; slots from the count on are padding whose cotangent is dropped. `doc_lengths`: each buffer's lengths fill its 512 slots; one length of each buffer equals half of 512.
All inputs are finite; a program needn't handle non-finite values. No bound on the sum of `token_counts` on one device may be relied on, other than what follows from the above.
Results may differ from a plain program's by a relative error of at most 0.019.
Values may be sent and summed in bfloat16 or wider, within the bound.
A program may use at most 640 MiB of HBM per device.

v0:
```python
import jax
import jax.numpy as jnp
from jax import lax
from jax.sharding import PartitionSpec as P

HD = 128
GROUP = 64


HIGH = lax.Precision.HIGHEST


def norm_rows(values, gain):
    return values * lax.rsqrt(jnp.mean(values * values, axis=-1, keepdims=True) + 1e-05) * gain


def unit_rows(values):
    return values * lax.rsqrt(jnp.sum(values * values, axis=-1, keepdims=True) + 1e-06)


def swiglu(gate, upward):
    return jax.nn.silu(gate) * upward


def causal_conv(values, weight, segment):
    summed = values * weight[0]
    for offset in range(1, weight.shape[0]):
        earlier = jnp.pad(values, ((offset, 0), (0, 0)))[:-offset]
        earlier_segment = jnp.pad(segment, (offset, 0), constant_values=-1)[:-offset]
        summed = summed + earlier * weight[offset] * (earlier_segment == segment)[:, None].astype(
            jnp.float32
        )
    return summed


def block_step(state, block):
    query, key_vec, value, log_alpha, beta, segment, prior = block
    length = query.shape[0]
    row_ids = lax.broadcasted_iota(jnp.int32, (length, length), 0)
    col_ids = lax.broadcasted_iota(jnp.int32, (length, length), 1)
    same = segment[:, None] == segment[None, :]
    below = (row_ids >= col_ids) & same
    decay_sum = jnp.cumsum(log_alpha, axis=0).T
    spread = decay_sum[:, :, None] - decay_sum[:, None, :]
    inside = jnp.exp(jnp.where(below[None], spread, 0.0)) * below[None].astype(jnp.float32)
    strict_decay = inside * (row_ids > col_ids)[None].astype(jnp.float32)
    carried = (segment == prior).astype(jnp.float32)
    head_beta = beta.T
    growth = jnp.exp(decay_sum) * carried[None, :]
    keys_dot = jnp.einsum("ihk,jhk->hij", key_vec, key_vec, precision=HIGH)
    power = -(head_beta[:, :, None] * keys_dot * strict_decay)
    inverse = jnp.eye(length, dtype=jnp.float32)[None] + power
    for repeat in range(length.bit_length() - 2):
        power = jnp.einsum("hij,hjl->hil", power, power, precision=HIGH)
        inverse = inverse + jnp.einsum("hij,hjl->hil", inverse, power, precision=HIGH)
    pseudo = jnp.einsum("hij,jhv->hiv", inverse, value * beta[:, :, None], precision=HIGH)
    key_weights = jnp.einsum(
        "hij,jhk->hik", inverse, key_vec * (head_beta * growth).T[:, :, None], precision=HIGH
    )
    update = pseudo - jnp.einsum("hik,hvk->hiv", key_weights, state, precision=HIGH)
    query_dot = jnp.einsum("ihk,jhk->hij", query, key_vec, precision=HIGH)
    output = jnp.einsum("hvk,ihk->hiv", state, query * growth.T[:, :, None], precision=HIGH)
    output = output + jnp.einsum("hij,hjv->hiv", query_dot * inside, update, precision=HIGH)
    last_decay = decay_sum[:, -1:]
    tail = jnp.exp(last_decay - decay_sum) * (segment == segment[-1]).astype(jnp.float32)[None, :]
    state = state * (jnp.exp(last_decay) * carried[-1])[:, :, None]
    state = state + jnp.einsum("hjv,jhk->hvk", update, key_vec * tail.T[:, :, None], precision=HIGH)
    return (state, jnp.transpose(output, (1, 0, 2)))


def mixer(
    query_raw,
    key_raw,
    value_raw,
    outgate_raw,
    decay_raw,
    beta_raw,
    conv_weight,
    decay_log,
    dt_bias,
    gain_out,
    segment,
):
    length, width = query_raw.shape
    heads = width // HD
    query = unit_rows(
        jax.nn.silu(causal_conv(query_raw, conv_weight[0], segment)).reshape(length, heads, HD)
    ) * HD ** (-0.5)
    key_vec = unit_rows(
        jax.nn.silu(causal_conv(key_raw, conv_weight[1], segment)).reshape(length, heads, HD)
    )
    value = jax.nn.silu(causal_conv(value_raw, conv_weight[2], segment)).reshape(length, heads, HD)
    log_alpha = -jnp.exp(decay_log) * jax.nn.softplus(decay_raw + dt_bias)
    beta = jax.nn.sigmoid(beta_raw)
    prior = jnp.concatenate([jnp.full((1,), -1, jnp.int32), segment[:-1]])
    blocks = length // GROUP

    def split(values):
        return values.reshape((blocks, GROUP) + values.shape[1:])

    initial = jnp.zeros((heads, HD, HD), jnp.float32)
    final, core = lax.scan(
        block_step,
        initial,
        (
            split(query),
            split(key_vec),
            split(value),
            split(log_alpha),
            split(beta),
            split(segment),
            prior[::GROUP],
        ),
    )
    core = core.reshape(length, heads, HD)
    core = core * lax.rsqrt(jnp.mean(core * core, axis=-1, keepdims=True) + 1e-05)
    return core.reshape(length, width) * gain_out * jax.nn.silu(outgate_raw)


def contract_rows(left, right):
    return lax.dot_general(
        left, right, (((0,), (0,)), ((), ())), preferred_element_type=jnp.float32
    )


def contract_cols(left, right):
    return lax.dot_general(
        left, right, (((1,), (1,)), ((), ())), preferred_element_type=jnp.float32
    )


def share_sums(row_terms, out_term):
    row_shares = (
        lax.psum_scatter(
            row_terms[0].astype(jnp.bfloat16), "dp", scatter_dimension=0, tiled=True
        ).astype(jnp.float32),
        lax.psum_scatter(
            row_terms[1].astype(jnp.bfloat16), "dp", scatter_dimension=0, tiled=True
        ).astype(jnp.float32),
        lax.psum_scatter(
            row_terms[2].astype(jnp.bfloat16), "dp", scatter_dimension=0, tiled=True
        ).astype(jnp.float32),
        lax.psum_scatter(
            row_terms[3].astype(jnp.bfloat16), "dp", scatter_dimension=0, tiled=True
        ).astype(jnp.float32),
        lax.psum_scatter(
            row_terms[4].astype(jnp.bfloat16), "dp", scatter_dimension=0, tiled=True
        ).astype(jnp.float32),
        lax.psum_scatter(
            row_terms[5].astype(jnp.bfloat16), "dp", scatter_dimension=0, tiled=True
        ).astype(jnp.float32),
        lax.psum_scatter(
            row_terms[6].astype(jnp.bfloat16), "dp", scatter_dimension=0, tiled=True
        ).astype(jnp.float32),
        lax.psum_scatter(
            row_terms[7].astype(jnp.bfloat16), "dp", scatter_dimension=0, tiled=True
        ).astype(jnp.float32),
        lax.psum_scatter(
            row_terms[8].astype(jnp.bfloat16), "dp", scatter_dimension=0, tiled=True
        ).astype(jnp.float32),
    )
    out_share = lax.psum_scatter(
        out_term.astype(jnp.bfloat16), "dp", scatter_dimension=1, tiled=True
    ).astype(jnp.float32)
    return (tuple(row_shares), out_share)


def on_device(
    tokens,
    cotangent,
    token_counts,
    doc_lengths,
    norm_in,
    w_query,
    w_key,
    w_value,
    w_outgate,
    w_decay,
    w_beta,
    conv_weight,
    decay_log,
    dt_bias,
    gain_out,
    w_out,
    norm_mid,
    w_gate,
    w_up,
    w_down,
):
    micro_count, rows, width = tokens.shape
    span = rows * lax.axis_size("head")
    my_places = lax.axis_index("head") * rows + lax.iota(jnp.int32, rows)
    places = lax.iota(jnp.int32, span)
    ffn_gate, ffn_up, ffn_down = (
        lax.all_gather(w_gate, "dp", axis=0, tiled=True),
        lax.all_gather(w_up, "dp", axis=0, tiled=True),
        lax.all_gather(w_down, "dp", axis=0, tiled=True),
    )
    projections = (w_query, w_key, w_value, w_outgate, w_decay, w_beta)
    share_rows = None
    share_out = None
    gain_first = jnp.zeros_like(norm_in)
    gain_second = jnp.zeros_like(norm_mid)
    mixer_params = (
        jnp.zeros_like(conv_weight),
        jnp.zeros_like(decay_log),
        jnp.zeros_like(dt_bias),
        jnp.zeros_like(gain_out),
    )
    results = []
    input_grads = []
    for micro_index in range(micro_count):
        inputs = tokens[micro_index].astype(jnp.float32)
        ends = jnp.cumsum(doc_lengths[micro_index, 0])
        segment = jnp.sum((places[:, None] >= ends[None, :]).astype(jnp.int32), axis=1)
        live = (my_places < token_counts[micro_index, 0]).astype(jnp.float32)
        normed_in, first_pull = jax.vjp(norm_rows, inputs, norm_in)
        full_in = lax.all_gather(normed_in.astype(jnp.bfloat16), "head", axis=0, tiled=True)
        raw_parts = tuple(
            (jnp.dot(full_in, weight, preferred_element_type=jnp.float32) for weight in projections)
        )
        mixed, mixer_pull = jax.vjp(
            lambda *inputs_all: mixer(*inputs_all, segment),
            *raw_parts,
            conv_weight,
            decay_log,
            dt_bias,
            gain_out
        )
        mixed_low = mixed.astype(jnp.bfloat16)
        attn = lax.psum_scatter(
            jnp.dot(mixed_low, w_out, preferred_element_type=jnp.float32),
            "head",
            scatter_dimension=0,
            tiled=True,
        )
        resid = inputs + attn
        normed_mid, second_pull = jax.vjp(norm_rows, resid, norm_mid)
        full_mid = lax.all_gather(normed_mid.astype(jnp.bfloat16), "head", axis=0, tiled=True)
        gate = jnp.dot(full_mid, ffn_gate, preferred_element_type=jnp.float32)
        upward = jnp.dot(full_mid, ffn_up, preferred_element_type=jnp.float32)
        act_full, act_pull = jax.vjp(swiglu, gate, upward)
        act = act_full.astype(jnp.bfloat16)
        ffn = lax.psum_scatter(
            contract_cols(act, ffn_down).astype(jnp.bfloat16),
            "head",
            scatter_dimension=0,
            tiled=True,
        ).astype(jnp.float32)
        results.append((resid + ffn).astype(jnp.bfloat16))
        grad_out = cotangent[micro_index].astype(jnp.float32) * live[:, None]
        full_grad = lax.all_gather(grad_out.astype(jnp.bfloat16), "head", axis=0, tiled=True)
        grad_act = jnp.dot(full_grad, ffn_down, preferred_element_type=jnp.float32)
        grad_down = contract_rows(full_grad, act)
        grad_gate_f, grad_up_f = act_pull(grad_act)
        grad_gate_low = grad_gate_f.astype(jnp.bfloat16)
        grad_up_low = grad_up_f.astype(jnp.bfloat16)
        grad_gate_w = contract_rows(full_mid, grad_gate_low)
        grad_up_w = contract_rows(full_mid, grad_up_low)
        part_gate = contract_cols(grad_gate_low, ffn_gate)
        grad_mid = lax.psum_scatter(
            (part_gate + contract_cols(grad_up_low, ffn_up)).astype(jnp.bfloat16),
            "head",
            scatter_dimension=0,
            tiled=True,
        ).astype(jnp.float32)
        grad_resid_norm, grad_norm_mid = second_pull(grad_mid)
        grad_resid = grad_out + grad_resid_norm
        full_resid_grad = lax.all_gather(
            grad_resid.astype(jnp.bfloat16), "head", axis=0, tiled=True
        )
        grad_mixed = contract_cols(full_resid_grad, w_out)
        grad_out_w = contract_rows(mixed_low, full_resid_grad)
        mixer_grads = mixer_pull(grad_mixed)
        raw_grads = tuple((item.astype(jnp.bfloat16) for item in mixer_grads[:6]))
        proj_grads = [contract_rows(full_in, item) for item in raw_grads]
        summed = jnp.zeros((lax.axis_size("head") * rows, width), jnp.float32)
        for grad_item, input_weight in zip(raw_grads, projections):
            summed = summed + contract_cols(grad_item, input_weight)
        grad_normed = lax.psum_scatter(
            summed.astype(jnp.bfloat16), "head", scatter_dimension=0, tiled=True
        ).astype(jnp.float32)
        grad_inputs, grad_norm_in = first_pull(grad_normed)
        input_grads.append((grad_inputs + grad_resid).astype(jnp.bfloat16))
        gain_first = gain_first + grad_norm_in
        gain_second = gain_second + grad_norm_mid
        mixer_params = tuple((total + item for total, item in zip(mixer_params, mixer_grads[6:])))
        new_rows = proj_grads + [grad_gate_w, grad_up_w, grad_down]
        row_part, out_part = share_sums(new_rows, grad_out_w)
        if share_rows is None:
            share_rows, share_out = (row_part, out_part)
        else:
            share_rows = tuple((total + item for total, item in zip(share_rows, row_part)))
            share_out = share_out + out_part
    gain_sums = lax.psum((gain_first, gain_second), ("dp", "head"))
    param_sums = lax.psum(
        (mixer_params[0], mixer_params[1], mixer_params[2], mixer_params[3]), "dp"
    )
    return (
        jnp.stack(results),
        jnp.stack(input_grads),
        gain_sums[0],
        share_rows[0],
        share_rows[1],
        share_rows[2],
        share_rows[3],
        share_rows[4],
        share_rows[5],
        param_sums[0],
        param_sums[1],
        param_sums[2],
        param_sums[3],
        share_out,
        gain_sums[1],
        share_rows[6],
        share_rows[7],
        share_rows[8],
    )


def solution(mesh):
    return jax.shard_map(
        on_device,
        mesh=mesh,
        in_specs=(
            P(None, ("dp", "head"), None),
            P(None, ("dp", "head"), None),
            P(None, "dp"),
            P(None, "dp", None),
            P(),
            P(None, "head"),
            P(None, "head"),
            P(None, "head"),
            P(None, "head"),
            P(None, "head"),
            P(None, "head"),
            P(None, None, "head"),
            P("head"),
            P("head"),
            P("head"),
            P("head", None),
            P(),
            P("dp", "head"),
            P("dp", "head"),
            P("dp", "head"),
        ),
        out_specs=(
            P(None, ("dp", "head"), None),
            P(None, ("dp", "head"), None),
            P(),
            P("dp", "head"),
            P("dp", "head"),
            P("dp", "head"),
            P("dp", "head"),
            P("dp", "head"),
            P("dp", "head"),
            P(None, None, "head"),
            P("head"),
            P("head"),
            P("head"),
            P("head", "dp"),
            P(),
            P("dp", "head"),
            P("dp", "head"),
            P("dp", "head"),
        ),
        check_vma=False,
    )
```

profile of v0, /device:TPU:0, one launch (start us, length us, event | category | flops | bytes accessed | tf_op | source)
XLA Modules:
  0.0 7386.4 jit_solution(4161739373595897981)
XLA Ops:
  22.3 28.6 all-gather.20.cloned.1.call-done
  54.4 34.3 all-gather.30.cloned.1.call-done
  128.7 35.4 all-gather.38.cloned.1.call-done
  230.5 454.4 %while.500 = (s32[]{:T(128)}, f32[4,128,128]{2,1,0:T(8,128)}, f32[8,64,4,128]{3,1,2,0:T(8,128)}, pred[8,4,64,64]{3,2,1,0:T(32,128)(4,1)}, f32[8,4,64,64]{3,2,1,0...) while((s32[]{:T(128)}, f32[4,128,128]{2,1,0:T(8,128)}, ...), condition=%wide.region_7.9_spmd.clone.clone, body=%wide.region_5.8_spmd.clone.clone.sunk | while | flops 404048704 | bytes 13630506 | solution.py:102
  756.0 454.4 %while.501 = (s32[]{:T(128)}, f32[4,128,128]{2,1,0:T(8,128)}, f32[8,64,4,128]{3,1,2,0:T(8,128)}, pred[8,4,64,64]{3,2,1,0:T(32,128)(4,1)}, f32[8,4,64,64]{3,2,1,0...) while((s32[]{:T(128)}, f32[4,128,128]{2,1,0:T(8,128)}, ...), condition=%wide.region_19.21_spmd.clone.clone, body=%wide.region_17.20_spmd.clone.clone.sunk | while | flops 404048704 | bytes 13630506 | solution.py:102
  1302.1 456.5 %while.502 = (s32[]{:T(128)}, f32[4,128,128]{2,1,0:T(8,128)}, f32[8,64,4,128]{3,1,2,0:T(8,128)}, pred[8,4,64,64]{3,2,1,0:T(32,128)(4,1)}, f32[8,4,64,64]{3,2,1,0...) while((s32[]{:T(128)}, f32[4,128,128]{2,1,0:T(8,128)}, ...), condition=%wide.region_31.33_spmd.clone.clone, body=%wide.region_29.32_spmd.clone.clone.sunk | while | flops 404048704 | bytes 13630506 | solution.py:102
  1829.8 457.4 %while.503 = (s32[]{:T(128)}, f32[4,128,128]{2,1,0:T(8,128)}, f32[8,64,4,128]{3,1,2,0:T(8,128)}, pred[8,4,64,64]{3,2,1,0:T(32,128)(4,1)}, f32[8,4,64,64]{3,2,1,0...) while((s32[]{:T(128)}, f32[4,128,128]{2,1,0:T(8,128)}, ...), condition=%wide.region_43.45_spmd.clone.clone, body=%wide.region_41.44_spmd.clone.clone.sunk | while | flops 404048704 | bytes 13630506 | solution.py:102
  2326.3 41.1 reduce-scatter.73.cloned.1.call-done
  2367.4 55.8 reduce-scatter.81.cloned.1.call-done
  2423.3 55.7 reduce-scatter.85.cloned.1.call-done
  2479.0 56.0 reduce-scatter.77.cloned.1.call-done
  2546.5 30.3 all-gather.40.cloned.1.call-done
  2585.1 53.5 all-gather.26.cloned.1.call-done
  2647.0 27.9 all-gather.54.cloned.1.call-done
  2674.9 62.0 all-gather.28.cloned.1.call-done
  2768.8 23.6 reduce-scatter.101.cloned.1.call-done
  2795.5 35.0 reduce-scatter.87.cloned.1.call-done
  2839.3 32.0 all-gather.36.cloned.1.call-done
  2887.7 21.0 all-gather.50.cloned.1.call-done
  2963.2 20.9 all-gather.42.cloned.1.call-done
  3038.1 20.8 all-gather.46.cloned.1.call-done
  3083.9 34.7 reduce-scatter.93.cloned.1.call-done
  3130.5 25.9 all-gather.56.cloned.1.call-done
  3172.1 499.8 %while.499 = (s32[]{:T(128)}, f32[4,128,128]{2,1,0:T(8,128)}, f32[8,64,4,128]{3,1,2,0:T(8,128)}, f32[8,64,4,128]{3,1,2,0:T(8,128)}, f32[8,64,4,128]{3,2,1,0:T(4,...) while((s32[]{:T(128)}, f32[4,128,128]{2,1,0:T(8,128)}, ...), condition=%wide.region_119.121_spmd.clone, body=%wide.region_108.120_spmd.clone.sunk | while | flops 807152128 | bytes 18728172 | solution.py:102
  3718.2 500.2 %while.498 = (s32[]{:T(128)}, f32[4,128,128]{2,1,0:T(8,128)}, f32[8,64,4,128]{3,1,2,0:T(8,128)}, f32[8,64,4,128]{3,1,2,0:T(8,128)}, f32[8,64,4,128]{3,2,1,0:T(4,...) while((s32[]{:T(128)}, f32[4,128,128]{2,1,0:T(8,128)}, ...), condition=%wide.region_100.102_spmd.clone, body=%wide.region_89.101_spmd.clone.sunk | while | flops 807152128 | bytes 18728172 | solution.py:102
  4241.0 500.0 %while.496 = (s32[]{:T(128)}, f32[4,128,128]{2,1,0:T(8,128)}, f32[8,64,4,128]{3,1,2,0:T(8,128)}, f32[8,64,4,128]{3,1,2,0:T(8,128)}, f32[8,64,4,128]{3,2,1,0:T(4,...) while((s32[]{:T(128)}, f32[4,128,128]{2,1,0:T(8,128)}, ...), condition=%wide.region_62.64_spmd.clone, body=%wide.region_51.63_spmd.clone.sunk | while | flops 807152128 | bytes 18728172 | solution.py:102
  4763.6 499.8 %while.497 = (s32[]{:T(128)}, f32[4,128,128]{2,1,0:T(8,128)}, f32[8,64,4,128]{3,1,2,0:T(8,128)}, f32[8,64,4,128]{3,1,2,0:T(8,128)}, f32[8,64,4,128]{3,2,1,0:T(4,...) while((s32[]{:T(128)}, f32[4,128,128]{2,1,0:T(8,128)}, ...), condition=%wide.region_81.83_spmd.clone, body=%wide.region_70.82_spmd.clone.sunk | while | flops 807152128 | bytes 18728172 | solution.py:102
  5669.1 29.6 all-reduce.149
  5706.6 34.9 reduce-scatter.91.cloned.1.call-done
  5745.2 40.1 all-reduce.148
  5785.5 31.1 reduce-scatter.109.cloned.1.call-done
  5816.5 36.5 reduce-scatter.107.cloned.1.call-done
  5853.0 36.6 reduce-scatter.105.cloned.1.call-done
  5891.8 34.6 reduce-scatter.119.cloned.1.call-done
  5926.4 36.6 reduce-scatter.117.cloned.1.call-done
  5963.0 36.7 reduce-scatter.115.cloned.1.call-done
  5999.6 36.7 reduce-scatter.113.cloned.1.call-done
  6038.5 34.5 reduce-scatter.127.cloned.1.call-done
  6073.0 36.6 reduce-scatter.125.cloned.1.call-done
  6109.6 36.7 reduce-scatter.123.cloned.1.call-done
  6146.3 36.7 reduce-scatter.121.cloned.1.call-done
  6185.1 34.4 reduce-scatter.135.cloned.1.call-done
  6219.6 36.6 reduce-scatter.133.cloned.1.call-done
  6256.2 36.7 reduce-scatter.131.cloned.1.call-done
  6292.9 36.5 reduce-scatter.129.cloned.1.call-done
  6331.4 34.5 reduce-scatter.143.cloned.1.call-done
  6365.9 36.7 reduce-scatter.141.cloned.1.call-done
  6402.6 36.6 reduce-scatter.139.cloned.1.call-done
  6439.3 36.8 reduce-scatter.137.cloned.1.call-done
  6478.1 35.0 reduce-scatter.83.cloned.1.call-done
  6516.6 34.6 reduce-scatter.79.cloned.1.call-done
  6554.9 34.6 reduce-scatter.75.cloned.1.call-done
  6598.0 58.6 reduce-scatter.151.cloned.1.call-done
  6656.5 65.3 reduce-scatter.149.cloned.1.call-done
  6721.9 65.5 reduce-scatter.147.cloned.1.call-done
  6787.3 65.3 reduce-scatter.145.cloned.1.call-done
  6855.8 62.3 reduce-scatter.159.cloned.1.call-done
  6918.1 65.3 reduce-scatter.157.cloned.1.call-done
  6983.5 65.3 reduce-scatter.155.cloned.1.call-done
  7048.8 65.3 reduce-scatter.153.cloned.1.call-done
  7117.3 62.3 reduce-scatter.167.cloned.1.call-done
  7179.6 65.5 reduce-scatter.165.cloned.1.call-done
  7245.0 65.5 reduce-scatter.163.cloned.1.call-done
  7310.5 65.3 reduce-scatter.161.cloned.1.call-done
  (6567 shorter events, 4991.6 us)
Async XLA Ops:
  14.2 149.9 %all-gather.38.cloned.1.call-start = ((), (), s32[]{:S(2)}) async-start(), calls=%async_computation.71 | async-start | bytes 2621440 | tf_op jit(solution)/shard_map/all_gather | solution.py:218
  14.8 2352.7 %reduce-scatter.73.cloned.1.call-start = ((), (), s32[]{:S(2)}) async-start(), calls=%async_computation.57 | async-start | bytes 5242880 | tf_op jit(solution)/shard_map/reduce_scatter | solution.py:231
  2317.9 161.0 %reduce-scatter.85.cloned.1.call-start = ((), (), s32[]{:S(2)}) async-start(), calls=%async_computation.72 | async-start | bytes 5242880 | tf_op jit(solution)/shard_map/reduce_scatter | solution.py:231
  2322.3 212.6 %reduce-scatter.77.cloned.1.call-start = ((), (), s32[]{:S(2)}) async-start(), calls=%async_computation.64 | async-start | bytes 5242880 | tf_op jit(solution)/shard_map/reduce_scatter | solution.py:231
  2325.7 220.8 %all-gather.24.cloned.1.call-start = ((), (), s32[]{:S(2)}) async-start(), calls=%async_computation.59 | async-start | bytes 6488064 | tf_op jit(solution)/shard_map/all_gather | solution.py:195
  2326.3 250.5 %all-gather.40.cloned.1.call-start = ((), (), s32[]{:S(2)}) async-start(), calls=%async_computation.73 | async-start | bytes 2621440 | tf_op jit(solution)/shard_map/all_gather | solution.py:239
  2542.1 132.8 %all-gather.54.cloned.1.call-start = ((), (), s32[]{:S(2)}) async-start(), calls=%async_computation.87 | async-start | bytes 2621440 | tf_op jit(solution)/shard_map/all_gather | solution.py:252
  2545.4 191.4 %all-gather.28.cloned.1.call-start = ((), (), s32[]{:S(2)}) async-start(), calls=%async_computation.61 | async-start | bytes 6488064 | tf_op jit(solution)/shard_map/all_gather | solution.py:197
  2546.2 246.1 %reduce-scatter.101.cloned.1.call-start = ((), (), s32[]{:S(2)}) async-start(), calls=%async_computation.88 | async-start | bytes 2621440 | tf_op jit(solution)/shard_map/reduce_scatter | solution.py:261
  2837.3 146.8 %all-gather.42.cloned.1.call-start = ((), (), s32[]{:S(2)}) async-start(), calls=%async_computation.75 | async-start | bytes 2621440 | tf_op jit(solution)/shard_map/all_gather | solution.py:252
  2837.9 183.6 %all-gather.32.cloned.1.call-start = ((), (), s32[]{:S(2)}) async-start(), calls=%async_computation.65 | async-start | bytes 2621440 | tf_op jit(solution)/shard_map/all_gather | solution.py:239
  2838.6 220.3 %all-gather.46.cloned.1.call-start = ((), (), s32[]{:S(2)}) async-start(), calls=%async_computation.79 | async-start | bytes 2621440 | tf_op jit(solution)/shard_map/all_gather | solution.py:252
  2839.2 244.7 %reduce-scatter.97.cloned.1.call-start = ((), (), s32[]{:S(2)}) async-start(), calls=%async_computation.84 | async-start | bytes 2621440 | tf_op jit(solution)/shard_map/reduce_scatter | solution.py:261
  2932.9 151.0 %reduce-scatter.89.cloned.1.call-start = ((), (), s32[]{:S(2)}) async-start(), calls=%async_computation.76 | async-start | bytes 2621440 | tf_op jit(solution)/shard_map/reduce_scatter | solution.py:261
  3083.8 618.5 %all-gather.52.cloned.1.call-start = ((), (), s32[]{:S(2)}) async-start(), calls=%async_computation.85 | async-start | bytes 2621440 | tf_op jit(solution)/shard_map/all_gather | solution.py:269
  3125.9 1099.4 %all-gather.44.cloned.1.call-start = ((), (), s32[]{:S(2)}) async-start(), calls=%async_computation.77 | async-start | bytes 2621440 | tf_op jit(solution)/shard_map/all_gather | solution.py:269
  3126.5 1621.5 %all-gather.48.cloned.1.call-start = ((), (), s32[]{:S(2)}) async-start(), calls=%async_computation.81 | async-start | bytes 2621440 | tf_op jit(solution)/shard_map/all_gather | solution.py:269
  3168.0 2494.9 %reduce-scatter.183.cloned.1.call-start = ((), (), s32[]{:S(2)}) async-start(), calls=%async_computation.130 | async-start | bytes 589824
  3687.0 2011.7 %reduce-scatter.175.cloned.1.call-start = ((), (), s32[]{:S(2)}) async-start(), calls=%async_computation.126 | async-start | bytes 589824
  5371.1 328.5 %reduce-scatter.173.cloned.1.call-start = ((), (), s32[]{:S(2)}) async-start(), calls=%async_computation.125 | async-start | bytes 589824
  5374.2 326.4 %reduce-scatter.171.cloned.1.call-start = ((), (), s32[]{:S(2)}) async-start(), calls=%async_computation.124 | async-start | bytes 589824
  5377.4 324.1 %reduce-scatter.169.cloned.1.call-start = ((), (), s32[]{:S(2)}) async-start(), calls=%async_computation.123 | async-start | bytes 589824
  5380.6 321.8 %reduce-scatter.181.cloned.1.call-start = ((), (), s32[]{:S(2)}) async-start(), calls=%async_computation.129 | async-start | bytes 589824
  5383.9 319.5 %reduce-scatter.179.cloned.1.call-start = ((), (), s32[]{:S(2)}) async-start(), calls=%async_computation.128 | async-start | bytes 589824
  5387.0 317.3 %reduce-scatter.177.cloned.1.call-start = ((), (), s32[]{:S(2)}) async-start(), calls=%async_computation.127 | async-start | bytes 589824
  5390.1 316.4 %reduce-scatter.99.cloned.1.call-start = ((), (), s32[]{:S(2)}) async-start(), calls=%async_computation.86 | async-start | bytes 2621440 | tf_op jit(solution)/shard_map/reduce_scatter | solution.py:280
  5399.8 306.7 %reduce-scatter.103.cloned.1.call-start = ((), (), s32[]{:S(2)}) async-start(), calls=%async_computation.90 | async-start | bytes 2621440 | tf_op jit(solution)/shard_map/reduce_scatter | solution.py:280
  5412.0 294.5 %reduce-scatter.95.cloned.1.call-start = ((), (), s32[]{:S(2)}) async-start(), calls=%async_computation.82 | async-start | bytes 2621440 | tf_op jit(solution)/shard_map/reduce_scatter | solution.py:280
  5422.8 318.7 %reduce-scatter.91.cloned.1.call-start = ((), (), s32[]{:S(2)}) async-start(), calls=%async_computation.78 | async-start | bytes 2621440 | tf_op jit(solution)/shard_map/reduce_scatter | solution.py:280
  5433.7 351.7 %reduce-scatter.111.cloned.1.call-start = ((), (), s32[]{:S(2)}) async-start(), calls=%async_computation.94 | async-start | bytes 2359296 | tf_op jit(solution)/shard_map/reduce_scatter | solution.py:134
  5438.0 378.5 %reduce-scatter.109.cloned.1.call-start = ((), (), s32[]{:S(2)}) async-start(), calls=%async_computation.93 | async-start | bytes 2359296 | tf_op jit(solution)/shard_map/reduce_scatter | solution.py:134
  5442.4 410.6 %reduce-scatter.107.cloned.1.call-start = ((), (), s32[]{:S(2)}) async-start(), calls=%async_computation.92 | async-start | bytes 2359296 | tf_op jit(solution)/shard_map/reduce_scatter | solution.py:134
  5446.7 442.9 %reduce-scatter.105.cloned.1.call-start = ((), (), s32[]{:S(2)}) async-start(), calls=%async_computation.91 | async-start | bytes 2359296 | tf_op jit(solution)/shard_map/reduce_scatter | solution.py:134
  5451.1 475.2 %reduce-scatter.119.cloned.1.call-start = ((), (), s32[]{:S(2)}) async-start(), calls=%async_computation.98 | async-start | bytes 2359296 | tf_op jit(solution)/shard_map/reduce_scatter | solution.py:137
  5455.6 507.4 %reduce-scatter.117.cloned.1.call-start = ((), (), s32[]{:S(2)}) async-start(), calls=%async_computation.97 | async-start | bytes 2359296 | tf_op jit(solution)/shard_map/reduce_scatter | solution.py:137
  5460.4 539.2 %reduce-scatter.115.cloned.1.call-start = ((), (), s32[]{:S(2)}) async-start(), calls=%async_computation.96 | async-start | bytes 2359296 | tf_op jit(solution)/shard_map/reduce_scatter | solution.py:137
  5464.8 571.6 %reduce-scatter.113.cloned.1.call-start = ((), (), s32[]{:S(2)}) async-start(), calls=%async_computation.95 | async-start | bytes 2359296 | tf_op jit(solution)/shard_map/reduce_scatter | solution.py:137
  5469.2 603.8 %reduce-scatter.127.cloned.1.call-start = ((), (), s32[]{:S(2)}) async-start(), calls=%async_computation.102 | async-start | bytes 2359296 | tf_op jit(solution)/shard_map/reduce_scatter | solution.py:140
  5473.7 635.9 %reduce-scatter.125.cloned.1.call-start = ((), (), s32[]{:S(2)}) async-start(), calls=%async_computation.101 | async-start | bytes 2359296 | tf_op jit(solution)/shard_map/reduce_scatter | solution.py:140
  5478.1 668.2 %reduce-scatter.123.cloned.1.call-start = ((), (), s32[]{:S(2)}) async-start(), calls=%async_computation.100 | async-start | bytes 2359296 | tf_op jit(solution)/shard_map/reduce_scatter | solution.py:140
  5482.4 700.6 %reduce-scatter.121.cloned.1.call-start = ((), (), s32[]{:S(2)}) async-start(), calls=%async_computation.99 | async-start | bytes 2359296 | tf_op jit(solution)/shard_map/reduce_scatter | solution.py:140
  5486.7 732.9 %reduce-scatter.135.cloned.1.call-start = ((), (), s32[]{:S(2)}) async-start(), calls=%async_computation.106 | async-start | bytes 2359296 | tf_op jit(solution)/shard_map/reduce_scatter | solution.py:143
  5492.0 764.2 %reduce-scatter.133.cloned.1.call-start = ((), (), s32[]{:S(2)}) async-start(), calls=%async_computation.105 | async-start | bytes 2359296 | tf_op jit(solution)/shard_map/reduce_scatter | solution.py:143
  5497.2 795.6 %reduce-scatter.131.cloned.1.call-start = ((), (), s32[]{:S(2)}) async-start(), calls=%async_computation.104 | async-start | bytes 2359296 | tf_op jit(solution)/shard_map/reduce_scatter | solution.py:143
  5502.4 826.9 %reduce-scatter.129.cloned.1.call-start = ((), (), s32[]{:S(2)}) async-start(), calls=%async_computation.103 | async-start | bytes 2359296 | tf_op jit(solution)/shard_map/reduce_scatter | solution.py:143
  5507.7 858.2 %reduce-scatter.143.cloned.1.call-start = ((), (), s32[]{:S(2)}) async-start(), calls=%async_computation.110 | async-start | bytes 2359296 | tf_op jit(solution)/shard_map/reduce_scatter | solution.py:162
  5513.0 889.6 %reduce-scatter.141.cloned.1.call-start = ((), (), s32[]{:S(2)}) async-start(), calls=%async_computation.109 | async-start | bytes 2359296 | tf_op jit(solution)/shard_map/reduce_scatter | solution.py:162
  5518.2 921.0 %reduce-scatter.139.cloned.1.call-start = ((), (), s32[]{:S(2)}) async-start(), calls=%async_computation.108 | async-start | bytes 2359296 | tf_op jit(solution)/shard_map/reduce_scatter | solution.py:162
  5523.5 952.6 %reduce-scatter.137.cloned.1.call-start = ((), (), s32[]{:S(2)}) async-start(), calls=%async_computation.107 | async-start | bytes 2359296 | tf_op jit(solution)/shard_map/reduce_scatter | solution.py:162
  5528.7 984.4 %reduce-scatter.83.cloned.1.call-start = ((), (), s32[]{:S(2)}) async-start(), calls=%async_computation.70 | async-start | bytes 2621440 | tf_op jit(solution)/shard_map/reduce_scatter | solution.py:244
  5537.3 1013.9 %reduce-scatter.79.cloned.1.call-start = ((), (), s32[]{:S(2)}) async-start(), calls=%async_computation.66 | async-start | bytes 2621440 | tf_op jit(solution)/shard_map/reduce_scatter | solution.py:244
  5546.0 1043.5 %reduce-scatter.75.cloned.1.call-start = ((), (), s32[]{:S(2)}) async-start(), calls=%async_computation.62 | async-start | bytes 2621440 | tf_op jit(solution)/shard_map/reduce_scatter | solution.py:244
  5554.7 1101.9 %reduce-scatter.151.cloned.1.call-start = ((), (), s32[]{:S(2)}) async-start(), calls=%async_computation.114 | async-start | bytes 6488064 | tf_op jit(solution)/shard_map/reduce_scatter | solution.py:152
  5563.7 1158.2 %reduce-scatter.149.cloned.1.call-start = ((), (), s32[]{:S(2)}) async-start(), calls=%async_computation.113 | async-start | bytes 6488064 | tf_op jit(solution)/shard_map/reduce_scatter | solution.py:152
  5572.5 1214.8 %reduce-scatter.147.cloned.1.call-start = ((), (), s32[]{:S(2)}) async-start(), calls=%async_computation.112 | async-start | bytes 6488064 | tf_op jit(solution)/shard_map/reduce_scatter | solution.py:152
  5581.3 1271.3 %reduce-scatter.145.cloned.1.call-start = ((), (), s32[]{:S(2)}) async-start(), calls=%async_computation.111 | async-start | bytes 6488064 | tf_op jit(solution)/shard_map/reduce_scatter | solution.py:152
  5590.3 1327.9 %reduce-scatter.159.cloned.1.call-start = ((), (), s32[]{:S(2)}) async-start(), calls=%async_computation.118 | async-start | bytes 6488064 | tf_op jit(solution)/shard_map/reduce_scatter | solution.py:155
  5599.2 1384.3 %reduce-scatter.157.cloned.1.call-start = ((), (), s32[]{:S(2)}) async-start(), calls=%async_computation.117 | async-start | bytes 6488064 | tf_op jit(solution)/shard_map/reduce_scatter | solution.py:155
  5608.2 1440.6 %reduce-scatter.155.cloned.1.call-start = ((), (), s32[]{:S(2)}) async-start(), calls=%async_computation.116 | async-start | bytes 6488064 | tf_op jit(solution)/shard_map/reduce_scatter | solution.py:155
  5617.2 1496.9 %reduce-scatter.153.cloned.1.call-start = ((), (), s32[]{:S(2)}) async-start(), calls=%async_computation.115 | async-start | bytes 6488064 | tf_op jit(solution)/shard_map/reduce_scatter | solution.py:155
  5626.4 1553.2 %reduce-scatter.167.cloned.1.call-start = ((), (), s32[]{:S(2)}) async-start(), calls=%async_computation.122 | async-start | bytes 6488064 | tf_op jit(solution)/shard_map/reduce_scatter | solution.py:158
  5635.3 1609.8 %reduce-scatter.165.cloned.1.call-start = ((), (), s32[]{:S(2)}) async-start(), calls=%async_computation.121 | async-start | bytes 6488064 | tf_op jit(solution)/shard_map/reduce_scatter | solution.py:158
  5644.2 1666.4 %reduce-scatter.163.cloned.1.call-start = ((), (), s32[]{:S(2)}) async-start(), calls=%async_computation.120 | async-start | bytes 6488064 | tf_op jit(solution)/shard_map/reduce_scatter | solution.py:158
  5653.2 1722.7 %reduce-scatter.161.cloned.1.call-start = ((), (), s32[]{:S(2)}) async-start(), calls=%async_computation.119 | async-start | bytes 6488064 | tf_op jit(solution)/shard_map/reduce_scatter | solution.py:158
  (904 other events, 18326.1 us)
Sparse Core Ops, SparseCore 0:
  12.8 38.0 all-gather.19
  53.3 35.2 all-gather.29
  91.1 35.2 all-gather.33
  128.7 35.2 all-gather.37
  2314.7 52.6 reduce-scatter.72
  2370.5 52.6 reduce-scatter.80
  2426.2 52.6 reduce-scatter.84
  2482.2 52.6 reduce-scatter.76
  2933.0 39.6 reduce-scatter.96
  3008.4 39.0 reduce-scatter.88
  3083.4 35.1 reduce-scatter.92
  3121.0 35.3 all-gather.55
  3158.8 35.3 all-gather.51
  3196.4 35.3 all-gather.43
  3233.5 35.3 all-gather.47
Sparse Core Ops, SparseCore 1:
  2327.8 60.2 all-gather.23
  2541.6 35.1 all-gather.39
  2578.3 60.2 all-gather.25
  2641.0 33.8 all-gather.53
  2676.5 60.2 all-gather.27
  2758.5 33.7 reduce-scatter.100
  2795.4 35.0 reduce-scatter.86
  2836.1 35.1 all-gather.35
  2873.5 35.1 all-gather.49
  2911.1 35.4 all-gather.21
  2948.9 35.1 all-gather.41
  2986.0 35.4 all-gather.31
  3023.8 35.1 all-gather.45
  3687.0 31.0 reduce-scatter.182
  5371.2 31.2 reduce-scatter.174
  5404.8 28.7 reduce-scatter.172
  5435.8 28.9 reduce-scatter.170
  5467.2 29.0 reduce-scatter.168
  5498.4 28.9 reduce-scatter.180
  5529.7 29.0 reduce-scatter.178
  5560.9 28.9 reduce-scatter.176
  5593.5 33.2 reduce-scatter.98
  5630.2 35.0 reduce-scatter.102
  5668.5 35.0 reduce-scatter.94
  5706.4 35.0 reduce-scatter.90
  5743.9 35.7 reduce-scatter.110
  5782.1 34.3 reduce-scatter.108
  5818.8 34.2 reduce-scatter.106
  5855.3 34.3 reduce-scatter.104
  5892.1 34.2 reduce-scatter.118
  5928.6 34.3 reduce-scatter.116
  5965.2 34.3 reduce-scatter.114
  6002.0 34.3 reduce-scatter.112
  6038.6 34.3 reduce-scatter.126
  6075.2 34.3 reduce-scatter.124
  6112.0 34.3 reduce-scatter.122
  6148.7 34.3 reduce-scatter.120
  6185.3 34.2 reduce-scatter.134
  6222.0 34.1 reduce-scatter.132
  6258.5 34.3 reduce-scatter.130
  6295.1 34.1 reduce-scatter.128
  6331.6 34.3 reduce-scatter.142
  6368.3 34.2 reduce-scatter.140
  6404.9 34.3 reduce-scatter.138
  6441.7 34.3 reduce-scatter.136
  6479.3 33.8 reduce-scatter.82
  6516.1 35.0 reduce-scatter.78
  6554.4 35.0 reduce-scatter.74
  6591.8 64.7 reduce-scatter.150
  6658.7 63.1 reduce-scatter.148
  6724.2 63.1 reduce-scatter.146
  6789.5 63.1 reduce-scatter.144
  6855.0 63.1 reduce-scatter.158
  6920.3 63.1 reduce-scatter.156
  6985.6 63.1 reduce-scatter.154
  7050.9 63.1 reduce-scatter.152
  7116.4 63.1 reduce-scatter.166
  7181.9 63.1 reduce-scatter.164
  7247.4 63.1 reduce-scatter.162
  7312.7 63.1 reduce-scatter.160
where the time goes:
time: 7460 us; the launch traced here: 7390 us
  matrix products  2820 us (38%)
  waiting for transfers between devices  2340 us (31%)
  local copies, waits for them, and re-layouts  1140 us (15%)
  other arithmetic  975 us (13%)
    dot_general x480, matrix products, block_step(): jnp.einsum('hij,hjl->hil', inverse, power, precision=HIGH)  571 us
    dot_general x480, matrix products, block_step(): power = jnp.einsum('hij,hjl->hil', power, power, precision=HIGH)  560 us
    dynamic_update_slice x256, other arithmetic, mixer(): lax.scan(block_step, initial, (split(query), split(key_vec), split(value)...  379 us
    dynamic_update_slice x608, local copies, waits for them, and re-layouts, mixer(): lax.scan(block_step, initial, (split(query), split(key_vec), split(value)...  293 us
    reduce_scatter x4, waiting for transfers between devices, share_sums(): lax.psum_scatter(row_terms[8].astype(jnp.bfloat16), 'dp', scatter_dimensi...  259 us
    reduce_scatter x4, waiting for transfers between devices, share_sums(): lax.psum_scatter(row_terms[7].astype(jnp.bfloat16), 'dp', scatter_dimensi...  258 us
    reduce_scatter x4, waiting for transfers between devices, share_sums(): lax.psum_scatter(row_terms[6].astype(jnp.bfloat16), 'dp', scatter_dimensi...  255 us
    reduce_scatter x4, waiting for transfers between devices, on_device(): lax.psum_scatter(jnp.dot(mixed_low, w_out, preferred_element_type=jnp.flo...  209 us

commit v1 on v0

v1 whole, which is shorter than its diff:
```python
import jax
import jax.numpy as jnp
from jax import lax
from jax.experimental import pallas as pl
from jax.experimental.pallas import tpu as pltpu
from jax.sharding import PartitionSpec as P

HD = 128
LANES = 128
SCALE = HD ** (-0.5)
BF = jnp.bfloat16
F32 = jnp.float32


def norm_rows(values, gain):
    return values * lax.rsqrt(jnp.mean(values * values, axis=-1, keepdims=True) + 1e-05) * gain


def swiglu(gate, upward):
    return jax.nn.silu(gate) * upward


def mm(left, right):
    return jnp.dot(left.astype(BF), right.astype(BF), preferred_element_type=F32)


def mm_nt(left, right):
    return lax.dot_general(
        left.astype(BF), right.astype(BF), (((1,), (1,)), ((), ())), preferred_element_type=F32
    )


def mm_tn(left, right):
    return lax.dot_general(
        left.astype(BF), right.astype(BF), (((0,), (0,)), ((), ())), preferred_element_type=F32
    )


def mm_exact(left, right):
    return jnp.dot(left, right, preferred_element_type=F32, precision=lax.Precision.HIGHEST)


def sigmoid(values):
    return 1.0 / (1.0 + jnp.exp(-values))


def softplus(values):
    return jnp.maximum(values, 0.0) + jnp.log(1.0 + jnp.exp(-jnp.abs(values)))


def chunk_gates(small, scal_ref, aux, heads):
    rows = small.shape[0]
    row_ids = lax.broadcasted_iota(jnp.int32, (rows, rows), 0)
    col_ids = lax.broadcasted_iota(jnp.int32, (rows, rows), 1)
    log_alpha = scal_ref[0:1, :] * softplus(small + scal_ref[1:2, :])
    beta = sigmoid(small)
    tri = (row_ids >= col_ids).astype(F32)
    decay_sum = mm_exact(tri, log_alpha)
    last = decay_sum[rows - 1 : rows, :]
    carried = aux[:, 4:5]
    growth = jnp.exp(decay_sum) * carried
    tail = jnp.exp(last - decay_sum) * aux[:, 5:6]
    keep = jnp.exp(last) * carried[rows - 1 : rows, :]
    return log_alpha, beta, decay_sum, growth, tail, keep, row_ids, col_ids


def transpose_lanes(values):
    return values.T


def conv_silu(ext, weights, aux, rows):
    total = ext(0) * weights[0]
    for offset in range(1, 4):
        total = total + ext(offset) * weights[offset] * aux[:, offset : offset + 1]
    return total


def forward_kernel(
    heads, place_ref, raw_ref, aux_ref, segrow_ref, conv_ref, scal_ref, gain_ref,
    mixed_ref, core_ref, inv_ref, upd_ref, st_ref, ext_ref, state_ref,
):
    step = pl.program_id(0)
    rows = raw_ref.shape[1]
    width = heads * HD

    @pl.when(step == 0)
    def _():
        ext_ref[0:8, :] = jnp.zeros_like(ext_ref[0:8, :])
        state_ref[...] = jnp.zeros_like(state_ref)

    aux = aux_ref[0]
    ext_ref[8 : 8 + rows, :] = raw_ref[0, :, 0 : 3 * width]
    small = raw_ref[0, :, 4 * width : 4 * width + LANES]
    _, beta, decay_sum, growth, tail, keep, row_ids, col_ids = chunk_gates(
        small, scal_ref, aux, heads
    )
    decay_rows = transpose_lanes(decay_sum)
    below = (row_ids >= col_ids) & (aux[:, 0:1] == segrow_ref[0, 0:1, :])
    strict = row_ids > col_ids
    eye = (row_ids == col_ids).astype(F32)

    def branch(index, head):
        lanes = slice(index * width + head * HD, index * width + (head + 1) * HD)
        weights = [conv_ref[4 * index + j : 4 * index + j + 1, head * HD : (head + 1) * HD] for j in range(4)]
        conv = conv_silu(lambda j: ext_ref[8 - j : 8 - j + rows, lanes], weights, aux, rows)
        return conv * sigmoid(conv)

    for head in range(heads):
        lanes = slice(head * HD, (head + 1) * HD)
        query = branch(0, head)
        query = query * (lax.rsqrt(jnp.sum(query * query, axis=-1, keepdims=True) + 1e-06) * SCALE)
        key = branch(1, head)
        key = key * lax.rsqrt(jnp.sum(key * key, axis=-1, keepdims=True) + 1e-06)
        value = branch(2, head)
        b_col = beta[:, heads + head : heads + head + 1]
        g_col = growth[:, head : head + 1]
        spread = decay_sum[:, head : head + 1] - decay_rows[head : head + 1, :]
        inside = jnp.exp(jnp.where(below, spread, -1e30))
        stacked = jnp.concatenate([key, query], axis=0).astype(BF)
        dots = mm_nt(stacked, key)
        power = jnp.where(strict, b_col * dots[:rows] * inside, 0.0)
        inverse = eye - jnp.where((row_ids // 2) == (col_ids // 2), power, 0.0)
        half = 2
        while half < rows:
            joint = ((row_ids // (2 * half)) == (col_ids // (2 * half))) & ((row_ids // half) != (col_ids // half))
            inv_low = inverse.astype(BF)
            inverse = inverse - mm(mm(inv_low, jnp.where(joint, power, 0.0)), inv_low)
            half *= 2
        state = state_ref[head]
        state_low = state.astype(BF)
        st_ref[0, head] = state_low
        applied = mm(stacked, state_low)
        rest = b_col * (value - g_col * applied[:rows])
        inv_low = inverse.astype(BF)
        inv_ref[0, head] = inv_low
        update = mm(inv_low, rest).astype(BF)
        upd_ref[0, :, lanes] = update
        core = g_col * applied[rows:] + mm(dots[rows:] * inside, update)
        state_ref[head] = keep[:, head : head + 1] * state + mm_tn(
            key * tail[:, head : head + 1], update
        )
        core_ref[0, :, lanes] = core
        outgate = raw_ref[0, :, 3 * width + head * HD : 3 * width + (head + 1) * HD]
        normed = core * lax.rsqrt(jnp.mean(core * core, axis=-1, keepdims=True) + 1e-05)
        mixed_ref[0, :, lanes] = (
            normed * gain_ref[0:1, lanes] * (outgate * sigmoid(outgate))
        ).astype(BF)
    ext_ref[0:8, :] = ext_ref[rows : rows + 8, :]


def backward_kernel(
    heads, place_ref, raw_ref, prev_ref, aux_ref, segrow_ref, conv_ref, scal_ref, gain_ref,
    dmix_ref, core_ref, inv_ref, upd_ref, st_ref,
    draw_ref, dconv_ref, dscal_ref, dgain_ref, ext_ref, dext_ref, dstate_ref,
):
    step = pl.program_id(0)
    rows = raw_ref.shape[1]
    width = heads * HD

    @pl.when(step == 0)
    def _():
        dext_ref[rows : rows + 8, :] = jnp.zeros_like(dext_ref[rows : rows + 8, :])
        dstate_ref[...] = jnp.zeros_like(dstate_ref)
        dconv_ref[...] = jnp.zeros_like(dconv_ref)
        dscal_ref[...] = jnp.zeros_like(dscal_ref)
        dgain_ref[...] = jnp.zeros_like(dgain_ref)

    @pl.when(step > 0)
    def _():
        dext_ref[rows : rows + 8, :] = dext_ref[0:8, :]

    aux = aux_ref[0]
    ext_ref[0:8, :] = prev_ref[0, :, 0 : 3 * width]
    ext_ref[8 : 8 + rows, :] = raw_ref[0, :, 0 : 3 * width]
    small = raw_ref[0, :, 4 * width : 4 * width + LANES]
    log_alpha, beta, decay_sum, growth, tail, keep, row_ids, col_ids = chunk_gates(
        small, scal_ref, aux, heads
    )
    decay_rows = transpose_lanes(decay_sum)
    below = (row_ids >= col_ids) & (aux[:, 0:1] == segrow_ref[0, 0:1, :])
    strict = row_ids > col_ids
    lane_ids = lax.broadcasted_iota(jnp.int32, (rows, LANES), 1)
    line_ids = lax.broadcasted_iota(jnp.int32, (LANES, rows), 0)
    last_row = lax.broadcasted_iota(jnp.int32, (rows, 1), 0) == rows - 1
    d_decay = jnp.zeros((rows, LANES), F32)
    d_beta = jnp.zeros((rows, LANES), F32)
    d_decay_lines = jnp.zeros((LANES, rows), F32)

    def branch(index, head):
        lanes = slice(index * width + head * HD, index * width + (head + 1) * HD)
        weights = [conv_ref[4 * index + j : 4 * index + j + 1, head * HD : (head + 1) * HD] for j in range(4)]
        conv = conv_silu(lambda j: ext_ref[8 - j : 8 - j + rows, lanes], weights, aux, rows)
        gate = sigmoid(conv)
        return conv * gate, gate * (1.0 + conv * (1.0 - gate))

    def conv_back(index, head, d_conv):
        lanes = slice(index * width + head * HD, index * width + (head + 1) * HD)
        own = slice(head * HD, (head + 1) * HD)
        dext_ref[0:rows, lanes] = d_conv
        total = d_conv * conv_ref[4 * index : 4 * index + 1, own]
        dconv_ref[4 * index : 4 * index + 1, own] += jnp.sum(
            d_conv * ext_ref[8 : 8 + rows, lanes], axis=0, keepdims=True
        )
        for j in range(1, 4):
            line = slice(4 * index + j, 4 * index + j + 1)
            total = total + dext_ref[j : j + rows, lanes] * conv_ref[line, own] * aux[:, 7 + j : 8 + j]
            dconv_ref[line, own] += jnp.sum(
                d_conv * ext_ref[8 - j : 8 - j + rows, lanes] * aux[:, j : j + 1],
                axis=0,
                keepdims=True,
            )
        draw_ref[0, :, lanes] = total.astype(BF)

    for head in range(heads):
        lanes = slice(head * HD, (head + 1) * HD)
        outgate = raw_ref[0, :, 3 * width + head * HD : 3 * width + (head + 1) * HD]
        gate = sigmoid(outgate)
        core = core_ref[0, :, lanes]
        inv_norm = lax.rsqrt(jnp.mean(core * core, axis=-1, keepdims=True) + 1e-05)
        normed = core * inv_norm
        d_mixed = dmix_ref[0, :, lanes].astype(F32)
        gain = gain_ref[0:1, lanes]
        d_silu = d_mixed * (outgate * gate)
        dgain_ref[0:1, lanes] += jnp.sum(d_silu * normed, axis=0, keepdims=True)
        draw_ref[0, :, 3 * width + head * HD : 3 * width + (head + 1) * HD] = (
            d_mixed * normed * gain * (gate * (1.0 + outgate * (1.0 - gate)))
        ).astype(BF)
        d_normed = d_silu * gain
        d_core = inv_norm * (
            d_normed - normed * jnp.mean(d_normed * normed, axis=-1, keepdims=True)
        )
        query_s, query_slope = branch(0, head)
        query_r = lax.rsqrt(jnp.sum(query_s * query_s, axis=-1, keepdims=True) + 1e-06)
        query_n = query_s * query_r
        query = query_n * SCALE
        key_s, key_slope = branch(1, head)
        key_r = lax.rsqrt(jnp.sum(key_s * key_s, axis=-1, keepdims=True) + 1e-06)
        key = key_s * key_r
        value, value_slope = branch(2, head)
        b_col = beta[:, heads + head : heads + head + 1]
        g_col = growth[:, head : head + 1]
        t_col = tail[:, head : head + 1]
        keep_one = keep[:, head : head + 1]
        spread = decay_sum[:, head : head + 1] - decay_rows[head : head + 1, :]
        inside = jnp.exp(jnp.where(below, spread, -1e30))
        inside_strict = jnp.where(strict, inside, 0.0)
        key_low = key.astype(BF)
        query_low = query.astype(BF)
        dots = mm_nt(jnp.concatenate([key_low, query_low], axis=0), key_low)
        inverse = inv_ref[0, head]
        update = upd_ref[0, :, lanes]
        state = st_ref[0, head]
        d_state = dstate_ref[head]
        d_state_low = d_state.astype(BF)
        d_core_low = d_core.astype(BF)
        weights_out = dots[rows:] * inside
        key_tail = key * t_col
        d_update = mm_tn(weights_out, d_core_low) + mm(key_tail, d_state_low)
        d_rest = mm_tn(inverse, d_update)
        d_rest_low = d_rest.astype(BF)
        both = mm_nt(jnp.concatenate([d_core_low, d_rest_low], axis=0), update)
        d_weights = both[:rows]
        d_power = -both[rows:]
        sides = mm_nt(jnp.concatenate([d_core_low, d_rest_low], axis=0), state)
        core_state = sides[:rows]
        rest_state = sides[rows:]
        d_tail_key = mm_nt(update, d_state_low)
        d_query_dots = d_weights * inside
        power_in = d_power * inside_strict
        d_key_dots = power_in * b_col
        key_dots = dots[:rows]
        reach = d_weights * weights_out + d_key_dots * key_dots
        d_beta_col = (
            jnp.sum(power_in * key_dots, axis=-1, keepdims=True)
            + jnp.sum(d_rest * value, axis=-1, keepdims=True)
            - g_col * jnp.sum(key * rest_state, axis=-1, keepdims=True)
        )
        d_growth = jnp.sum(query * core_state, axis=-1, keepdims=True) - b_col * jnp.sum(
            key * rest_state, axis=-1, keepdims=True
        )
        tail_part = t_col * jnp.sum(d_tail_key * key, axis=-1, keepdims=True)
        last_part = jnp.sum(tail_part, axis=0, keepdims=True) + keep_one * jnp.sum(
            jnp.sum(d_state * state.astype(F32), axis=-1, keepdims=True), axis=0, keepdims=True
        )
        d_sum_col = (
            jnp.sum(reach, axis=-1, keepdims=True)
            + g_col * d_growth
            - tail_part
            + jnp.where(last_row, last_part, 0.0)
        )
        d_decay = jnp.where(lane_ids == head, d_sum_col, d_decay)
        d_beta = jnp.where(lane_ids == heads + head, d_beta_col, d_beta)
        d_decay_lines = jnp.where(
            line_ids == head, jnp.sum(reach, axis=0, keepdims=True), d_decay_lines
        )
        scale_rest = -(b_col * g_col)
        d_value = b_col * d_rest
        d_query = g_col * core_state + mm(d_query_dots, key_low)
        d_key = (
            scale_rest * rest_state
            + t_col * d_tail_key
            + mm(d_key_dots, key_low)
            + mm_tn(jnp.concatenate([d_key_dots, d_query_dots], axis=0),
                    jnp.concatenate([key_low, query_low], axis=0))
        )
        dstate_ref[head] = keep_one * d_state + mm_tn(
            jnp.concatenate([query * g_col, key], axis=0),
            jnp.concatenate([d_core, scale_rest * d_rest], axis=0),
        )
        d_query_n = d_query * SCALE
        d_query_s = query_r * (
            d_query_n - query_n * jnp.sum(query_n * d_query_n, axis=-1, keepdims=True)
        )
        d_key_s = key_r * (d_key - key * jnp.sum(key * d_key, axis=-1, keepdims=True))
        conv_back(0, head, d_query_s * query_slope)
        conv_back(1, head, d_key_s * key_slope)
        conv_back(2, head, d_value * value_slope)

    d_decay = d_decay - transpose_lanes(d_decay_lines)
    upper = (row_ids <= col_ids).astype(F32)
    d_log = mm_exact(upper, d_decay)
    d_arg = d_log * scal_ref[0:1, :] * sigmoid(small + scal_ref[1:2, :])
    dscal_ref[0:1, :] += jnp.sum(d_log * log_alpha, axis=0, keepdims=True)
    dscal_ref[1:2, :] += jnp.sum(d_arg, axis=0, keepdims=True)
    draw_ref[0, :, 4 * width : 4 * width + LANES] = (
        d_arg + d_beta * beta * (1.0 - beta)
    ).astype(BF)


def mixer_shapes(raw):
    blocks, rows, total = raw.shape
    heads = (total - LANES) // (4 * HD)
    return blocks, rows, heads, heads * HD, total


def whole(shape):
    return pl.BlockSpec(shape, lambda c, place: (0,) * len(shape))


def mixer_forward(place, raw, aux, segrow, conv_rows, scal, gain):
    blocks, rows, heads, width, total = mixer_shapes(raw)
    at = lambda c, place: (place[c], 0, 0)
    seq = lambda c, place: (c, 0, 0)
    seq4 = lambda c, place: (c, 0, 0, 0)

    def body(*refs):
        forward_kernel(heads, *refs)

    return pl.pallas_call(
        body,
        grid_spec=pltpu.PrefetchScalarGridSpec(
            num_scalar_prefetch=1,
            grid=(blocks,),
            in_specs=[
                pl.BlockSpec((1, rows, total), at),
                pl.BlockSpec((1, rows, 16), seq),
                pl.BlockSpec((1, 8, rows), seq),
                whole(conv_rows.shape),
                whole(scal.shape),
                whole(gain.shape),
            ],
            out_specs=[
                pl.BlockSpec((1, rows, width), at),
                pl.BlockSpec((1, rows, width), seq),
                pl.BlockSpec((1, heads, rows, rows), seq4),
                pl.BlockSpec((1, rows, width), seq),
                pl.BlockSpec((1, heads, HD, HD), seq4),
            ],
            scratch_shapes=[
                pltpu.VMEM((rows + 8, 3 * width), F32),
                pltpu.VMEM((heads, HD, HD), F32),
            ],
        ),
        out_shape=[
            jax.ShapeDtypeStruct((blocks, rows, width), BF),
            jax.ShapeDtypeStruct((blocks, rows, width), F32),
            jax.ShapeDtypeStruct((blocks, heads, rows, rows), BF),
            jax.ShapeDtypeStruct((blocks, rows, width), BF),
            jax.ShapeDtypeStruct((blocks, heads, HD, HD), BF),
        ],
        compiler_params=pltpu.CompilerParams(
            dimension_semantics=("arbitrary",), vmem_limit_bytes=48 * 1024 * 1024
        ),
        cost_estimate=pl.CostEstimate(
            flops=blocks * heads * 2 * HD * HD * HD * 80, bytes_accessed=8_000_000, transcendentals=0
        ),
        name="mixer_forward",
    )(place, raw, aux, segrow, conv_rows, scal, gain)


def mixer_backward(place, raw, aux, segrow, conv_rows, scal, gain, d_mixed, saved):
    blocks, rows, heads, width, total = mixer_shapes(raw)
    core, inverse, update, states = saved
    back = lambda c: blocks - 1 - c
    at = lambda c, place: (place[back(c)], 0, 0)
    before = lambda c, place: (place[jnp.maximum(back(c) - 1, 0)], rows // 8 - 1, 0)
    seq = lambda c, place: (back(c), 0, 0)
    seq4 = lambda c, place: (back(c), 0, 0, 0)

    def body(*refs):
        backward_kernel(heads, *refs)

    return pl.pallas_call(
        body,
        grid_spec=pltpu.PrefetchScalarGridSpec(
            num_scalar_prefetch=1,
            grid=(blocks,),
            in_specs=[
                pl.BlockSpec((1, rows, total), at),
                pl.BlockSpec((1, 8, total), before),
                pl.BlockSpec((1, rows, 16), seq),
                pl.BlockSpec((1, 8, rows), seq),
                whole(conv_rows.shape),
                whole(scal.shape),
                whole(gain.shape),
                pl.BlockSpec((1, rows, width), at),
                pl.BlockSpec((1, rows, width), seq),
                pl.BlockSpec((1, heads, rows, rows), seq4),
                pl.BlockSpec((1, rows, width), seq),
                pl.BlockSpec((1, heads, HD, HD), seq4),
            ],
            out_specs=[
                pl.BlockSpec((1, rows, total), at),
                whole((16, width)),
                whole((8, LANES)),
                whole((8, width)),
            ],
            scratch_shapes=[
                pltpu.VMEM((rows + 8, 3 * width), F32),
                pltpu.VMEM((rows + 8, 3 * width), F32),
                pltpu.VMEM((heads, HD, HD), F32),
            ],
        ),
        out_shape=[
            jax.ShapeDtypeStruct((blocks, rows, total), BF),
            jax.ShapeDtypeStruct((16, width), F32),
            jax.ShapeDtypeStruct((8, LANES), F32),
            jax.ShapeDtypeStruct((8, width), F32),
        ],
        compiler_params=pltpu.CompilerParams(
            dimension_semantics=("arbitrary",), vmem_limit_bytes=48 * 1024 * 1024
        ),
        cost_estimate=pl.CostEstimate(
            flops=blocks * heads * 2 * HD * HD * HD * 160, bytes_accessed=12_000_000, transcendentals=0
        ),
        name="mixer_backward",
    )(place, raw, raw, aux, segrow, conv_rows, scal, gain, d_mixed, core, inverse, update, states)


def hop(values, bit):
    size = lax.axis_size("head")
    return lax.ppermute(values, "head", [(i, i ^ bit) for i in range(size)])


def gather(values):
    if lax.axis_size("head") != 4:
        return lax.all_gather(values, "head", axis=0, tiled=False)
    half = values.shape[0] // 2
    from_x = hop(values, 1)
    from_y = hop(values, 2)
    far_a = hop(from_y[:half], 1)
    far_b = hop(from_x[half:], 2)
    full = jnp.concatenate([values, from_x, from_y, far_a, far_b], axis=0)
    return full.reshape((4,) + values.shape)


def scatter(parts):
    if lax.axis_size("head") != 4:
        return lax.psum_scatter(
            parts.astype(BF), "head", scatter_dimension=0, tiled=False
        ).astype(F32)
    half = parts.shape[1] // 2
    low = parts.astype(BF)
    top, end = low[:, :half], low[:, half:]
    in_x = hop(jnp.stack([top[1], top[3]]), 1).astype(F32)
    in_y = hop(jnp.stack([end[2], end[3]]), 2).astype(F32)
    pass_y = (parts[2, :half] + in_x[1]).astype(BF)
    pass_x = (parts[1, half:] + in_y[1]).astype(BF)
    last_y = hop(pass_y, 2).astype(F32)
    last_x = hop(pass_x, 1).astype(F32)
    return jnp.concatenate(
        [parts[0, :half] + in_x[0] + last_y, parts[0, half:] + in_y[0] + last_x], axis=0
    )


def block_places(size):
    base = lax.iota(jnp.int32, size)
    if size != 4:
        return base
    return base ^ lax.axis_index("head").astype(jnp.int32)


def contract_rows(left, right):
    return lax.dot_general(left, right, (((0,), (0,)), ((), ())), preferred_element_type=F32)


def contract_cols(left, right):
    return lax.dot_general(left, right, (((1,), (1,)), ((), ())), preferred_element_type=F32)


def times(left, right):
    return jnp.dot(left, right, preferred_element_type=F32)


def sequence_facts(doc_lengths, blocks, rows):
    span = blocks * rows
    ends = jnp.cumsum(doc_lengths, axis=-1)
    places = lax.iota(jnp.int32, span)
    segment = jnp.sum((places[None, :, None] >= ends[:, None, :]).astype(jnp.int32), axis=-1)
    columns = [segment]
    for j in range(1, 4):
        columns.append(
            (jnp.pad(segment, ((0, 0), (j, 0)), constant_values=-1)[:, :-j] == segment)
        )
    by_chunk = segment.reshape(-1, blocks, rows)
    prior = jnp.pad(by_chunk[:, :-1, -1], ((0, 0), (1, 0)), constant_values=-1)
    columns.append((by_chunk == prior[:, :, None]).reshape(segment.shape))
    columns.append((by_chunk == by_chunk[:, :, -1:]).reshape(segment.shape))
    columns += [jnp.zeros_like(segment)] * 2
    for j in range(1, 4):
        columns.append(
            (jnp.pad(segment, ((0, 0), (0, j)), constant_values=-1)[:, j:] == segment)
        )
    columns += [jnp.zeros_like(segment)] * (16 - len(columns))
    aux = jnp.stack([item.astype(F32) for item in columns], axis=-1)
    aux = aux.reshape(-1, blocks, rows, 16)
    lines = jnp.broadcast_to(by_chunk.astype(F32)[:, :, None, :], by_chunk.shape[:2] + (8, rows))
    return aux, lines


def on_device(
    tokens, cotangent, token_counts, doc_lengths, norm_in, w_query, w_key, w_value, w_outgate,
    w_decay, w_beta, conv_weight, decay_log, dt_bias, gain_out, w_out, norm_mid, w_gate, w_up,
    w_down,
):
    micro_count, rows, width = tokens.shape
    blocks = lax.axis_size("head")
    span = rows * blocks
    heads = decay_log.shape[0]
    own = heads * HD
    micros = range(micro_count)
    my_places = lax.axis_index("head") * rows + lax.iota(jnp.int32, rows)
    place = block_places(blocks)
    aux, lines = sequence_facts(doc_lengths[:, 0], blocks, rows)
    conv_rows = jnp.pad(conv_weight.reshape(12, own), ((0, 4), (0, 0)))
    scal = jnp.zeros((8, LANES), F32)
    scal = scal.at[0, :heads].set(-jnp.exp(decay_log)).at[1, :heads].set(dt_bias)
    gain_row = jnp.broadcast_to(gain_out[None], (8, own))
    w_in = jnp.concatenate(
        [w_query, w_key, w_value, w_outgate, w_decay, w_beta,
         jnp.zeros((width, LANES - 2 * heads), BF)], axis=1
    )
    ffn_gate = lax.all_gather(w_gate, "dp", axis=0, tiled=True)
    ffn_up = lax.all_gather(w_up, "dp", axis=0, tiled=True)
    ffn_down = lax.all_gather(w_down, "dp", axis=0, tiled=True)

    inputs, grads, pulls_in, full_in, full_grad = [], [], [], [], []
    for m in micros:
        x = tokens[m].astype(F32)
        normed, pull = jax.vjp(norm_rows, x, norm_in)
        live = (my_places < token_counts[m, 0]).astype(F32)
        inputs.append(x)
        pulls_in.append(pull)
        full_in.append(gather(normed.astype(BF)))
        grads.append(cotangent[m].astype(F32) * live[:, None])
    raws, saved, mixed, resids, pulls_mid, full_mid = [], [], [], [], [], []
    for m in micros:
        raw = times(full_in[m].reshape(span, width), w_in).reshape(blocks, rows, 4 * own + LANES)
        mixed_m, *saved_m = mixer_forward(place, raw, aux[m], lines[m], conv_rows, scal, gain_row)
        raws.append(raw)
        saved.append(saved_m)
        mixed.append(mixed_m.reshape(span, own))
        attn = scatter(times(mixed[m], w_out).reshape(blocks, rows, width))
        full_grad.append(gather(grads[m].astype(BF)).reshape(span, width))
        resid = inputs[m] + attn
        normed, pull = jax.vjp(norm_rows, resid, norm_mid)
        resids.append(resid)
        pulls_mid.append(pull)
        full_mid.append(gather(normed.astype(BF)).reshape(span, width))
    results, acts, gates, ups, resid_grads, full_resid = [], [], [], [], [], []
    gain_mid = jnp.zeros_like(norm_mid)
    for m in micros:
        gate = times(full_mid[m], ffn_gate)
        upward = times(full_mid[m], ffn_up)
        act_full, act_pull = jax.vjp(swiglu, gate, upward)
        act = act_full.astype(BF)
        d_gate, d_up = act_pull(times(full_grad[m], ffn_down))
        d_gate, d_up = d_gate.astype(BF), d_up.astype(BF)
        d_mid = scatter(
            (contract_cols(d_gate, ffn_gate) + contract_cols(d_up, ffn_up)).reshape(
                blocks, rows, width
            )
        )
        ffn = scatter(contract_cols(act, ffn_down).reshape(blocks, rows, width))
        results.append((resids[m] + ffn).astype(BF))
        d_resid, d_norm = pulls_mid[m](d_mid)
        d_resid = grads[m] + d_resid
        gain_mid = gain_mid + d_norm
        resid_grads.append(d_resid)
        full_resid.append(gather(d_resid.astype(BF)).reshape(span, width))
        acts.append(act)
        gates.append(d_gate)
        ups.append(d_up)

    def over_micros(left, right):
        return contract_rows(
            jnp.concatenate(left, axis=0), jnp.concatenate(right, axis=0)
        ).astype(BF)

    def share(term):
        return lax.psum_scatter(term, "dp", scatter_dimension=0, tiled=True).astype(F32)

    grad_gate = share(over_micros(full_mid, gates))
    grad_up = share(over_micros(full_mid, ups))
    grad_down = share(over_micros(full_grad, acts))
    grad_out = share(over_micros(full_resid, mixed)).T

    d_raws, input_grads = [], []
    gain_in = jnp.zeros_like(norm_in)
    small_sums = None
    for m in micros:
        d_mixed = contract_cols(full_resid[m], w_out).reshape(blocks, rows, own)
        d_raw, *d_params = mixer_backward(
            place, raws[m], aux[m], lines[m], conv_rows, scal, gain_row, d_mixed, saved[m]
        )
        small_sums = d_params if small_sums is None else [
            total + item for total, item in zip(small_sums, d_params)
        ]
        d_raws.append(d_raw.reshape(span, 4 * own + LANES))
        d_normed = scatter(contract_cols(d_raws[m], w_in).reshape(blocks, rows, width))
        d_inputs, d_norm = pulls_in[m](d_normed)
        input_grads.append((d_inputs + resid_grads[m]).astype(BF))
        gain_in = gain_in + d_norm
    flat_in = [item.reshape(span, width) for item in full_in]
    grad_in = share(over_micros(flat_in, d_raws))
    gain_sums = lax.psum((gain_in, gain_mid), ("dp", "head"))
    param_sums = lax.psum(
        (small_sums[0][:12], small_sums[1][:2, :heads], small_sums[2][0]), "dp"
    )
    return (
        jnp.stack(results),
        jnp.stack(input_grads),
        gain_sums[0],
        grad_in[:, :own],
        grad_in[:, own : 2 * own],
        grad_in[:, 2 * own : 3 * own],
        grad_in[:, 3 * own : 4 * own],
        grad_in[:, 4 * own : 4 * own + heads],
        grad_in[:, 4 * own + heads : 4 * own + 2 * heads],
        param_sums[0].reshape(conv_weight.shape),
        param_sums[1][0],
        param_sums[1][1],
        param_sums[2],
        grad_out,
        gain_sums[1],
        grad_gate,
        grad_up,
        grad_down,
    )


def solution(mesh):
    return jax.shard_map(
        on_device,
        mesh=mesh,
        in_specs=(
            P(None, ("dp", "head"), None),
            P(None, ("dp", "head"), None),
            P(None, "dp"),
            P(None, "dp", None),
            P(),
            P(None, "head"),
            P(None, "head"),
            P(None, "head"),
            P(None, "head"),
            P(None, "head"),
            P(None, "head"),
            P(None, None, "head"),
            P("head"),
            P("head"),
            P("head"),
            P("head", None),
            P(),
            P("dp", "head"),
            P("dp", "head"),
            P("dp", "head"),
        ),
        out_specs=(
            P(None, ("dp", "head"), None),
            P(None, ("dp", "head"), None),
            P(),
            P("dp", "head"),
            P("dp", "head"),
            P("dp", "head"),
            P("dp", "head"),
            P("dp", "head"),
            P("dp", "head"),
            P(None, None, "head"),
            P("head"),
            P("head"),
            P("head"),
            P("head", "dp"),
            P(),
            P("dp", "head"),
            P("dp", "head"),
            P("dp", "head"),
        ),
        check_vma=False,
    )
```

time: 7460 us -> 1230 us (0.16)
  matrix products: 2820 us -> 312 us
  waiting for transfers between devices: 2340 us -> 243 us
  local copies, waits for them, and re-layouts: 1140 us -> 121 us
  other arithmetic: 975 us -> 81.2 us
  Pallas kernels: 0 us -> 238 us
  starting transfers between devices: 6.56 us -> 139 us
    dot_general x1768 -> x20, matrix products: 2480 us -> 120 us  [times(): return jnp.dot(left, right, preferred_element_type=F32)]
    reduce_scatter x48 -> x5, waiting for transfers between devices: 1890 us -> 0.01 us  [share(): lax.psum_scatter(term, 'dp', scatter_dimension=0, tiled=True).astype(F32)]
    all_gather x19 -> x3, waiting for transfers between devices: 432 us -> 7.72 us  [the longest x1 7.72 us: on_device(): ffn_up = lax.all_gather(w_up, 'dp', axis=0, tiled=True)]
    dynamic_update_slice x256 -> x0, other arithmetic: 379 us -> none  [mixer(): lax.scan(block_step, initial, (split(query), split(key_vec), split(value)...]
    dynamic_update_slice x608 -> x0, local copies, waits for them, and re-layouts: 293 us -> none  [mixer(): lax.scan(block_step, initial, (split(query), split(key_vec), split(value)...]
    pallas_call x0 -> x8, Pallas kernels: none -> 238 us  [the longest x4 128 us: mixer_forward(): pl.pallas_call(body, grid_spec=pltpu.PrefetchScalarGridSpec(num_scalar_pr...]
    ppermute x0 -> x128, waiting for transfers between devices: none -> 234 us  [hop(): return lax.ppermute(values, 'head', [(i, i ^ bit) for i in range(size)])]
    mul x344 -> x0, local copies, waits for them, and re-layouts: 230 us -> none  [the longest x64 66.8 us: block_step(): jnp.exp(last_decay - decay_sum)]
where the time goes in v1:
time: 1230 us; the launch traced here: 1220 us
  matrix products  312 us (25%)
  waiting for transfers between devices  243 us (20%)
  Pallas kernels  238 us (19%)
  starting transfers between devices  139 us (11%)
  local copies, waits for them, and re-layouts  121 us (10%)
  other arithmetic  81.2 us (7%)
  blocking collectives  64.3 us (5%)
  between operations  19.1 us (2%)
    ppermute x128, waiting for transfers between devices, hop(): return lax.ppermute(values, 'head', [(i, i ^ bit) for i in range(size)])  234 us
    ppermute x128, starting transfers between devices, hop(): return lax.ppermute(values, 'head', [(i, i ^ bit) for i in range(size)])  139 us
    pallas_call x4, Pallas kernels, mixer_forward(): pl.pallas_call(body, grid_spec=pltpu.PrefetchScalarGridSpec(num_scalar_pr...  128 us
    dot_general x20, matrix products, times(): return jnp.dot(left, right, preferred_element_type=F32)  120 us
    pallas_call x4, Pallas kernels, mixer_backward(): pl.pallas_call(body, grid_spec=pltpu.PrefetchScalarGridSpec(num_scalar_pr...  109 us
    dot_general x20, matrix products, contract_cols(): lax.dot_general(left, right, (((1,), (1,)), ((), ())), preferred_element_...  100 us
    dot_general x5, matrix products, contract_rows(): lax.dot_general(left, right, (((0,), (0,)), ((), ())), preferred_element_...  91.8 us
    unnamed x637, local copies, waits for them, and re-layouts  79 us
  transfers between devices with their start and end apart: 136, of which 65 were waited for; matrix products, arithmetic and copies ran while one was open for 38% of the time, Pallas kernels for 20%

profile of v1, /device:TPU:0, one launch (start us, length us, event | category | flops | bytes accessed | tf_op | source)
XLA Modules:
  0.0 1217.2 jit_solution(16139603366023136231)
XLA Ops:
  28.0 13.8 %concatenate.293 = bf16[2048,2176]{1,0:T(8,128)(2,1)} concatenate(bf16[2048,512]{1,0:T(8,128)(2,1)} %param.29, bf16[2048,512]{1,0:T(8,128)(2,1)} %param.30, bf16[2048,512]{1,0:T(8,128)(2,1)} %param.31, bf16[2048,512]{1,0:T(8,128)(2,1)} %param.32, bf16[2048,4]{1,0:T(8,128)(2,1)} %copy.96, bf16[2048,4]{1,0:T(8,128)(2,1)} %copy.97, bf16[2048,120]{1,0:T(8,128)(2,1)} %broadcast_in_dim.85), dimensions={1} | concatenate | bytes 17825792 | tf_op jit(solution)/shard_map/concatenate | solution.py:549
  63.2 7.8 fusion.349
  71.0 32.1 %mixer_forward.5 = (bf16[4,128,512]{2,1,0:T(8,128)(2,1)S(1)}, f32[4,128,512]{2,1,0:T(8,128)S(1)}, bf16[4,4,128,128]{3,2,1,0:T(8,128)(2,1)S(1)}, bf16[4,128,512]{...) custom-call(s32[4]{0:T(128)S(1)} %iota_xor_fusion.refs_0_, f32[4,128,2176]{2,1,0:T(8,128)} %bitcast.721, ...), custom_call_target="tpu_custom_call" | custom-call | flops 5368709120 | bytes 8000000 | tf_op jit(solution)/shard_map/mixer_forward/pallas_call | solution.py:349
  111.9 8.1 collective-permute-done.20
  124.0 8.9 collective-permute-done.81
  148.6 6.8 collective-permute-done.25
  159.3 8.0 collective-permute-done.26
  170.2 8.4 fusion.350
  178.6 8.3 fusion.363
  186.9 7.7 all-gather.6.cloned.1.call-done
  194.6 10.3 multiply_convert_fusion.6
  204.9 6.8 fusion.364
  251.3 5.8 collective-permute-done.1
  270.8 6.6 fusion.346
  277.4 32.3 %mixer_forward.4 = (bf16[4,128,512]{2,1,0:T(8,128)(2,1)S(1)}, f32[4,128,512]{2,1,0:T(8,128)S(1)}, bf16[4,4,128,128]{3,2,1,0:T(8,128)(2,1)S(1)}, bf16[4,128,512]{...) custom-call(s32[4]{0:T(128)S(1)} %iota_xor_fusion.refs_0_, f32[4,128,2176]{2,1,0:T(8,128)} %bitcast.727, ...), custom_call_target="tpu_custom_call" | custom-call | flops 5368709120 | bytes 8000000 | tf_op jit(solution)/shard_map/mixer_forward/pallas_call | solution.py:349
  316.0 10.5 collective-permute-done.4
  333.7 6.6 fusion.352
  340.3 32.0 %mixer_forward.6 = (bf16[4,128,512]{2,1,0:T(8,128)(2,1)S(1)}, f32[4,128,512]{2,1,0:T(8,128)S(1)}, bf16[4,4,128,128]{3,2,1,0:T(8,128)(2,1)S(1)}, bf16[4,128,512]{...) custom-call(s32[4]{0:T(128)S(1)} %iota_xor_fusion.refs_0_, f32[4,128,2176]{2,1,0:T(8,128)} %bitcast.724, ...), custom_call_target="tpu_custom_call" | custom-call | flops 5368709120 | bytes 8000000 | tf_op jit(solution)/shard_map/mixer_forward/pallas_call | solution.py:349
  383.7 8.0 collective-permute-done.36
  394.9 9.3 collective-permute-done.49
  405.0 5.2 collective-permute-done.9
  423.0 5.0 fusion.347
  428.1 8.5 multiply_convert_fusion.7
  441.5 7.0 convolution_add_fusion.3
  452.8 10.6 fusion.356
  463.4 31.9 %mixer_forward.7 = (bf16[4,128,512]{2,1,0:T(8,128)(2,1)S(1)}, f32[4,128,512]{2,1,0:T(8,128)S(1)}, bf16[4,4,128,128]{3,2,1,0:T(8,128)(2,1)S(1)}, bf16[4,128,512]{...) custom-call(s32[4]{0:T(128)S(1)} %iota_xor_fusion.refs_0_, f32[4,128,2176]{2,1,0:T(8,128)} %bitcast.730, ...), custom_call_target="tpu_custom_call" | custom-call | flops 5368709120 | bytes 8000000 | tf_op jit(solution)/shard_map/mixer_forward/pallas_call | solution.py:349
  506.3 6.0 collective-permute-done.68
  523.1 5.4 collective-permute-done.53
  538.3 9.9 collective-permute-done.113
  552.6 7.5 collective-permute-done.40
  575.4 5.1 fusion.354
  585.4 8.7 multiply_convert_fusion.1
  594.1 5.0 fusion.366
  599.1 7.0 convolution_add_fusion.1
  615.3 5.4 collective-permute-done.100
  631.8 5.8 collective-permute-done.57
  650.1 5.0 fusion.358
  655.1 5.0 fusion.357
  660.1 8.9 multiply_convert_fusion
  669.0 8.2 fusion.368
  677.2 7.1 convolution_add_fusion
  686.6 12.5 %collective-permute-done.116 = bf16[2,64,2048]{2,1,0:T(8,128)(2,1)S(1)} collective-permute-done((bf16[2,64,2048]{2,1,0:T(8,128)(2,1)S(1)}, bf16[2,64,2048]{2,1,0:T(8,128)(2,1)S(1)}, u32[]{:S(2)}, u32[]{:S(2)}) %collective-permute-start.116) | collective-permute-done | bytes 524320 | tf_op jit(solution)/shard_map/ppermute | solution.py:452
  712.0 9.9 collective-permute-done.105
  734.8 6.6 collective-permute-done.121
  751.1 9.5 convolution_convert_fusion.4
  760.6 20.4 %convolution_convert_fusion.1 = bf16[2048,1408]{1,0:T(8,128)(2,1)} fusion(bf16[2048,2048]{1,0:T(8,128)(2,1)} %get-tuple-element.455, bf16[512,1408]{1,0:T(8,128)(2,1)} %get-tuple-element.268, bf16[512,1408]{1,0:T(8,128)(2,1)} %get-tuple-element.271, bf16[512,1408]{1,0:T(8,128)(2,1)} %get-tuple-element.275, bf16[512,1408]{1,0:T(8,128)(2,1)} %get-tuple-element.272), kind=kOutput, calls=%fused_computation.16 | convolution fusion | flops 11837112320 | bytes 19922944 | tf_op jit(solution)/shard_map/dot_general | solution.py:494
  781.1 20.0 %convolution_convert_fusion.2 = bf16[2048,1408]{1,0:T(8,128)(2,1)} fusion(bf16[2048,2048]{1,0:T(8,128)(2,1)} %get-tuple-element.459, bf16[512,1408]{1,0:T(8,128)(2,1)} %get-tuple-element.266, bf16[512,1408]{1,0:T(8,128)(2,1)} %copy-done.234, bf16[512,1408]{1,0:T(8,128)(2,1)} %copy-done.232, bf16[512,1408]{1,0:T(8,128)(2,1)} %copy-done.233), kind=kOutput, calls=%fused_computation.17 | convolution fusion | flops 11837112320 | bytes 19922944 | tf_op jit(solution)/shard_map/dot_general | solution.py:494
  801.1 6.2 fusion.351
  810.4 6.6 collective-permute-done.28
  828.1 6.1 collective-permute-done.12
  845.2 16.8 %convolution_convert_fusion.3 = bf16[2048,1408]{1,0:T(8,128)(2,1)} fusion(bf16[2048,2048]{1,0:T(8,128)(2,1)S(1)} %bitcast.695, bf16[512,1408]{1,0:T(8,128)(2,1)} %copy-done.242, bf16[512,1408]{1,0:T(8,128)(2,1)} %copy-done.240, bf16[512,1408]{1,0:T(8,128)(2,1)S(1)} %copy-done.237, bf16[512,1408]{1,0:T(8,128)(2,1)} %copy-done.238), kind=kOutput, calls=%fused_computation.18 | convolution fusion | flops 11837112320 | bytes 19922944 | tf_op jit(solution)/shard_map/dot_general | solution.py:494
  865.3 28.0 %mixer_backward.4 = (bf16[4,128,2176]{2,1,0:T(8,128)(2,1)}, f32[16,512]{1,0:T(8,128)S(1)}, f32[8,128]{1,0:T(8,128)S(1)}, f32[8,512]{1,0:T(8,128)S(1)}) custom-call(s32[4]{0:T(128)S(1)} %copy-done.20, f32[4,128,2176]{2,1,0:T(8,128)} %bitcast.728, f32[4,128,2176]{2,1,0:T(8,128)} %bitcast.729, f32[4,128,16]{2,1,0:T(8,128)S(1)} %bitcast.625, ...), custom_call_target="tpu_custom_call" | custom-call | flops 10737418240 | bytes 12000000 | tf_op jit(solution)/shard_map/mixer_backward/pallas_call | solution.py:403
  893.4 6.8 fusion.344
  923.8 26.9 %mixer_backward.5 = (bf16[4,128,2176]{2,1,0:T(8,128)(2,1)}, f32[16,512]{1,0:T(8,128)S(1)}, f32[8,128]{1,0:T(8,128)S(1)}, f32[8,512]{1,0:T(8,128)S(1)}) custom-call(s32[4]{0:T(128)S(1)} %copy-done.20, f32[4,128,2176]{2,1,0:T(8,128)} %bitcast.722, f32[4,128,2176]{2,1,0:T(8,128)} %bitcast.723, f32[4,128,16]{2,1,0:T(8,128)S(1)} %bitcast.623, ...), custom_call_target="tpu_custom_call" | custom-call | flops 10737418240 | bytes 12000000 | tf_op jit(solution)/shard_map/mixer_backward/pallas_call | solution.py:403
  952.3 27.2 %mixer_backward.6 = (bf16[4,128,2176]{2,1,0:T(8,128)(2,1)}, f32[16,512]{1,0:T(8,128)S(1)}, f32[8,128]{1,0:T(8,128)S(1)}, f32[8,512]{1,0:T(8,128)S(1)}) custom-call(s32[4]{0:T(128)S(1)} %copy-done.20, f32[4,128,2176]{2,1,0:T(8,128)} %bitcast.725, f32[4,128,2176]{2,1,0:T(8,128)} %bitcast.726, f32[4,128,16]{2,1,0:T(8,128)S(1)} %bitcast.621, ...), custom_call_target="tpu_custom_call" | custom-call | flops 10737418240 | bytes 12000000 | tf_op jit(solution)/shard_map/mixer_backward/pallas_call | solution.py:403
  981.2 27.3 %mixer_backward.7 = (bf16[4,128,2176]{2,1,0:T(8,128)(2,1)}, f32[16,512]{1,0:T(8,128)S(1)}, f32[8,128]{1,0:T(8,128)S(1)}, f32[8,512]{1,0:T(8,128)S(1)}) custom-call(s32[4]{0:T(128)S(1)} %copy-done.20, f32[4,128,2176]{2,1,0:T(8,128)} %bitcast.731, f32[4,128,2176]{2,1,0:T(8,128)} %bitcast.732, f32[4,128,16]{2,1,0:T(8,128)S(1)} %bitcast.619, ...), custom_call_target="tpu_custom_call" | custom-call | flops 10737418240 | bytes 12000000 | tf_op jit(solution)/shard_map/mixer_backward/pallas_call | solution.py:403
  1008.5 25.2 %convolution_convert_fusion = bf16[2048,2176]{1,0:T(8,128)(2,1)} fusion(bf16[2048,2048]{1,0:T(8,128)(2,1)S(1)} %bitcast.697, bf16[512,2176]{1,0:T(8,128)(2,1)} %bitcast.733, bf16[512,2176]{1,0:T(8,128)(2,1)} %bitcast.734, bf16[512,2176]{1,0:T(8,128)(2,1)} %bitcast.736, bf16[512,2176]{1,0:T(8,128)(2,1)} %bitcast.735), kind=kOutput, calls=%fused_computation | convolution fusion | flops 18293719040 | bytes 26214400 | tf_op jit(solution)/shard_map/dot_general | solution.py:494
  1033.8 5.9 fusion.359
  1041.7 7.8 fusion.345
  1062.4 6.6 collective-permute-done.94
  1078.8 5.1 fusion.343
  1096.4 5.1 fusion.342
  1115.4 27.1 %all-reduce.10 = (f32[3,4,512]{2,1,0:T(4,128)}, f32[2,4]{1,0:T(2,128)S(1)}, f32[512]{0:T(512)}) all-reduce(f32[3,4,512]{2,1,0:T(4,128)S(1)} %reshape.1250, f32[2,4]{1,0:T(2,128)S(1)} %slice.1123, f32[512]{0:T(512)S(1)} %bitcast.698), channel_id=1, replica_groups=mesh['dp'=8,'head'=4] {'dp'}, use_global_device_ids=true, to_apply=%region_24.25 | all-reduce | flops 6664 | bytes 53312 | tf_op jit(solution)/shard_map/psum | solution.py:637
  1148.7 37.2 %all-reduce.9 = (f32[2048]{0:T(1024)}, f32[2048]{0:T(1024)}) all-reduce(f32[2048]{0:T(1024)S(1)} %get-tuple-element.556, f32[2048]{0:T(1024)S(1)} %get-tuple-element.555), channel_id=1, replica_groups=mesh['dp'=8,'head'=4] {'dp','head'}, use_global_device_ids=true, to_apply=%region_22.23 | all-reduce | flops 4096 | bytes 32768 | tf_op jit(solution)/shard_map/psum | solution.py:636
  (1190 shorter events, 441.3 us)
Async XLA Ops:
  7.2 163.0 %all-gather.4.cloned.1.call-start = ((), (), s32[]{:S(2)}) async-start(), calls=%async_computation.5 | async-start | bytes 6488064 | tf_op jit(solution)/shard_map/all_gather | solution.py:553
  8.0 170.6 %all-gather.8.cloned.1.call-start = ((), (), s32[]{:S(2)}) async-start(), calls=%async_computation.7 | async-start | bytes 6488064 | tf_op jit(solution)/shard_map/all_gather | solution.py:555
  8.7 185.9 %all-gather.6.cloned.1.call-start = ((), (), s32[]{:S(2)}) async-start(), calls=%async_computation.6 | async-start | bytes 6488064 | tf_op jit(solution)/shard_map/all_gather | solution.py:554
  12.3 32.0 %collective-permute-start.17 = (bf16[128,2048]{1,0:T(8,128)(2,1)}, bf16[128,2048]{1,0:T(8,128)(2,1)}, u32[]{:S(2)}, u32[]{:S(2)}) collective-permute-start(bf16[128,2048]{1,0:T(8,128)(2,1)} %get-tuple-element.265), channel_id=1, source_target_pairs={{0,2},{1,3},{2,0},{3,1},{4,6},{5,7},{6,4},{7,5},{8,10},{9,11},{10,... | collective-permute-start | bytes 1572872 | tf_op jit(solution)/shard_map/ppermute | solution.py:452
  15.2 32.3 %collective-permute-start.16 = (bf16[128,2048]{1,0:T(8,128)(2,1)}, bf16[128,2048]{1,0:T(8,128)(2,1)}, u32[]{:S(2)}, u32[]{:S(2)}) collective-permute-start(bf16[128,2048]{1,0:T(8,128)(2,1)} %get-tuple-element.265), channel_id=1, source_target_pairs={{0,1},{1,0},{2,3},{3,2},{4,5},{5,4},{6,7},{7,6},{8,9},{9,8},{10,11... | collective-permute-start | bytes 1572872 | tf_op jit(solution)/shard_map/ppermute | solution.py:452
  20.2 29.9 %collective-permute-start.65 = (bf16[128,2048]{1,0:T(8,128)(2,1)}, bf16[128,2048]{1,0:T(8,128)(2,1)}, u32[]{:S(2)}, u32[]{:S(2)}) collective-permute-start(bf16[128,2048]{1,0:T(8,128)(2,1)} %get-tuple-element.241), channel_id=1, source_target_pairs={{0,2},{1,3},{2,0},{3,1},{4,6},{5,7},{6,4},{7,5},{8,10},{9,11},{10,... | collective-permute-start | bytes 1572872 | tf_op jit(solution)/shard_map/ppermute | solution.py:452
  20.7 31.0 %collective-permute-start.64 = (bf16[128,2048]{1,0:T(8,128)(2,1)}, bf16[128,2048]{1,0:T(8,128)(2,1)}, u32[]{:S(2)}, u32[]{:S(2)}) collective-permute-start(bf16[128,2048]{1,0:T(8,128)(2,1)} %get-tuple-element.241), channel_id=1, source_target_pairs={{0,1},{1,0},{2,3},{3,2},{4,5},{5,4},{6,7},{7,6},{8,9},{9,8},{10,11... | collective-permute-start | bytes 1572872 | tf_op jit(solution)/shard_map/ppermute | solution.py:452
  20.8 1175.4 %reduce-scatter.8.cloned.1.call-start = ((), (), s32[]{:S(2)}) async-start(), calls=%async_computation.9 | async-start | bytes 2359296 | tf_op jit(solution)/shard_map/reduce_scatter | solution.py:611
  51.1 57.3 %collective-permute-start.66 = (bf16[64,2048]{1,0:T(8,128)(2,1)S(1)}, bf16[64,2048]{1,0:T(8,128)(2,1)S(1)}, u32[]{:S(2)}, u32[]{:S(2)}) collective-permute-start(bf16[64,2048]{1,0:T(8,128)(2,1)S(1)} %slice.1233), channel_id=1, source_target_pairs={{0,1},{1,0},{2,3},{3,2},{4,5},{5,4},{6,7},{7,6},{8,9},{9,8},{10,11... | collective-permute-start | bytes 786440 | tf_op jit(solution)/shard_map/ppermute | solution.py:452
  52.6 56.7 %collective-permute-start.67 = (bf16[64,2048]{1,0:T(8,128)(2,1)S(1)}, bf16[64,2048]{1,0:T(8,128)(2,1)S(1)}, u32[]{:S(2)}, u32[]{:S(2)}) collective-permute-start(bf16[64,2048]{1,0:T(8,128)(2,1)S(1)} %slice.1234), channel_id=1, source_target_pairs={{0,2},{1,3},{2,0},{3,1},{4,6},{5,7},{6,4},{7,5},{8,10},{9,11},{10,... | collective-permute-start | bytes 786440 | tf_op jit(solution)/shard_map/ppermute | solution.py:452
  111.1 21.8 %collective-permute-start.81 = (bf16[128,2048]{1,0:T(8,128)(2,1)S(1)}, bf16[128,2048]{1,0:T(8,128)(2,1)S(1)}, u32[]{:S(2)}, u32[]{:S(2)}) collective-permute-start(bf16[128,2048]{1,0:T(8,128)(2,1)S(1)} %get-tuple-element.239), channel_id=1, source_target_pairs={{0,2},{1,3},{2,0},{3,1},{4,6},{5,7},{6,4},{7,5},{8,10},{9,11},{10,... | collective-permute-start | bytes 1572872 | tf_op jit(solution)/shard_map/ppermute | solution.py:452
  111.5 21.8 %collective-permute-start.80 = (bf16[128,2048]{1,0:T(8,128)(2,1)S(1)}, bf16[128,2048]{1,0:T(8,128)(2,1)S(1)}, u32[]{:S(2)}, u32[]{:S(2)}) collective-permute-start(bf16[128,2048]{1,0:T(8,128)(2,1)S(1)} %get-tuple-element.239), channel_id=1, source_target_pairs={{0,1},{1,0},{2,3},{3,2},{4,5},{5,4},{6,7},{7,6},{8,9},{9,8},{10,11... | collective-permute-start | bytes 1572872 | tf_op jit(solution)/shard_map/ppermute | solution.py:452
  121.9 16.6 %collective-permute-start.21 = (bf16[64,2048]{1,0:T(8,128)(2,1)S(1)}, bf16[64,2048]{1,0:T(8,128)(2,1)S(1)}, u32[]{:S(2)}, u32[]{:S(2)}) collective-permute-start(bf16[64,2048]{1,0:T(8,128)(2,1)S(1)} %get-tuple-element.340), channel_id=1, source_target_pairs={{0,2},{1,3},{2,0},{3,1},{4,6},{5,7},{6,4},{7,5},{8,10},{9,11},{10,... | collective-permute-start | bytes 786440 | tf_op jit(solution)/shard_map/ppermute | solution.py:452
  146.2 73.7 %collective-permute-start.97 = (bf16[128,2048]{1,0:T(8,128)(2,1)}, bf16[128,2048]{1,0:T(8,128)(2,1)}, u32[]{:S(2)}, u32[]{:S(2)}) collective-permute-start(bf16[128,2048]{1,0:T(8,128)(2,1)} %get-tuple-element.237), channel_id=1, source_target_pairs={{0,2},{1,3},{2,0},{3,1},{4,6},{5,7},{6,4},{7,5},{8,10},{9,11},{10,... | collective-permute-start | bytes 1572872 | tf_op jit(solution)/shard_map/ppermute | solution.py:452
  147.8 73.7 %collective-permute-start.96 = (bf16[128,2048]{1,0:T(8,128)(2,1)}, bf16[128,2048]{1,0:T(8,128)(2,1)}, u32[]{:S(2)}, u32[]{:S(2)}) collective-permute-start(bf16[128,2048]{1,0:T(8,128)(2,1)} %get-tuple-element.237), channel_id=1, source_target_pairs={{0,1},{1,0},{2,3},{3,2},{4,5},{5,4},{6,7},{7,6},{8,9},{9,8},{10,11... | collective-permute-start | bytes 1572872 | tf_op jit(solution)/shard_map/ppermute | solution.py:452
  268.6 45.0 %collective-permute-start.33 = (bf16[128,2048]{1,0:T(8,128)(2,1)S(1)}, bf16[128,2048]{1,0:T(8,128)(2,1)S(1)}, u32[]{:S(2)}, u32[]{:S(2)}) collective-permute-start(bf16[128,2048]{1,0:T(8,128)(2,1)S(1)} %get-tuple-element.259), channel_id=1, source_target_pairs={{0,2},{1,3},{2,0},{3,1},{4,6},{5,7},{6,4},{7,5},{8,10},{9,11},{10,... | collective-permute-start | bytes 1572872 | tf_op jit(solution)/shard_map/ppermute | solution.py:452
  269.4 45.1 %collective-permute-start.32 = (bf16[128,2048]{1,0:T(8,128)(2,1)S(1)}, bf16[128,2048]{1,0:T(8,128)(2,1)S(1)}, u32[]{:S(2)}, u32[]{:S(2)}) collective-permute-start(bf16[128,2048]{1,0:T(8,128)(2,1)S(1)} %get-tuple-element.259), channel_id=1, source_target_pairs={{0,1},{1,0},{2,3},{3,2},{4,5},{5,4},{6,7},{7,6},{8,9},{9,8},{10,11... | collective-permute-start | bytes 1572872 | tf_op jit(solution)/shard_map/ppermute | solution.py:452
  313.6 18.5 %collective-permute-start.34 = (bf16[64,2048]{1,0:T(8,128)(2,1)S(1)}, bf16[64,2048]{1,0:T(8,128)(2,1)S(1)}, u32[]{:S(2)}, u32[]{:S(2)}) collective-permute-start(bf16[64,2048]{1,0:T(8,128)(2,1)S(1)} %slice.1181), channel_id=1, source_target_pairs={{0,1},{1,0},{2,3},{3,2},{4,5},{5,4},{6,7},{7,6},{8,9},{9,8},{10,11... | collective-permute-start | bytes 786440 | tf_op jit(solution)/shard_map/ppermute | solution.py:452
  314.4 18.5 %collective-permute-start.35 = (bf16[64,2048]{1,0:T(8,128)(2,1)S(1)}, bf16[64,2048]{1,0:T(8,128)(2,1)S(1)}, u32[]{:S(2)}, u32[]{:S(2)}) collective-permute-start(bf16[64,2048]{1,0:T(8,128)(2,1)S(1)} %slice.1182), channel_id=1, source_target_pairs={{0,2},{1,3},{2,0},{3,1},{4,6},{5,7},{6,4},{7,5},{8,10},{9,11},{10,... | collective-permute-start | bytes 786440 | tf_op jit(solution)/shard_map/ppermute | solution.py:452
  328.3 45.7 %collective-permute-start.5 = (bf16[64,2048]{1,0:T(8,128)(2,1)}, bf16[64,2048]{1,0:T(8,128)(2,1)S(1)}, u32[]{:S(2)}, u32[]{:S(2)}) collective-permute-start(bf16[64,2048]{1,0:T(8,128)(2,1)} %get-tuple-element.332), channel_id=1, source_target_pairs={{0,2},{1,3},{2,0},{3,1},{4,6},{5,7},{6,4},{7,5},{8,10},{9,11},{10,... | collective-permute-start | bytes 786440 | tf_op jit(solution)/shard_map/ppermute | solution.py:452
  329.6 44.4 %collective-permute-start.7 = (bf16[64,2048]{1,0:T(8,128)(2,1)}, bf16[64,2048]{1,0:T(8,128)(2,1)}, u32[]{:S(2)}, u32[]{:S(2)}) collective-permute-start(bf16[64,2048]{1,0:T(8,128)(2,1)} %get-tuple-element.333), channel_id=1, source_target_pairs={{0,1},{1,0},{2,3},{3,2},{4,5},{5,4},{6,7},{7,6},{8,9},{9,8},{10,11... | collective-permute-start | bytes 786440 | tf_op jit(solution)/shard_map/ppermute | solution.py:452
  380.2 24.1 %collective-permute-start.49 = (bf16[128,2048]{1,0:T(8,128)(2,1)S(1)}, bf16[128,2048]{1,0:T(8,128)(2,1)S(1)}, u32[]{:S(2)}, u32[]{:S(2)}) collective-permute-start(bf16[128,2048]{1,0:T(8,128)(2,1)S(1)} %get-tuple-element.257), channel_id=1, source_target_pairs={{0,2},{1,3},{2,0},{3,1},{4,6},{5,7},{6,4},{7,5},{8,10},{9,11},{10,... | collective-permute-start | bytes 1572872 | tf_op jit(solution)/shard_map/ppermute | solution.py:452
  381.5 31.8 %collective-permute-start.48 = (bf16[128,2048]{1,0:T(8,128)(2,1)S(1)}, bf16[128,2048]{1,0:T(8,128)(2,1)S(1)}, u32[]{:S(2)}, u32[]{:S(2)}) collective-permute-start(bf16[128,2048]{1,0:T(8,128)(2,1)S(1)} %get-tuple-element.257), channel_id=1, source_target_pairs={{0,1},{1,0},{2,3},{3,2},{4,5},{5,4},{6,7},{7,6},{8,9},{9,8},{10,11... | collective-permute-start | bytes 1572872 | tf_op jit(solution)/shard_map/ppermute | solution.py:452
  382.2 27.9 %collective-permute-start.9 = (bf16[128,2048]{1,0:T(8,128)(2,1)S(1)}, bf16[128,2048]{1,0:T(8,128)(2,1)S(1)}, u32[]{:S(2)}, u32[]{:S(2)}) collective-permute-start(bf16[128,2048]{1,0:T(8,128)(2,1)S(1)} %get-tuple-element.382), channel_id=1, source_target_pairs={{0,2},{1,3},{2,0},{3,1},{4,6},{5,7},{6,4},{7,5},{8,10},{9,11},{10,... | collective-permute-start | bytes 1572872 | tf_op jit(solution)/shard_map/ppermute | solution.py:452
  391.7 20.8 %collective-permute-start.8 = (bf16[128,2048]{1,0:T(8,128)(2,1)S(1)}, bf16[128,2048]{1,0:T(8,128)(2,1)S(1)}, u32[]{:S(2)}, u32[]{:S(2)}) collective-permute-start(bf16[128,2048]{1,0:T(8,128)(2,1)S(1)} %get-tuple-element.382), channel_id=1, source_target_pairs={{0,1},{1,0},{2,3},{3,2},{4,5},{5,4},{6,7},{7,6},{8,9},{9,8},{10,11... | collective-permute-start | bytes 1572872 | tf_op jit(solution)/shard_map/ppermute | solution.py:452
  394.2 108.0 %collective-permute-start.37 = (bf16[64,2048]{1,0:T(8,128)(2,1)}, bf16[64,2048]{1,0:T(8,128)(2,1)S(1)}, u32[]{:S(2)}, u32[]{:S(2)}) collective-permute-start(bf16[64,2048]{1,0:T(8,128)(2,1)} %get-tuple-element.324), channel_id=1, source_target_pairs={{0,2},{1,3},{2,0},{3,1},{4,6},{5,7},{6,4},{7,5},{8,10},{9,11},{10,... | collective-permute-start | bytes 786440 | tf_op jit(solution)/shard_map/ppermute | solution.py:452
  404.3 98.6 %collective-permute-start.39 = (bf16[64,2048]{1,0:T(8,128)(2,1)}, bf16[64,2048]{1,0:T(8,128)(2,1)}, u32[]{:S(2)}, u32[]{:S(2)}) collective-permute-start(bf16[64,2048]{1,0:T(8,128)(2,1)} %get-tuple-element.325), channel_id=1, source_target_pairs={{0,1},{1,0},{2,3},{3,2},{4,5},{5,4},{6,7},{7,6},{8,9},{9,8},{10,11... | collective-permute-start | bytes 786440 | tf_op jit(solution)/shard_map/ppermute | solution.py:452
  410.1 41.1 %collective-permute-start.50 = (bf16[64,2048]{1,0:T(8,128)(2,1)S(1)}, bf16[64,2048]{1,0:T(8,128)(2,1)S(1)}, u32[]{:S(2)}, u32[]{:S(2)}) collective-permute-start(bf16[64,2048]{1,0:T(8,128)(2,1)S(1)} %slice.1207), channel_id=1, source_target_pairs={{0,1},{1,0},{2,3},{3,2},{4,5},{5,4},{6,7},{7,6},{8,9},{9,8},{10,11... | collective-permute-start | bytes 786440 | tf_op jit(solution)/shard_map/ppermute | solution.py:452
  421.0 31.1 %collective-permute-start.51 = (bf16[64,2048]{1,0:T(8,128)(2,1)S(1)}, bf16[64,2048]{1,0:T(8,128)(2,1)S(1)}, u32[]{:S(2)}, u32[]{:S(2)}) collective-permute-start(bf16[64,2048]{1,0:T(8,128)(2,1)S(1)} %slice.1208), channel_id=1, source_target_pairs={{0,2},{1,3},{2,0},{3,1},{4,6},{5,7},{6,4},{7,5},{8,10},{9,11},{10,... | collective-permute-start | bytes 786440 | tf_op jit(solution)/shard_map/ppermute | solution.py:452
  500.0 17.9 %collective-permute-start.52 = (bf16[2,64,2048]{2,1,0:T(8,128)(2,1)S(1)}, bf16[2,64,2048]{2,1,0:T(8,128)(2,1)S(1)}, u32[]{:S(2)}, u32[]{:S(2)}) collective-permute-start(bf16[2,64,2048]{2,1,0:T(8,128)(2,1)S(1)} %pad_maximum_fusion.16), channel_id=1, source_target_pairs={{0,1},{1,0},{2,3},{3,2},{4,5},{5,4},{6,7},{7,6},{8,9},{9,8},{10,11... | collective-permute-start | bytes 1572872 | tf_op jit(solution)/shard_map/ppermute | solution.py:452
  502.3 15.9 %collective-permute-start.54 = (bf16[2,64,2048]{2,1,0:T(8,128)(2,1)S(1)}, bf16[2,64,2048]{2,1,0:T(8,128)(2,1)S(1)}, u32[]{:S(2)}, u32[]{:S(2)}) collective-permute-start(bf16[2,64,2048]{2,1,0:T(8,128)(2,1)S(1)} %stack.223), channel_id=1, source_target_pairs={{0,2},{1,3},{2,0},{3,1},{4,6},{5,7},{6,4},{7,5},{8,10},{9,11},{10,... | collective-permute-start | bytes 1572872 | tf_op jit(solution)/shard_map/ppermute | solution.py:452
  534.0 15.8 %collective-permute-start.112 = (bf16[128,2048]{1,0:T(8,128)(2,1)S(1)}, bf16[128,2048]{1,0:T(8,128)(2,1)S(1)}, u32[]{:S(2)}, u32[]{:S(2)}) collective-permute-start(bf16[128,2048]{1,0:T(8,128)(2,1)S(1)} %get-tuple-element.235), channel_id=1, source_target_pairs={{0,1},{1,0},{2,3},{3,2},{4,5},{5,4},{6,7},{7,6},{8,9},{9,8},{10,11... | collective-permute-start | bytes 1572872 | tf_op jit(solution)/shard_map/ppermute | solution.py:452
  535.8 24.2 %collective-permute-start.40 = (bf16[128,2048]{1,0:T(8,128)(2,1)S(1)}, bf16[128,2048]{1,0:T(8,128)(2,1)S(1)}, u32[]{:S(2)}, u32[]{:S(2)}) collective-permute-start(bf16[128,2048]{1,0:T(8,128)(2,1)S(1)} %get-tuple-element.363), channel_id=1, source_target_pairs={{0,1},{1,0},{2,3},{3,2},{4,5},{5,4},{6,7},{7,6},{8,9},{9,8},{10,11... | collective-permute-start | bytes 1572872 | tf_op jit(solution)/shard_map/ppermute | solution.py:452
  536.0 25.4 %collective-permute-start.41 = (bf16[128,2048]{1,0:T(8,128)(2,1)S(1)}, bf16[128,2048]{1,0:T(8,128)(2,1)S(1)}, u32[]{:S(2)}, u32[]{:S(2)}) collective-permute-start(bf16[128,2048]{1,0:T(8,128)(2,1)S(1)} %get-tuple-element.363), channel_id=1, source_target_pairs={{0,2},{1,3},{2,0},{3,1},{4,6},{5,7},{6,4},{7,5},{8,10},{9,11},{10,... | collective-permute-start | bytes 1572872 | tf_op jit(solution)/shard_map/ppermute | solution.py:452
  537.4 28.5 %collective-permute-start.73 = (bf16[128,2048]{1,0:T(8,128)(2,1)S(1)}, bf16[128,2048]{1,0:T(8,128)(2,1)S(1)}, u32[]{:S(2)}, u32[]{:S(2)}) collective-permute-start(bf16[128,2048]{1,0:T(8,128)(2,1)S(1)} %get-tuple-element.365), channel_id=1, source_target_pairs={{0,2},{1,3},{2,0},{3,1},{4,6},{5,7},{6,4},{7,5},{8,10},{9,11},{10,... | collective-permute-start | bytes 1572872 | tf_op jit(solution)/shard_map/ppermute | solution.py:452
  548.1 21.1 %collective-permute-start.72 = (bf16[128,2048]{1,0:T(8,128)(2,1)S(1)}, bf16[128,2048]{1,0:T(8,128)(2,1)S(1)}, u32[]{:S(2)}, u32[]{:S(2)}) collective-permute-start(bf16[128,2048]{1,0:T(8,128)(2,1)S(1)} %get-tuple-element.365), channel_id=1, source_target_pairs={{0,1},{1,0},{2,3},{3,2},{4,5},{5,4},{6,7},{7,6},{8,9},{9,8},{10,11... | collective-permute-start | bytes 1572872 | tf_op jit(solution)/shard_map/ppermute | solution.py:452
  549.8 63.9 %collective-permute-start.114 = (bf16[64,2048]{1,0:T(8,128)(2,1)S(1)}, bf16[64,2048]{1,0:T(8,128)(2,1)S(1)}, u32[]{:S(2)}, u32[]{:S(2)}) collective-permute-start(bf16[64,2048]{1,0:T(8,128)(2,1)S(1)} %slice.1305), channel_id=1, source_target_pairs={{0,1},{1,0},{2,3},{3,2},{4,5},{5,4},{6,7},{7,6},{8,9},{9,8},{10,11... | collective-permute-start | bytes 786440 | tf_op jit(solution)/shard_map/ppermute | solution.py:452
  560.1 54.9 %collective-permute-start.115 = (bf16[64,2048]{1,0:T(8,128)(2,1)S(1)}, bf16[64,2048]{1,0:T(8,128)(2,1)S(1)}, u32[]{:S(2)}, u32[]{:S(2)}) collective-permute-start(bf16[64,2048]{1,0:T(8,128)(2,1)S(1)} %slice.1306), channel_id=1, source_target_pairs={{0,2},{1,3},{2,0},{3,1},{4,6},{5,7},{6,4},{7,5},{8,10},{9,11},{10,... | collective-permute-start | bytes 786440 | tf_op jit(solution)/shard_map/ppermute | solution.py:452
  569.3 39.1 %collective-permute-start.74 = (bf16[64,2048]{1,0:T(8,128)(2,1)S(1)}, bf16[64,2048]{1,0:T(8,128)(2,1)S(1)}, u32[]{:S(2)}, u32[]{:S(2)}) collective-permute-start(bf16[64,2048]{1,0:T(8,128)(2,1)S(1)} %slice.1245), channel_id=1, source_target_pairs={{0,1},{1,0},{2,3},{3,2},{4,5},{5,4},{6,7},{7,6},{8,9},{9,8},{10,11... | collective-permute-start | bytes 786440 | tf_op jit(solution)/shard_map/ppermute | solution.py:452
  572.3 36.8 %collective-permute-start.75 = (bf16[64,2048]{1,0:T(8,128)(2,1)S(1)}, bf16[64,2048]{1,0:T(8,128)(2,1)S(1)}, u32[]{:S(2)}, u32[]{:S(2)}) collective-permute-start(bf16[64,2048]{1,0:T(8,128)(2,1)S(1)} %slice.1246), channel_id=1, source_target_pairs={{0,2},{1,3},{2,0},{3,1},{4,6},{5,7},{6,4},{7,5},{8,10},{9,11},{10,... | collective-permute-start | bytes 786440 | tf_op jit(solution)/shard_map/ppermute | solution.py:452
  611.5 19.8 %collective-permute-start.89 = (bf16[128,2048]{1,0:T(8,128)(2,1)S(1)}, bf16[128,2048]{1,0:T(8,128)(2,1)S(1)}, u32[]{:S(2)}, u32[]{:S(2)}) collective-permute-start(bf16[128,2048]{1,0:T(8,128)(2,1)S(1)} %get-tuple-element.253), channel_id=1, source_target_pairs={{0,2},{1,3},{2,0},{3,1},{4,6},{5,7},{6,4},{7,5},{8,10},{9,11},{10,... | collective-permute-start | bytes 1572872 | tf_op jit(solution)/shard_map/ppermute | solution.py:452
  611.9 17.3 %collective-permute-start.102 = (bf16[2,64,2048]{2,1,0:T(8,128)(2,1)S(1)}, bf16[2,64,2048]{2,1,0:T(8,128)(2,1)S(1)}, u32[]{:S(2)}, u32[]{:S(2)}) collective-permute-start(bf16[2,64,2048]{2,1,0:T(8,128)(2,1)S(1)} %stack.229), channel_id=1, source_target_pairs={{0,2},{1,3},{2,0},{3,1},{4,6},{5,7},{6,4},{7,5},{8,10},{9,11},{10,... | collective-permute-start | bytes 1572872 | tf_op jit(solution)/shard_map/ppermute | solution.py:452
  613.7 26.0 %collective-permute-start.88 = (bf16[128,2048]{1,0:T(8,128)(2,1)S(1)}, bf16[128,2048]{1,0:T(8,128)(2,1)S(1)}, u32[]{:S(2)}, u32[]{:S(2)}) collective-permute-start(bf16[128,2048]{1,0:T(8,128)(2,1)S(1)} %get-tuple-element.253), channel_id=1, source_target_pairs={{0,1},{1,0},{2,3},{3,2},{4,5},{5,4},{6,7},{7,6},{8,9},{9,8},{10,11... | collective-permute-start | bytes 1572872 | tf_op jit(solution)/shard_map/ppermute | solution.py:452
  614.9 22.7 %collective-permute-start.57 = (bf16[128,2048]{1,0:T(8,128)(2,1)S(1)}, bf16[128,2048]{1,0:T(8,128)(2,1)S(1)}, u32[]{:S(2)}, u32[]{:S(2)}) collective-permute-start(bf16[128,2048]{1,0:T(8,128)(2,1)S(1)} %get-tuple-element.349), channel_id=1, source_target_pairs={{0,2},{1,3},{2,0},{3,1},{4,6},{5,7},{6,4},{7,5},{8,10},{9,11},{10,... | collective-permute-start | bytes 1572872 | tf_op jit(solution)/shard_map/ppermute | solution.py:452
  620.8 18.1 %collective-permute-start.56 = (bf16[128,2048]{1,0:T(8,128)(2,1)S(1)}, bf16[128,2048]{1,0:T(8,128)(2,1)S(1)}, u32[]{:S(2)}, u32[]{:S(2)}) collective-permute-start(bf16[128,2048]{1,0:T(8,128)(2,1)S(1)} %get-tuple-element.349), channel_id=1, source_target_pairs={{0,1},{1,0},{2,3},{3,2},{4,5},{5,4},{6,7},{7,6},{8,9},{9,8},{10,11... | collective-permute-start | bytes 1572872 | tf_op jit(solution)/shard_map/ppermute | solution.py:452
  629.4 56.0 %collective-permute-start.101 = (bf16[64,2048]{1,0:T(8,128)(2,1)S(1)}, bf16[64,2048]{1,0:T(8,128)(2,1)S(1)}, u32[]{:S(2)}, u32[]{:S(2)}) collective-permute-start(bf16[64,2048]{1,0:T(8,128)(2,1)S(1)} %get-tuple-element.300), channel_id=1, source_target_pairs={{0,2},{1,3},{2,0},{3,1},{4,6},{5,7},{6,4},{7,5},{8,10},{9,11},{10,... | collective-permute-start | bytes 786440 | tf_op jit(solution)/shard_map/ppermute | solution.py:452
  631.3 55.1 %collective-permute-start.103 = (bf16[64,2048]{1,0:T(8,128)(2,1)S(1)}, bf16[64,2048]{1,0:T(8,128)(2,1)S(1)}, u32[]{:S(2)}, u32[]{:S(2)}) collective-permute-start(bf16[64,2048]{1,0:T(8,128)(2,1)S(1)} %get-tuple-element.301), channel_id=1, source_target_pairs={{0,1},{1,0},{2,3},{3,2},{4,5},{5,4},{6,7},{7,6},{8,9},{9,8},{10,11... | collective-permute-start | bytes 786440 | tf_op jit(solution)/shard_map/ppermute | solution.py:452
  637.6 64.1 %collective-permute-start.90 = (bf16[64,2048]{1,0:T(8,128)(2,1)S(1)}, bf16[64,2048]{1,0:T(8,128)(2,1)S(1)}, u32[]{:S(2)}, u32[]{:S(2)}) collective-permute-start(bf16[64,2048]{1,0:T(8,128)(2,1)S(1)} %slice.1269), channel_id=1, source_target_pairs={{0,1},{1,0},{2,3},{3,2},{4,5},{5,4},{6,7},{7,6},{8,9},{9,8},{10,11... | collective-permute-start | bytes 786440 | tf_op jit(solution)/shard_map/ppermute | solution.py:452
  646.8 55.6 %collective-permute-start.91 = (bf16[64,2048]{1,0:T(8,128)(2,1)S(1)}, bf16[64,2048]{1,0:T(8,128)(2,1)S(1)}, u32[]{:S(2)}, u32[]{:S(2)}) collective-permute-start(bf16[64,2048]{1,0:T(8,128)(2,1)S(1)} %slice.1270), channel_id=1, source_target_pairs={{0,2},{1,3},{2,0},{3,1},{4,6},{5,7},{6,4},{7,5},{8,10},{9,11},{10,... | collective-permute-start | bytes 786440 | tf_op jit(solution)/shard_map/ppermute | solution.py:452
  760.6 437.6 %reduce-scatter.14.cloned.1.call-start = ((), (), s32[]{:S(2)}) async-start(), calls=%async_computation.12 | async-start | bytes 6488064 | tf_op jit(solution)/shard_map/reduce_scatter | solution.py:611
  781.0 419.5 %reduce-scatter.12.cloned.1.call-start = ((), (), s32[]{:S(2)}) async-start(), calls=%async_computation.11 | async-start | bytes 6488064 | tf_op jit(solution)/shard_map/reduce_scatter | solution.py:611
  801.1 401.7 %reduce-scatter.10.cloned.1.call-start = ((), (), s32[]{:S(2)}) async-start(), calls=%async_computation.10 | async-start | bytes 6488064 | tf_op jit(solution)/shard_map/reduce_scatter | solution.py:611
  836.1 70.0 %collective-permute-start.13 = (bf16[64,2048]{1,0:T(8,128)(2,1)}, bf16[64,2048]{1,0:T(8,128)(2,1)}, u32[]{:S(2)}, u32[]{:S(2)}) collective-permute-start(bf16[64,2048]{1,0:T(8,128)(2,1)} %get-tuple-element.304), channel_id=1, source_target_pairs={{0,2},{1,3},{2,0},{3,1},{4,6},{5,7},{6,4},{7,5},{8,10},{9,11},{10,... | collective-permute-start | bytes 786440 | tf_op jit(solution)/shard_map/ppermute | solution.py:452
  837.2 69.5 %collective-permute-start.15 = (bf16[64,2048]{1,0:T(8,128)(2,1)}, bf16[64,2048]{1,0:T(8,128)(2,1)}, u32[]{:S(2)}, u32[]{:S(2)}) collective-permute-start(bf16[64,2048]{1,0:T(8,128)(2,1)} %get-tuple-element.305), channel_id=1, source_target_pairs={{0,1},{1,0},{2,3},{3,2},{4,5},{5,4},{6,7},{7,6},{8,9},{9,8},{10,11... | collective-permute-start | bytes 786440 | tf_op jit(solution)/shard_map/ppermute | solution.py:452
  862.0 343.1 %reduce-scatter.6.cloned.1.call-start = ((), (), s32[]{:S(2)}) async-start(), calls=%async_computation.8 | async-start | bytes 10027008 | tf_op jit(solution)/shard_map/reduce_scatter | solution.py:611
  915.8 133.8 %collective-permute-start.45 = (bf16[64,2048]{1,0:T(8,128)(2,1)}, bf16[64,2048]{1,0:T(8,128)(2,1)S(1)}, u32[]{:S(2)}, u32[]{:S(2)}) collective-permute-start(bf16[64,2048]{1,0:T(8,128)(2,1)} %get-tuple-element.312), channel_id=1, source_target_pairs={{0,2},{1,3},{2,0},{3,1},{4,6},{5,7},{6,4},{7,5},{8,10},{9,11},{10,... | collective-permute-start | bytes 786440 | tf_op jit(solution)/shard_map/ppermute | solution.py:452
  916.5 133.9 %collective-permute-start.47 = (bf16[64,2048]{1,0:T(8,128)(2,1)}, bf16[64,2048]{1,0:T(8,128)(2,1)}, u32[]{:S(2)}, u32[]{:S(2)}) collective-permute-start(bf16[64,2048]{1,0:T(8,128)(2,1)} %get-tuple-element.313), channel_id=1, source_target_pairs={{0,1},{1,0},{2,3},{3,2},{4,5},{5,4},{6,7},{7,6},{8,9},{9,8},{10,11... | collective-permute-start | bytes 786440 | tf_op jit(solution)/shard_map/ppermute | solution.py:452
  920.0 133.3 %collective-permute-start.77 = (bf16[64,2048]{1,0:T(8,128)(2,1)}, bf16[64,2048]{1,0:T(8,128)(2,1)}, u32[]{:S(2)}, u32[]{:S(2)}) collective-permute-start(bf16[64,2048]{1,0:T(8,128)(2,1)} %get-tuple-element.280), channel_id=1, source_target_pairs={{0,2},{1,3},{2,0},{3,1},{4,6},{5,7},{6,4},{7,5},{8,10},{9,11},{10,... | collective-permute-start | bytes 786440 | tf_op jit(solution)/shard_map/ppermute | solution.py:452
  920.7 133.4 %collective-permute-start.79 = (bf16[64,2048]{1,0:T(8,128)(2,1)}, bf16[64,2048]{1,0:T(8,128)(2,1)}, u32[]{:S(2)}, u32[]{:S(2)}) collective-permute-start(bf16[64,2048]{1,0:T(8,128)(2,1)} %get-tuple-element.281), channel_id=1, source_target_pairs={{0,1},{1,0},{2,3},{3,2},{4,5},{5,4},{6,7},{7,6},{8,9},{9,8},{10,11... | collective-permute-start | bytes 786440 | tf_op jit(solution)/shard_map/ppermute | solution.py:452
  1040.2 16.8 %collective-permute-start.60 = (bf16[2,64,2048]{2,1,0:T(8,128)(2,1)S(1)}, bf16[2,64,2048]{2,1,0:T(8,128)(2,1)S(1)}, u32[]{:S(2)}, u32[]{:S(2)}) collective-permute-start(bf16[2,64,2048]{2,1,0:T(8,128)(2,1)S(1)} %pad_maximum_fusion.17), channel_id=1, source_target_pairs={{0,1},{1,0},{2,3},{3,2},{4,5},{5,4},{6,7},{7,6},{8,9},{9,8},{10,11... | collective-permute-start | bytes 1572872 | tf_op jit(solution)/shard_map/ppermute | solution.py:452
  1053.3 15.7 %collective-permute-start.94 = (bf16[2,64,2048]{2,1,0:T(8,128)(2,1)S(1)}, bf16[2,64,2048]{2,1,0:T(8,128)(2,1)S(1)}, u32[]{:S(2)}, u32[]{:S(2)}) collective-permute-start(bf16[2,64,2048]{2,1,0:T(8,128)(2,1)S(1)} %stack.228), channel_id=1, source_target_pairs={{0,2},{1,3},{2,0},{3,1},{4,6},{5,7},{6,4},{7,5},{8,10},{9,11},{10,... | collective-permute-start | bytes 1572872 | tf_op jit(solution)/shard_map/ppermute | solution.py:452
  1070.1 16.2 %collective-permute-start.93 = (bf16[64,2048]{1,0:T(8,128)(2,1)}, bf16[64,2048]{1,0:T(8,128)(2,1)S(1)}, u32[]{:S(2)}, u32[]{:S(2)}) collective-permute-start(bf16[64,2048]{1,0:T(8,128)(2,1)} %get-tuple-element.288), channel_id=1, source_target_pairs={{0,2},{1,3},{2,0},{3,1},{4,6},{5,7},{6,4},{7,5},{8,10},{9,11},{10,... | collective-permute-start | bytes 786440 | tf_op jit(solution)/shard_map/ppermute | solution.py:452
  1113.5 29.6 %collective-permute-start.125 = (bf16[64,2048]{1,0:T(8,128)(2,1)}, bf16[64,2048]{1,0:T(8,128)(2,1)S(1)}, u32[]{:S(2)}, u32[]{:S(2)}) collective-permute-start(bf16[64,2048]{1,0:T(8,128)(2,1)} %get-tuple-element.292), channel_id=1, source_target_pairs={{0,2},{1,3},{2,0},{3,1},{4,6},{5,7},{6,4},{7,5},{8,10},{9,11},{10,... | collective-permute-start | bytes 786440 | tf_op jit(solution)/shard_map/ppermute | solution.py:452
  1114.3 28.8 %collective-permute-start.127 = (bf16[64,2048]{1,0:T(8,128)(2,1)}, bf16[64,2048]{1,0:T(8,128)(2,1)S(1)}, u32[]{:S(2)}, u32[]{:S(2)}) collective-permute-start(bf16[64,2048]{1,0:T(8,128)(2,1)} %get-tuple-element.293), channel_id=1, source_target_pairs={{0,1},{1,0},{2,3},{3,2},{4,5},{5,4},{6,7},{7,6},{8,9},{9,8},{10,11... | collective-permute-start | bytes 786440 | tf_op jit(solution)/shard_map/ppermute | solution.py:452
  (350 other events, 7097.8 us)
Sparse Core Ops, SparseCore 0:
  9.7 63.1 all-gather.3
  74.5 59.2 all-gather.7
  135.5 59.0 all-gather.5
  760.7 33.6 reduce-scatter.7
  796.6 63.5 reduce-scatter.13
  862.3 63.1 reduce-scatter.11
  927.8 63.2 reduce-scatter.9
  1033.9 92.0 reduce-scatter.5

commit v2 on v1

v2 whole, which is shorter than its diff:
```python
import jax
import jax.numpy as jnp
from jax import lax
from jax.experimental import pallas as pl
from jax.experimental.pallas import tpu as pltpu
from jax.sharding import PartitionSpec as P

HD = 128
LANES = 128
SCALE = HD ** (-0.5)
BF = jnp.bfloat16
F32 = jnp.float32
FORWARD_COST = 735_000_000
BACKWARD_COST = 1_650_000_000


def norm_rows(values, gain):
    return values * lax.rsqrt(jnp.mean(values * values, axis=-1, keepdims=True) + 1e-05) * gain


def swiglu(gate, upward):
    return jax.nn.silu(gate) * upward


def mm(left, right):
    return jnp.dot(left.astype(BF), right.astype(BF), preferred_element_type=F32)


def mm_nt(left, right):
    return lax.dot_general(
        left.astype(BF), right.astype(BF), (((1,), (1,)), ((), ())), preferred_element_type=F32
    )


def mm_tn(left, right):
    return lax.dot_general(
        left.astype(BF), right.astype(BF), (((0,), (0,)), ((), ())), preferred_element_type=F32
    )


def mm_exact(left, right):
    return jnp.dot(left, right, preferred_element_type=F32, precision=lax.Precision.HIGHEST)


def sigmoid(values):
    return 1.0 / (1.0 + jnp.exp(-values))


def softplus(values):
    return jnp.maximum(values, 0.0) + jnp.log1p(jnp.exp(-jnp.abs(values)))


def chunk_masks(rows):
    row_ids = lax.broadcasted_iota(jnp.int32, (rows, rows), 0)
    col_ids = lax.broadcasted_iota(jnp.int32, (rows, rows), 1)
    return row_ids, col_ids


def chunk_gates(small, scal_ref, aux, tri):
    rows = small.shape[0]
    log_alpha = scal_ref[0:1, :] * softplus(small + scal_ref[1:2, :])
    beta = sigmoid(small)
    decay_sum = mm_exact(tri, log_alpha)
    last = decay_sum[rows - 1 : rows, :]
    carried = aux[:, 4:5]
    growth = jnp.exp(decay_sum) * carried
    tail = jnp.exp(last - decay_sum) * aux[:, 5:6]
    keep = jnp.exp(last) * carried[rows - 1 : rows, :]
    return log_alpha, beta, decay_sum, growth, tail, keep


def conv_of(ext_ref, conv_ref, aux, m, index, head, rows, width):
    lanes = slice(index * width + head * HD, index * width + (head + 1) * HD)
    own = slice(head * HD, (head + 1) * HD)
    total = ext_ref[m, 8 : 8 + rows, lanes] * conv_ref[4 * index : 4 * index + 1, own]
    for j in range(1, 4):
        line = slice(4 * index + j, 4 * index + j + 1)
        total = total + ext_ref[m, 8 - j : 8 - j + rows, lanes] * conv_ref[line, own] * aux[:, j : j + 1]
    return total


def invert_unit_lower(powers, row_ids, col_ids):
    rows = row_ids.shape[0]
    eye = (row_ids == col_ids).astype(F32)
    pair = (row_ids // 2) == (col_ids // 2)
    inverses = [eye - jnp.where(pair, power, 0.0) for power in powers]
    half = 2
    while half < rows:
        joint = ((row_ids // (2 * half)) == (col_ids // (2 * half))) & (
            (row_ids // half) != (col_ids // half)
        )
        lows = [inverse.astype(BF) for inverse in inverses]
        firsts = [mm(low, jnp.where(joint, power, 0.0)) for low, power in zip(lows, powers)]
        inverses = [
            inverse - mm(first, low) for inverse, first, low in zip(inverses, firsts, lows)
        ]
        half *= 2
    return [inverse.astype(BF) for inverse in inverses]


def forward_kernel(
    heads, place_ref, raw_ref, aux_ref, segrow_ref, conv_ref, scal_ref, gain_ref,
    mixed_ref, core_ref, inv_ref, upd_ref, st_ref, ext_ref, state_ref,
):
    step = pl.program_id(0)
    group, rows = raw_ref.shape[1:3]
    width = heads * HD
    row_ids, col_ids = chunk_masks(rows)
    tri = (row_ids >= col_ids).astype(F32)
    strict = row_ids > col_ids

    @pl.when(step == 0)
    def _():
        ext_ref[:, 0:8, :] = jnp.zeros((group, 8, 3 * width), F32)
        state_ref[...] = jnp.zeros_like(state_ref)

    ext_ref[:, 8 : 8 + rows, :] = raw_ref[0, :, :, 0 : 3 * width]
    chains = [(m, h) for m in range(group) for h in range(heads)]
    stacked, values, powers, outs, betas, growths, tails, keeps = [], [], [], [], [], [], [], []
    for m in range(group):
        aux = aux_ref[m, 0]
        small = raw_ref[0, m, :, 4 * width : 4 * width + LANES]
        _, beta, decay_sum, growth, tail, keep = chunk_gates(small, scal_ref, aux, tri)
        decay_rows = decay_sum.T
        below = (row_ids >= col_ids) & (aux[:, 0:1] == segrow_ref[m, 0, 0:1, :])
        for head in range(heads):
            query = conv_of(ext_ref, conv_ref, aux, m, 0, head, rows, width)
            query = query * sigmoid(query)
            query = query * (
                lax.rsqrt(jnp.sum(query * query, axis=-1, keepdims=True) + 1e-06) * SCALE
            )
            key = conv_of(ext_ref, conv_ref, aux, m, 1, head, rows, width)
            key = key * sigmoid(key)
            key = key * lax.rsqrt(jnp.sum(key * key, axis=-1, keepdims=True) + 1e-06)
            value = conv_of(ext_ref, conv_ref, aux, m, 2, head, rows, width)
            value = value * sigmoid(value)
            b_col = beta[:, heads + head : heads + head + 1]
            spread = decay_sum[:, head : head + 1] - decay_rows[head : head + 1, :]
            inside = jnp.exp(jnp.where(below, spread, -1e30))
            both = jnp.concatenate([key, query], axis=0).astype(BF)
            dots = mm_nt(both, both[:rows])
            stacked.append(both)
            values.append(value)
            powers.append(jnp.where(strict, b_col * dots[:rows] * inside, 0.0))
            outs.append((dots[rows:] * inside).astype(BF))
            betas.append(b_col)
            growths.append(growth[:, head : head + 1])
            tails.append(tail[:, head : head + 1])
            keeps.append(keep[:, head : head + 1])
    inverses = invert_unit_lower(powers, row_ids, col_ids)
    states = [state_ref[m, h] for m, h in chains]
    lows = [state.astype(BF) for state in states]
    applied = [mm(both, low) for both, low in zip(stacked, lows)]
    updates = []
    for i, (m, h) in enumerate(chains):
        st_ref[0, m, h] = lows[i]
        inv_ref[0, m, h] = inverses[i]
        rest = betas[i] * (values[i] - growths[i] * applied[i][:rows])
        updates.append(mm(inverses[i], rest).astype(BF))
    for i, (m, h) in enumerate(chains):
        lanes = slice(h * HD, (h + 1) * HD)
        upd_ref[0, m, :, lanes] = updates[i]
        state_ref[m, h] = keeps[i] * states[i] + mm_tn(
            stacked[i][:rows].astype(F32) * tails[i], updates[i]
        )
        core = growths[i] * applied[i][rows:] + mm(outs[i], updates[i])
        core_ref[0, m, :, lanes] = core
        outgate = raw_ref[0, m, :, 3 * width + h * HD : 3 * width + (h + 1) * HD]
        normed = core * lax.rsqrt(jnp.mean(core * core, axis=-1, keepdims=True) + 1e-05)
        mixed_ref[0, m, :, lanes] = (
            normed * gain_ref[0:1, lanes] * (outgate * sigmoid(outgate))
        ).astype(BF)
    ext_ref[:, 0:8, :] = ext_ref[:, rows : rows + 8, :]


def backward_kernel(
    heads, place_ref, raw_ref, prev_ref, aux_ref, segrow_ref, conv_ref, scal_ref, gain_ref,
    dmix_ref, core_ref, inv_ref, upd_ref, st_ref,
    draw_ref, dconv_ref, dscal_ref, dgain_ref, ext_ref, dext_ref, dstate_ref,
):
    step = pl.program_id(0)
    group, rows = raw_ref.shape[1:3]
    width = heads * HD

    @pl.when(step == 0)
    def _():
        dext_ref[:, rows : rows + 8, :] = jnp.zeros((group, 8, 3 * width), F32)
        dstate_ref[...] = jnp.zeros_like(dstate_ref)
        dconv_ref[...] = jnp.zeros_like(dconv_ref)
        dscal_ref[...] = jnp.zeros_like(dscal_ref)
        dgain_ref[...] = jnp.zeros_like(dgain_ref)

    @pl.when(step > 0)
    def _():
        dext_ref[:, rows : rows + 8, :] = dext_ref[:, 0:8, :]

    ext_ref[:, 0:8, :] = prev_ref[0, :, :, 0 : 3 * width]
    ext_ref[:, 8 : 8 + rows, :] = raw_ref[0, :, :, 0 : 3 * width]
    row_ids, col_ids = chunk_masks(rows)
    tri = (row_ids >= col_ids).astype(F32)
    upper = (row_ids <= col_ids).astype(F32)
    strict = row_ids > col_ids
    lane_ids = lax.broadcasted_iota(jnp.int32, (rows, LANES), 1)
    line_ids = lax.broadcasted_iota(jnp.int32, (LANES, rows), 0)
    last_row = lax.broadcasted_iota(jnp.int32, (rows, 1), 0) == rows - 1

    def conv_back(m, index, head, aux, d_conv):
        lanes = slice(index * width + head * HD, index * width + (head + 1) * HD)
        own = slice(head * HD, (head + 1) * HD)
        dext_ref[m, 0:rows, lanes] = d_conv
        total = d_conv * conv_ref[4 * index : 4 * index + 1, own]
        dconv_ref[4 * index : 4 * index + 1, own] += jnp.sum(
            d_conv * ext_ref[m, 8 : 8 + rows, lanes], axis=0, keepdims=True
        )
        for j in range(1, 4):
            line = slice(4 * index + j, 4 * index + j + 1)
            total = total + dext_ref[m, j : j + rows, lanes] * conv_ref[line, own] * aux[:, 7 + j : 8 + j]
            dconv_ref[line, own] += jnp.sum(
                d_conv * ext_ref[m, 8 - j : 8 - j + rows, lanes] * aux[:, j : j + 1],
                axis=0,
                keepdims=True,
            )
        draw_ref[0, m, :, lanes] = total.astype(BF)

    for m in range(group):
        aux = aux_ref[m, 0]
        small = raw_ref[0, m, :, 4 * width : 4 * width + LANES]
        log_alpha, beta, decay_sum, growth, tail, keep = chunk_gates(small, scal_ref, aux, tri)
        decay_rows = decay_sum.T
        below = (row_ids >= col_ids) & (aux[:, 0:1] == segrow_ref[m, 0, 0:1, :])
        d_decay = jnp.zeros((rows, LANES), F32)
        d_beta = jnp.zeros((rows, LANES), F32)
        d_decay_lines = jnp.zeros((LANES, rows), F32)
        everyone = range(heads)
        own_lanes = [slice(h * HD, (h + 1) * HD) for h in everyone]
        b_cols = [beta[:, heads + h : heads + h + 1] for h in everyone]
        g_cols = [growth[:, h : h + 1] for h in everyone]
        t_cols = [tail[:, h : h + 1] for h in everyone]
        keeps = [keep[:, h : h + 1] for h in everyone]
        d_cores, queries, keys, values = [], [], [], []
        for h in everyone:
            lanes = own_lanes[h]
            gate_lanes = slice(3 * width + h * HD, 3 * width + (h + 1) * HD)
            outgate = raw_ref[0, m, :, gate_lanes]
            gate = sigmoid(outgate)
            core = core_ref[0, m, :, lanes]
            inv_norm = lax.rsqrt(jnp.mean(core * core, axis=-1, keepdims=True) + 1e-05)
            normed = core * inv_norm
            d_mixed = dmix_ref[0, m, :, lanes].astype(F32)
            gain = gain_ref[0:1, lanes]
            d_silu = d_mixed * (outgate * gate)
            dgain_ref[0:1, lanes] += jnp.sum(d_silu * normed, axis=0, keepdims=True)
            draw_ref[0, m, :, gate_lanes] = (
                d_mixed * normed * gain * (gate * (1.0 + outgate * (1.0 - gate)))
            ).astype(BF)
            d_normed = d_silu * gain
            d_cores.append(
                (inv_norm * (d_normed - normed * jnp.mean(d_normed * normed, axis=-1, keepdims=True))).astype(BF)
            )
            parts = []
            for index in range(3):
                conv = conv_of(ext_ref, conv_ref, aux, m, index, h, rows, width)
                gate = sigmoid(conv)
                act = conv * gate
                slope = gate * (1.0 + conv * (1.0 - gate))
                if index == 2:
                    parts.append((act, slope))
                else:
                    root = lax.rsqrt(jnp.sum(act * act, axis=-1, keepdims=True) + 1e-06)
                    parts.append((act * root, slope * root))
            queries.append(parts[0])
            keys.append(parts[1])
            values.append(parts[2])
        insides = [
            jnp.exp(jnp.where(below, decay_sum[:, h : h + 1] - decay_rows[h : h + 1, :], -1e30))
            for h in everyone
        ]
        key_lows = [keys[h][0].astype(BF) for h in everyone]
        query_lows = [(queries[h][0] * SCALE).astype(BF) for h in everyone]
        dots = [
            mm_nt(jnp.concatenate([key_lows[h], query_lows[h]], axis=0), key_lows[h])
            for h in everyone
        ]
        updates = [upd_ref[0, m, :, own_lanes[h]] for h in everyone]
        states = [st_ref[0, m, h] for h in everyone]
        d_states = [dstate_ref[m, h] for h in everyone]
        d_state_lows = [item.astype(BF) for item in d_states]
        outs = [dots[h][rows:] * insides[h] for h in everyone]
        d_updates = [
            mm_tn(outs[h], d_cores[h]) + mm(keys[h][0] * t_cols[h], d_state_lows[h])
            for h in everyone
        ]
        d_rests = [mm_tn(inv_ref[0, m, h], d_updates[h]) for h in everyone]
        pairs = [
            jnp.concatenate([d_cores[h], d_rests[h].astype(BF)], axis=0) for h in everyone
        ]
        boths = [mm_nt(pairs[h], updates[h]) for h in everyone]
        sides = [mm_nt(pairs[h], states[h]) for h in everyone]
        d_tail_keys = [mm_nt(updates[h], d_state_lows[h]) for h in everyone]
        for h in everyone:
            key, query = keys[h][0], queries[h][0]
            d_weights, d_power = boths[h][:rows], -boths[h][rows:]
            core_state, rest_state = sides[h][:rows], sides[h][rows:]
            key_dots = dots[h][:rows]
            d_query_dots = d_weights * insides[h]
            power_in = jnp.where(strict, d_power * insides[h], 0.0)
            d_key_dots = power_in * b_cols[h]
            reach = d_weights * outs[h] + d_key_dots * key_dots
            key_rest = jnp.sum(key * rest_state, axis=-1, keepdims=True)
            d_beta_col = (
                jnp.sum(power_in * key_dots, axis=-1, keepdims=True)
                + jnp.sum(d_rests[h] * values[h][0], axis=-1, keepdims=True)
                - g_cols[h] * key_rest
            )
            d_growth = SCALE * jnp.sum(query * core_state, axis=-1, keepdims=True) - b_cols[h] * key_rest
            tail_part = t_cols[h] * jnp.sum(d_tail_keys[h] * key, axis=-1, keepdims=True)
            last_part = jnp.sum(tail_part, axis=0, keepdims=True) + keeps[h] * jnp.sum(
                jnp.sum(d_states[h] * states[h].astype(F32), axis=0, keepdims=True),
                axis=-1,
                keepdims=True,
            )
            d_sum_col = (
                jnp.sum(reach, axis=-1, keepdims=True)
                + g_cols[h] * d_growth
                - tail_part
                + jnp.where(last_row, last_part, 0.0)
            )
            d_decay = jnp.where(lane_ids == h, d_sum_col, d_decay)
            d_beta = jnp.where(lane_ids == heads + h, d_beta_col, d_beta)
            d_decay_lines = jnp.where(
                line_ids == h, jnp.sum(reach, axis=0, keepdims=True), d_decay_lines
            )
            scale_rest = -(b_cols[h] * g_cols[h])
            dot_grads = jnp.concatenate([d_key_dots, d_query_dots], axis=0).astype(BF)
            by_key = mm(dot_grads, key_lows[h])
            d_query = (g_cols[h] * core_state + by_key[rows:]) * SCALE
            d_key = (
                scale_rest * rest_state
                + t_cols[h] * d_tail_keys[h]
                + by_key[:rows]
                + mm_tn(dot_grads, jnp.concatenate([key_lows[h], query_lows[h]], axis=0))
            )
            dstate_ref[m, h] = keeps[h] * d_states[h] + mm_tn(
                jnp.concatenate([query * (SCALE * g_cols[h]), key * scale_rest], axis=0), pairs[h]
            )
            conv_back(
                m, 0, h, aux,
                queries[h][1] * (d_query - query * jnp.sum(query * d_query, axis=-1, keepdims=True)),
            )
            conv_back(
                m, 1, h, aux,
                keys[h][1] * (d_key - key * jnp.sum(key * d_key, axis=-1, keepdims=True)),
            )
            conv_back(m, 2, h, aux, b_cols[h] * d_rests[h] * values[h][1])
        d_log = mm_exact(upper, d_decay - d_decay_lines.T)
        d_arg = d_log * scal_ref[0:1, :] * sigmoid(small + scal_ref[1:2, :])
        dscal_ref[0:1, :] += jnp.sum(d_log * log_alpha, axis=0, keepdims=True)
        dscal_ref[1:2, :] += jnp.sum(d_arg, axis=0, keepdims=True)
        draw_ref[0, m, :, 4 * width : 4 * width + LANES] = (
            d_arg + d_beta * beta * (1.0 - beta)
        ).astype(BF)


def mixer_shapes(raw):
    blocks, group, rows, total = raw.shape
    heads = (total - LANES) // (4 * HD)
    return blocks, group, rows, heads, heads * HD, total


def whole(shape):
    return pl.BlockSpec(shape, lambda c, place: (0,) * len(shape))


PARAMS = dict(dimension_semantics=("arbitrary",), vmem_limit_bytes=56 * 1024 * 1024)


def mixer_forward(place, raw, aux, segrow, conv_rows, scal, gain):
    blocks, group, rows, heads, width, total = mixer_shapes(raw)
    at = lambda c, place: (place[c], 0, 0, 0)
    seq = lambda c, place: (c, 0, 0, 0)
    seq5 = lambda c, place: (c, 0, 0, 0, 0)
    fact = lambda c, place: (0, c, 0, 0)

    def body(*refs):
        forward_kernel(heads, *refs)

    return pl.pallas_call(
        body,
        grid_spec=pltpu.PrefetchScalarGridSpec(
            num_scalar_prefetch=1,
            grid=(blocks,),
            in_specs=[
                pl.BlockSpec((1, group, rows, total), at),
                pl.BlockSpec((group, 1, rows, 16), fact),
                pl.BlockSpec((group, 1, 8, rows), fact),
                whole(conv_rows.shape),
                whole(scal.shape),
                whole(gain.shape),
            ],
            out_specs=[
                pl.BlockSpec((1, group, rows, width), at),
                pl.BlockSpec((1, group, rows, width), seq),
                pl.BlockSpec((1, group, heads, rows, rows), seq5),
                pl.BlockSpec((1, group, rows, width), seq),
                pl.BlockSpec((1, group, heads, HD, HD), seq5),
            ],
            scratch_shapes=[
                pltpu.VMEM((group, rows + 8, 3 * width), F32),
                pltpu.VMEM((group, heads, HD, HD), F32),
            ],
        ),
        out_shape=[
            jax.ShapeDtypeStruct((blocks, group, rows, width), BF),
            jax.ShapeDtypeStruct((blocks, group, rows, width), F32),
            jax.ShapeDtypeStruct((blocks, group, heads, rows, rows), BF),
            jax.ShapeDtypeStruct((blocks, group, rows, width), BF),
            jax.ShapeDtypeStruct((blocks, group, heads, HD, HD), BF),
        ],
        compiler_params=pltpu.CompilerParams(**PARAMS),
        cost_estimate=pl.CostEstimate(
            flops=FORWARD_COST * blocks * group * heads, bytes_accessed=8_000_000, transcendentals=0
        ),
        name="mixer_forward",
    )(place, raw, aux, segrow, conv_rows, scal, gain)


def mixer_backward(place, raw, aux, segrow, conv_rows, scal, gain, d_mixed, saved):
    blocks, group, rows, heads, width, total = mixer_shapes(raw)
    core, inverse, update, states = saved
    back = lambda c: blocks - 1 - c
    at = lambda c, place: (place[back(c)], 0, 0, 0)
    before = lambda c, place: (place[jnp.maximum(back(c) - 1, 0)], 0, rows // 8 - 1, 0)
    seq = lambda c, place: (back(c), 0, 0, 0)
    seq5 = lambda c, place: (back(c), 0, 0, 0, 0)
    fact = lambda c, place: (0, back(c), 0, 0)

    def body(*refs):
        backward_kernel(heads, *refs)

    return pl.pallas_call(
        body,
        grid_spec=pltpu.PrefetchScalarGridSpec(
            num_scalar_prefetch=1,
            grid=(blocks,),
            in_specs=[
                pl.BlockSpec((1, group, rows, total), at),
                pl.BlockSpec((1, group, 8, total), before),
                pl.BlockSpec((group, 1, rows, 16), fact),
                pl.BlockSpec((group, 1, 8, rows), fact),
                whole(conv_rows.shape),
                whole(scal.shape),
                whole(gain.shape),
                pl.BlockSpec((1, group, rows, width), at),
                pl.BlockSpec((1, group, rows, width), seq),
                pl.BlockSpec((1, group, heads, rows, rows), seq5),
                pl.BlockSpec((1, group, rows, width), seq),
                pl.BlockSpec((1, group, heads, HD, HD), seq5),
            ],
            out_specs=[
                pl.BlockSpec((1, group, rows, total), at),
                whole((16, width)),
                whole((8, LANES)),
                whole((8, width)),
            ],
            scratch_shapes=[
                pltpu.VMEM((group, rows + 8, 3 * width), F32),
                pltpu.VMEM((group, rows + 8, 3 * width), F32),
                pltpu.VMEM((group, heads, HD, HD), F32),
            ],
        ),
        out_shape=[
            jax.ShapeDtypeStruct((blocks, group, rows, total), BF),
            jax.ShapeDtypeStruct((16, width), F32),
            jax.ShapeDtypeStruct((8, LANES), F32),
            jax.ShapeDtypeStruct((8, width), F32),
        ],
        compiler_params=pltpu.CompilerParams(**PARAMS),
        cost_estimate=pl.CostEstimate(
            flops=BACKWARD_COST * blocks * group * heads, bytes_accessed=12_000_000, transcendentals=0
        ),
        name="mixer_backward",
    )(place, raw, raw, aux, segrow, conv_rows, scal, gain, d_mixed, core, inverse, update, states)


def hop(values, bit, axis="head"):
    size = lax.axis_size(axis)
    return lax.ppermute(values, axis, [(i, i ^ bit) for i in range(size)])


def after(values, *earlier):
    kept = [item for group in earlier for item in (group if isinstance(group, list) else [group])]
    if not kept:
        return values
    return lax.optimization_barrier((values, *kept))[0]


def butterfly(values, axes):
    for axis in axes:
        bit = 1
        while bit < lax.axis_size(axis):
            values = values + hop(values, bit, axis)
            bit *= 2
    return values


def gather_near(values, *earlier):
    if earlier:
        values = after(values, *earlier)
    if lax.axis_size("head") != 4:
        return [lax.all_gather(values, "head", axis=0, tiled=True)]
    return [values, hop(values, 1), hop(values, 2)]


def gather_far(near, *earlier):
    if len(near) == 1:
        return []
    half = near[0].shape[0] // 2
    return [hop(after(near[2][:half], *earlier), 1), hop(after(near[1][half:], *earlier), 2)]


def block_parts(size, rows):
    if size != 4:
        return [[(0, r * rows, rows)] for r in range(size)]
    half = rows // 2
    return [[(0, 0, rows)], [(1, 0, rows)], [(2, 0, rows)], [(3, 0, half), (4, 0, half)]]


def joined(arrays):
    return arrays[0] if len(arrays) == 1 else jnp.concatenate(arrays, axis=0)


def scatter_plan(size, rows):
    half = rows // 2
    if size != 4:
        return [size * rows], {(r, h): (0, r * rows + h * half) for r in range(size) for h in (0, 1)}
    return [rows, rows, 2 * rows], {
        (1, 0): (0, 0), (3, 0): (0, half),
        (2, 1): (1, 0), (3, 1): (1, half),
        (0, 0): (2, 0), (0, 1): (2, half), (2, 0): (2, 2 * half), (1, 1): (2, 3 * half),
    }


def scatter_near(arrays, *earlier):
    if len(arrays) == 1:
        part = after(arrays[0], *earlier)
        return [lax.psum_scatter(part, "head", scatter_dimension=0, tiled=True)]
    to_x, to_y, keep = arrays
    return [hop(after(to_x, *earlier), 1), hop(after(to_y, *earlier), 2), keep]


def scatter_far(near):
    if len(near) == 1:
        return near[0].astype(F32)
    in_x, in_y, keep = near
    half = in_x.shape[0] // 2
    pass_y = (keep[2 * half : 3 * half].astype(F32) + in_x[half:].astype(F32)).astype(BF)
    pass_x = (keep[3 * half :].astype(F32) + in_y[half:].astype(F32)).astype(BF)
    last_y = hop(pass_y, 2).astype(F32)
    last_x = hop(pass_x, 1).astype(F32)
    near_sum = jnp.concatenate([in_x[:half], in_y[:half]], axis=0).astype(F32)
    last = jnp.concatenate([last_y, last_x], axis=0)
    return keep[: 2 * half].astype(F32) + near_sum + last


def arranged(product, size):
    rows = product.shape[0] // size
    counts, where = scatter_plan(size, rows)
    half = rows // 2
    pieces = [[None] * (count // half) for count in counts]
    for (block, h), (index, at) in where.items():
        start = block * rows + h * half
        pieces[index][at // half] = product[start : start + half]
    return [jnp.concatenate(item, axis=0).astype(BF) for item in pieces]


def ffn_kernel(turns, rows, parts, n_pieces, where, n_out, aliased, *refs):
    mids, cots = refs[:n_pieces], refs[n_pieces : 2 * n_pieces]
    wg_ref, wu_ref, wd_ref = refs[2 * n_pieces : 2 * n_pieces + 3]
    refs = refs[2 * n_pieces + 3 + (2 * n_out if aliased else 0) :]
    act_ref, dg_ref, du_ref, xo_ref, co_ref = refs[:5]
    gm_refs, ff_refs = refs[5 : 5 + n_out], refs[5 + n_out : 5 + 2 * n_out]
    wg, wu, wd, xbuf, cbuf, gm_buf, ff_buf, w_sem, x_sem, c_sem, o_sem = refs[5 + 2 * n_out :]
    step = pl.program_id(0)
    half = rows // 2
    steps = len(turns)

    def loads(turn):
        slot = turn % 2
        found = []
        for arrays, buf, sem in ((mids, xbuf, x_sem), (cots, cbuf, c_sem)):
            place = 0
            for k, (index, at, count) in enumerate(parts[turns[turn]]):
                found.append(
                    pltpu.make_async_copy(
                        arrays[index].at[at : at + count],
                        buf.at[slot, place : place + count],
                        sem.at[slot, k],
                    )
                )
                place += count
        return found

    def stores(turn):
        slot = turn % 2
        found = []
        for k, (buf, outs) in enumerate(((gm_buf, gm_refs), (ff_buf, ff_refs))):
            for h in (0, 1):
                index, at = where[(turns[turn], h)]
                found.append(
                    pltpu.make_async_copy(
                        buf.at[slot, h * half : (h + 1) * half],
                        outs[index].at[at : at + half],
                        o_sem.at[slot, 2 * k + h],
                    )
                )
        return found

    weights = [
        pltpu.make_async_copy(src, dst, w_sem.at[k])
        for k, (src, dst) in enumerate(((wg_ref, wg), (wu_ref, wu), (wd_ref, wd)))
    ]

    @pl.when(step == 0)
    def _():
        for copy in loads(0):
            copy.start()
        for copy in weights:
            copy.start()

    for turn in range(steps):
        @pl.when(step == turn)
        def _(turn=turn):
            if turn + 1 < steps:
                for copy in loads(turn + 1):
                    copy.start()
            for copy in loads(turn):
                copy.wait()
            if turn >= 2:
                for copy in stores(turn - 2):
                    copy.wait()

    slot = lax.rem(step, 2)

    @pl.when(step == 0)
    def _():
        weights[0].wait()

    x = xbuf[slot]
    gate = jnp.dot(x, wg[...], preferred_element_type=F32)

    @pl.when(step == 0)
    def _():
        weights[1].wait()

    upward = jnp.dot(x, wu[...], preferred_element_type=F32)

    @pl.when(step == 0)
    def _():
        weights[2].wait()

    cot = cbuf[slot]
    d_act = jnp.dot(cot, wd[...], preferred_element_type=F32)
    open_ = sigmoid(gate)
    silu = gate * open_
    act = (silu * upward).astype(BF)
    d_gate = (d_act * upward * open_ * (1.0 + gate * (1.0 - open_))).astype(BF)
    d_up = (d_act * silu).astype(BF)
    act_ref[0] = act
    dg_ref[0] = d_gate
    du_ref[0] = d_up
    xo_ref[0] = x
    co_ref[0] = cot
    gm_buf[slot] = (mm_nt(d_gate, wg[...]) + mm_nt(d_up, wu[...])).astype(BF)
    ff_buf[slot] = mm_nt(act, wd[...]).astype(BF)
    for turn in range(steps):
        @pl.when(step == turn)
        def _(turn=turn):
            for copy in stores(turn):
                copy.start()
            if turn == steps - 1:
                for earlier in range(max(0, steps - 2), steps):
                    for copy in stores(earlier):
                        copy.wait()


def ffn_stage(turns, mids, cots, weights, size, filled=None):
    width, hidden = weights[0].shape
    rows = mids[0].shape[0] if size == 4 else mids[0].shape[0] // size
    parts = block_parts(size, rows)
    counts, where = scatter_plan(size, rows)
    aliased = filled is not None
    filled = list(filled) if aliased else []

    def body(*refs):
        ffn_kernel(turns, rows, parts, len(mids), where, len(counts), aliased, *refs)

    anywhere = pl.BlockSpec(memory_space=pl.ANY)
    by_block = lambda last: pl.BlockSpec((1, rows, last), lambda i: (i, 0, 0))
    steps = len(turns)
    first = 2 * len(mids) + 3
    out = pl.pallas_call(
        body,
        grid=(steps,),
        in_specs=[anywhere] * (first + len(filled)),
        out_specs=[by_block(hidden)] * 3 + [by_block(width)] * 2 + [anywhere] * (2 * len(counts)),
        out_shape=[jax.ShapeDtypeStruct((steps, rows, hidden), BF)] * 3
        + [jax.ShapeDtypeStruct((steps, rows, width), BF)] * 2
        + [jax.ShapeDtypeStruct((c, width), BF) for c in counts] * 2,
        input_output_aliases={first + k: 5 + k for k in range(len(filled))},
        scratch_shapes=[
            pltpu.VMEM((width, hidden), BF),
            pltpu.VMEM((width, hidden), BF),
            pltpu.VMEM((width, hidden), BF),
            pltpu.VMEM((2, rows, width), BF),
            pltpu.VMEM((2, rows, width), BF),
            pltpu.VMEM((2, rows, width), BF),
            pltpu.VMEM((2, rows, width), BF),
            pltpu.SemaphoreType.DMA((3,)),
            pltpu.SemaphoreType.DMA((2, 2)),
            pltpu.SemaphoreType.DMA((2, 2)),
            pltpu.SemaphoreType.DMA((2, 4)),
        ],
        compiler_params=pltpu.CompilerParams(**PARAMS),
        cost_estimate=pl.CostEstimate(
            flops=steps * rows * width * hidden * 20, bytes_accessed=30_000_000, transcendentals=0
        ),
        name="ffn_stage",
    )(*mids, *cots, *weights, *filled)
    flat = [array.reshape(steps * rows, array.shape[-1]) for array in out[:5]]
    return flat, list(out[5:])


def wgrad_kernel(count, *refs):
    lefts, rights, out_ref = refs[:count], refs[count : 2 * count], refs[2 * count]
    total = mm_tn(lefts[0][...], rights[0][...])
    for left, right in zip(lefts[1:], rights[1:]):
        total = total + mm_tn(left[...], right[...])
    out_ref[...] = total.astype(BF)


def weight_gradient(lefts, rights):
    depth, wide = lefts[0].shape
    columns = rights[0].shape[1]
    tile = 512 if wide % 512 == 0 else wide
    count = len(lefts)
    return pl.pallas_call(
        lambda *refs: wgrad_kernel(count, *refs),
        grid=(wide // tile,),
        in_specs=[pl.BlockSpec((depth, tile), lambda i: (0, i))] * count
        + [pl.BlockSpec((depth, columns), lambda i: (0, 0))] * count,
        out_specs=pl.BlockSpec((tile, columns), lambda i: (i, 0)),
        out_shape=jax.ShapeDtypeStruct((wide, columns), BF),
        compiler_params=pltpu.CompilerParams(**PARAMS),
        cost_estimate=pl.CostEstimate(
            flops=3 * count * depth * wide * columns, bytes_accessed=20_000_000, transcendentals=0
        ),
        name="weight_gradient",
    )(*lefts, *rights)


def block_places(size):
    base = lax.iota(jnp.int32, size)
    if size != 4:
        return base
    return base ^ lax.axis_index("head").astype(jnp.int32)


def contract_rows(left, right):
    return lax.dot_general(left, right, (((0,), (0,)), ((), ())), preferred_element_type=F32)


def contract_cols(left, right):
    return lax.dot_general(left, right, (((1,), (1,)), ((), ())), preferred_element_type=F32)


def times(left, right):
    return jnp.dot(left, right, preferred_element_type=F32)


def sequence_facts(doc_lengths, blocks, rows):
    span = blocks * rows
    ends = jnp.cumsum(doc_lengths, axis=-1)
    places = lax.iota(jnp.int32, span)
    segment = jnp.sum((places[None, :, None] >= ends[:, None, :]).astype(jnp.int32), axis=-1)
    columns = [segment]
    for j in range(1, 4):
        columns.append(
            (jnp.pad(segment, ((0, 0), (j, 0)), constant_values=-1)[:, :-j] == segment)
        )
    by_chunk = segment.reshape(-1, blocks, rows)
    prior = jnp.pad(by_chunk[:, :-1, -1], ((0, 0), (1, 0)), constant_values=-1)
    columns.append((by_chunk == prior[:, :, None]).reshape(segment.shape))
    columns.append((by_chunk == by_chunk[:, :, -1:]).reshape(segment.shape))
    columns += [jnp.zeros_like(segment)] * 2
    for j in range(1, 4):
        columns.append(
            (jnp.pad(segment, ((0, 0), (0, j)), constant_values=-1)[:, j:] == segment)
        )
    columns += [jnp.zeros_like(segment)] * (16 - len(columns))
    aux = jnp.stack([item.astype(F32) for item in columns], axis=-1)
    aux = aux.reshape(-1, blocks, rows, 16)
    lines = jnp.broadcast_to(by_chunk.astype(F32)[:, :, None, :], by_chunk.shape[:2] + (8, rows))
    return aux, lines


def on_device(
    tokens, cotangent, token_counts, doc_lengths, norm_in, w_query, w_key, w_value, w_outgate,
    w_decay, w_beta, conv_weight, decay_log, dt_bias, gain_out, w_out, norm_mid, w_gate, w_up,
    w_down,
):
    micro_count, rows, width = tokens.shape
    blocks = lax.axis_size("head")
    group = micro_count // 2
    own_rows = group * rows
    span = own_rows * blocks
    heads = decay_log.shape[0]
    own = heads * HD
    groups = range(micro_count // group)
    my_places = lax.axis_index("head") * rows + lax.iota(jnp.int32, rows)
    live = (my_places[None, :] < token_counts[:, :1]).astype(F32)[:, :, None]
    place = block_places(blocks)
    aux, lines = sequence_facts(doc_lengths[:, 0], blocks, rows)
    conv_rows = jnp.pad(conv_weight.reshape(12, own), ((0, 4), (0, 0)))
    scal = jnp.zeros((8, LANES), F32)
    scal = scal.at[0, :heads].set(-jnp.exp(decay_log)).at[1, :heads].set(dt_bias)
    gain_row = jnp.broadcast_to(gain_out[None], (8, own))
    ffn_gate = lax.all_gather(w_gate, "dp", axis=0, tiled=True)
    ffn_up = lax.all_gather(w_up, "dp", axis=0, tiled=True)
    ffn_down = lax.all_gather(w_down, "dp", axis=0, tiled=True)

    def of_group(array, i):
        return array[i * group : (i + 1) * group]

    inputs, grads, lives, pulls_in, normed_in = [], [], [], [], []
    for i in groups:
        x = of_group(tokens, i).reshape(own_rows, width).astype(F32)
        normed, pull = jax.vjp(norm_rows, x, norm_in)
        inputs.append(x)
        pulls_in.append(pull)
        normed_in.append(normed.astype(BF))
        grads.append((of_group(cotangent, i).astype(F32) * of_group(live, i)).reshape(own_rows, width))
    cots = [item.astype(BF) for item in grads]
    in_a1 = gather_near(normed_in[0])
    w_in = jnp.concatenate(
        [after(w_query, in_a1), w_key, w_value, w_outgate, w_decay, w_beta,
         jnp.zeros((width, LANES - 2 * heads), BF)], axis=1
    )

    def project(full):
        return times(full, w_in).reshape(blocks, group, rows, 4 * own + LANES)

    def mix(raw, i):
        mixed, *saved = mixer_forward(
            place, raw, of_group(aux, i), of_group(lines, i), conv_rows, scal, gain_row
        )
        return mixed.reshape(span, own), saved

    def out_of(mixed):
        return arranged(times(mixed, w_out), blocks)

    def middle(i, attn):
        resid = inputs[i] + attn
        normed, pull = jax.vjp(norm_rows, resid, norm_mid)
        return resid, pull, normed.astype(BF)

    in_a2 = gather_far(in_a1)
    in_b1 = gather_near(normed_in[1], in_a2)
    full_a = joined(in_a1 + in_a2)
    raw_a = project(full_a)
    in_b2 = gather_far(in_b1)
    mixed_a, saved_a = mix(raw_a, 0)
    attn_a = out_of(after(mixed_a, in_b1))
    full_b = joined(in_b1 + in_b2)
    at_a1 = scatter_near(attn_a)
    raw_b = project(after(full_b, attn_a))
    cot_a1 = gather_near(cots[0], at_a1)
    mixed_b, saved_b = mix(after(raw_b, at_a1), 1)
    sum_a = scatter_far(at_a1)
    cot_a2 = gather_far(cot_a1)
    attn_b = out_of(after(mixed_b, sum_a, cot_a1))
    resid_a, pull_a, mid_a = middle(0, sum_a)
    mid_a1 = gather_near(mid_a)
    at_b1 = scatter_near(attn_b, cot_a1)
    mid_a2 = gather_far(mid_a1)
    sum_b = scatter_far(at_b1)
    resid_b, pull_b, mid_b = middle(1, sum_b)
    mid_b1 = gather_near(mid_b, mid_a2, cot_a2)
    cot_b1 = gather_near(cots[1], mid_a2, cot_a2)

    ffn_weights = [ffn_gate, ffn_up, ffn_down]
    first_turns = (1, 3) if blocks == 4 else tuple(range(blocks // 2))
    last_turns = tuple(r for r in range(blocks) if r not in first_turns)
    outs = len(scatter_plan(blocks, own_rows)[0])
    kept_a, begun = ffn_stage(first_turns, mid_a1 + mid_a2, cot_a1 + cot_a2, ffn_weights, blocks)
    mid_b2 = gather_far(mid_b1)
    cot_b2 = gather_far(cot_b1)
    begun = [after(begun[0], mid_b1)] + begun[1:]
    kept_a2, out_a = ffn_stage(
        last_turns, mid_a1 + mid_a2, cot_a1 + cot_a2, ffn_weights, blocks, begun
    )
    gm_a1 = scatter_near(out_a[:outs])
    near_b = mid_b1 + mid_b2
    near_b[0] = after(near_b[0], out_a[0])
    kept_b, begun = ffn_stage(first_turns, near_b, cot_b1 + cot_b2, ffn_weights, blocks)
    begun = [after(begun[0], gm_a1)] + begun[1:]
    kept_b2, out_b = ffn_stage(last_turns, near_b, cot_b1 + cot_b2, ffn_weights, blocks, begun)
    kept = [kept_a, kept_a2, kept_b, kept_b2]
    acts, gates, ups, mids, cot_all = [[item[k] for item in kept] for k in range(5)]

    def share(term):
        return lax.psum_scatter(term, "dp", scatter_dimension=0, tiled=True).astype(F32)

    def resid_back(i, pull, d_mid):
        d_resid, d_norm = pull(d_mid)
        d_resid = grads[i] + d_resid
        return d_resid, d_norm, d_resid.astype(BF)

    d_mid_a = scatter_far(gm_a1)
    gm_b1 = scatter_near(out_b[:outs], d_mid_a)
    d_resid_a, gain_mid_a, low_a = resid_back(0, pull_a, d_mid_a)
    gates[0] = after(gates[0], low_a)
    rg_a1 = gather_near(low_a)
    term_gate = weight_gradient(mids, gates)
    grad_gate = share(term_gate)
    rg_a2 = gather_far(rg_a1)
    d_mid_b = scatter_far(gm_b1)
    ups[0] = after(ups[0], term_gate, rg_a1, gm_b1)
    term_up = weight_gradient(mids, ups)
    grad_up = share(term_up)
    d_resid_b, gain_mid_b, low_b = resid_back(1, pull_b, d_mid_b)
    rg_b1 = gather_near(low_b)
    rg_b2 = gather_far(rg_b1)
    full_ra = joined(rg_a1 + rg_a2)
    full_rb = joined(rg_b1 + rg_b2)

    def back(i, full, raw, saved):
        d_mixed = contract_cols(full, w_out).reshape(blocks, group, rows, own)
        return mixer_backward(
            place, raw, of_group(aux, i), of_group(lines, i), conv_rows, scal, gain_row,
            d_mixed, saved,
        )

    def in_back(d_raw):
        return arranged(contract_cols(d_raw, w_in), blocks)

    d_raw_a, *sums_a = back(0, after(full_ra, term_up, low_b), raw_a, saved_a)
    d_raw_a = d_raw_a.reshape(span, 4 * own + LANES)
    acts[0] = after(acts[0], d_raw_a, rg_b1)
    term_down = weight_gradient(cot_all, acts)
    grad_down = share(term_down)
    d_in_a = in_back(after(d_raw_a, term_down, rg_b2))
    gi_a1 = scatter_near(d_in_a)
    ff_a1 = scatter_near(out_a[outs:], d_in_a)
    term_out = weight_gradient([after(full_ra, d_in_a), full_rb], [mixed_a, mixed_b])
    grad_out = share(term_out).T
    d_raw_b, *sums_b = back(1, after(full_rb, term_out, grad_gate), raw_b, saved_b)
    d_raw_b = d_raw_b.reshape(span, 4 * own + LANES)
    d_norm_a = scatter_far(gi_a1)
    ffn_a = scatter_far(ff_a1)
    ff_b1 = scatter_near(out_b[outs:], d_norm_a, ffn_a)
    d_in_b = in_back(after(d_raw_b, d_norm_a, ffn_a, grad_up))
    gi_b1 = scatter_near(d_in_b)
    term_in = weight_gradient([full_a, full_b], [d_raw_a, after(d_raw_b, d_in_b)])
    grad_in = share(term_in)
    ffn_b = scatter_far(ff_b1)
    d_norm_b = scatter_far(gi_b1)

    results, input_grads = [], []
    gain_in = jnp.zeros_like(norm_in)
    for i, (resid, ffn, d_resid, d_norm) in enumerate(
        ((resid_a, ffn_a, d_resid_a, d_norm_a), (resid_b, ffn_b, d_resid_b, d_norm_b))
    ):
        results.append((resid + ffn).astype(BF).reshape(group, rows, width))
        d_inputs, d_gain = pulls_in[i](d_norm)
        input_grads.append((d_inputs + d_resid).astype(BF).reshape(group, rows, width))
        gain_in = gain_in + d_gain
    gain_mid = gain_mid_a + gain_mid_b
    small_sums = [left + right for left, right in zip(sums_a, sums_b)]
    small_sums[0] = after(small_sums[0], d_in_b)
    wide = jnp.concatenate([small_sums[0][:12], small_sums[2][:4]], axis=0)
    wide = butterfly(wide, ("dp",))
    narrow = butterfly(small_sums[1], ("dp",))
    gains = butterfly(jnp.stack([gain_in, gain_mid]), ("dp", "head"))
    return (
        jnp.concatenate(results, axis=0),
        jnp.concatenate(input_grads, axis=0),
        gains[0],
        grad_in[:, :own],
        grad_in[:, own : 2 * own],
        grad_in[:, 2 * own : 3 * own],
        grad_in[:, 3 * own : 4 * own],
        grad_in[:, 4 * own : 4 * own + heads],
        grad_in[:, 4 * own + heads : 4 * own + 2 * heads],
        wide[:12].reshape(conv_weight.shape),
        narrow[0, :heads],
        narrow[1, :heads],
        wide[12],
        grad_out,
        gains[1],
        grad_gate,
        grad_up,
        grad_down,
    )


def solution(mesh):
    return jax.shard_map(
        on_device,
        mesh=mesh,
        in_specs=(
            P(None, ("dp", "head"), None),
            P(None, ("dp", "head"), None),
            P(None, "dp"),
            P(None, "dp", None),
            P(),
            P(None, "head"),
            P(None, "head"),
            P(None, "head"),
            P(None, "head"),
            P(None, "head"),
            P(None, "head"),
            P(None, None, "head"),
            P("head"),
            P("head"),
            P("head"),
            P("head", None),
            P(),
            P("dp", "head"),
            P("dp", "head"),
            P("dp", "head"),
        ),
        out_specs=(
            P(None, ("dp", "head"), None),
            P(None, ("dp", "head"), None),
            P(),
            P("dp", "head"),
            P("dp", "head"),
            P("dp", "head"),
            P("dp", "head"),
            P("dp", "head"),
            P("dp", "head"),
            P(None, None, "head"),
            P("head"),
            P("head"),
            P("head"),
            P("head", "dp"),
            P(),
            P("dp", "head"),
            P("dp", "head"),
            P("dp", "head"),
        ),
        check_vma=False,
    )
```

time: 1230 us -> 935 us (0.76)
  matrix products: 312 us -> 72.1 us
  Pallas kernels: 238 us -> 337 us
  blocking collectives: 64.3 us -> 0 us
  starting transfers between devices: 139 us -> 81.7 us
  local copies, waits for them, and re-layouts: 121 us -> 82.2 us
  waiting for transfers between devices: 243 us -> 272 us
  other arithmetic: 81.2 us -> 68.2 us
    pallas_call x0 -> x9, Pallas kernels: none -> 203 us  [the longest x4 113 us: ffn_stage(): pl.pallas_call(body, grid=(steps,), in_specs=[anywhere] * (first + len(fi...]
    dot_general x5 -> x0, matrix products: 91.8 us -> none  [contract_rows(): lax.dot_general(left, right, (((0,), (0,)), ((), ())), preferred_element_...]
    dot_general x20 -> x4, matrix products: 120 us -> 32 us  [times(): return jnp.dot(left, right, preferred_element_type=F32)]
    pallas_call x4 -> x2, Pallas kernels: 128 us -> 41.7 us  [mixer_forward(): pl.pallas_call(body, grid_spec=pltpu.PrefetchScalarGridSpec(num_scalar_pr...]
    psum x2 -> x0, blocking collectives: 64.3 us -> none  [the longest x1 37.2 us: on_device(): gain_sums = lax.psum((gain_in, gain_mid), ('dp', 'head'))]
    dot_general x20 -> x4, matrix products: 100 us -> 40 us  [contract_cols(): lax.dot_general(left, right, (((1,), (1,)), ((), ())), preferred_element_...]
    ppermute x128 -> x75, starting transfers between devices: 139 us -> 81.4 us  [hop(): return lax.ppermute(values, axis, [(i, i ^ bit) for i in range(size)])]
    unnamed x637 -> x199, local copies, waits for them, and re-layouts: 79 us -> 31.7 us
  transfers between devices with their start and end apart: 136 -> 83, of which waited for: 65 -> 44; matrix products, arithmetic and copies ran while one was open for 38% -> 21% of each run, Pallas kernels for 20% -> 34%
where the time goes in v2:
time: 935 us; the launch traced here: 929 us
  Pallas kernels  337 us (36%)
  waiting for transfers between devices  272 us (29%)
  local copies, waits for them, and re-layouts  82.2 us (9%)
  starting transfers between devices  81.7 us (9%)
  matrix products  72.1 us (8%)
  other arithmetic  68.2 us (7%)
  between operations  15.9 us (2%)
    ppermute x75, waiting for transfers between devices, hop(): return lax.ppermute(values, axis, [(i, i ^ bit) for i in range(size)])  259 us
    pallas_call x4, Pallas kernels, ffn_stage(): pl.pallas_call(body, grid=(steps,), in_specs=[anywhere] * (first + len(fi...  113 us
    pallas_call x2, Pallas kernels, mixer_backward(): pl.pallas_call(body, grid_spec=pltpu.PrefetchScalarGridSpec(num_scalar_pr...  92.6 us
    pallas_call x5, Pallas kernels, weight_gradient(): pl.pallas_call(lambda *refs: wgrad_kernel(count, *refs), grid=(wide // ti...  90.4 us
    ppermute x75, starting transfers between devices, hop(): return lax.ppermute(values, axis, [(i, i ^ bit) for i in range(size)])  81.4 us
    pallas_call x2, Pallas kernels, mixer_forward(): pl.pallas_call(body, grid_spec=pltpu.PrefetchScalarGridSpec(num_scalar_pr...  41.7 us
    dot_general x4, matrix products, contract_cols(): lax.dot_general(left, right, (((1,), (1,)), ((), ())), preferred_element_...  40 us
    dot_general x4, matrix products, times(): return jnp.dot(left, right, preferred_element_type=F32)  32 us
  transfers between devices with their start and end apart: 83, of which 44 were waited for; matrix products, arithmetic and copies ran while one was open for 21% of the time, Pallas kernels for 34%

profile of v2, /device:TPU:0, one launch (start us, length us, event | category | flops | bytes accessed | tf_op | source)
XLA Modules:
  0.0 929.4 jit_solution(12214156995529290088)
XLA Ops:
  12.9 3.0 collective-permute-start.1
  18.4 2.4 constant_dynamic-update-slice_fusion.4
  21.6 3.2 convert_multiply_fusion.2
  26.0 13.4 %collective-permute-done.1 = bf16[256,2048]{1,0:T(8,128)(2,1)} collective-permute-done((bf16[256,2048]{1,0:T(8,128)(2,1)}, bf16[256,2048]{1,0:T(8,128)(2,1)}, u32[]{:S(2)}, u32[]{:S(2)}) %collective-permute-start.1) | collective-permute-done | bytes 1048608 | tf_op jit(solution)/shard_map/ppermute | solution.py:487
  53.0 13.8 %concatenate.151 = bf16[2048,2176]{1,0:T(8,128)(2,1)} concatenate(bf16[2048,512]{1,0:T(8,128)(2,1)} %param.29, bf16[2048,512]{1,0:T(8,128)(2,1)} %param.30, bf16[2048,512]{1,0:T(8,128)(2,1)} %param.31, bf16[2048,512]{1,0:T(8,128)(2,1)} %param.32, bf16[2048,4]{1,0:T(8,128)(2,1)} %copy.106, bf16[2048,4]{1,0:T(8,128)(2,1)} %copy.107, bf16[2048,120]{1,0:T(8,128)(2,1)} %broadcast_in_dim.16), dimensions={1} | concatenate | bytes 17825792 | tf_op jit(solution)/shard_map/concatenate | solution.py:844
  69.0 2.4 constant_dynamic-update-slice_fusion.2
  76.0 15.0 %fusion.40 = f32[1024,2176]{1,0:T(8,128)} fusion(bf16[1024,2048]{1,0:T(8,128)(2,1)} %constant_dynamic-update-slice_fusion.refs_0_, bf16[2048,2176]{1,0:T(8,128)(2,1)} %concatenate.151), kind=kOutput, calls=%fused_computation.168 | convolution fusion | flops 9126805504 | bytes 22020096 | tf_op jit(solution)/shard_map/dot_general | solution.py:777
  92.2 20.4 %mixer_forward.2 = (bf16[4,2,128,512]{3,2,1,0:T(8,128)(2,1)}, f32[4,2,128,512]{3,2,1,0:T(8,128)}, bf16[4,2,4,128,128]{4,3,2,1,0:T(8,128)(2,1)}, bf16[4,2,128,512...) custom-call(s32[4]{0:T(128)} %iota_xor_fusion.refs_0_, f32[4,2,128,2176]{3,2,1,0:T(8,128)} %bitcast.172, ...), custom_call_target="tpu_custom_call" | custom-call | flops 23520000000 | bytes 8000000 | tf_op jit(solution)/shard_map/mixer_forward/pallas_call | solution.py:387
  120.2 7.5 collective-permute-done.18
  129.7 12.3 %fusion.41 = f32[1024,2176]{1,0:T(8,128)} fusion(bf16[1024,2048]{1,0:T(8,128)(2,1)S(1)} %constant_dynamic-update-slice_fusion.5.refs_1_, bf16[2048,2176]{1,0:T(8,128)(2,1)S(1)} %bitcast.145), kind=kOutput, calls=%fused_computation.169 | convolution fusion | flops 9126805504 | bytes 22020096 | tf_op jit(solution)/shard_map/dot_general | solution.py:777
  142.0 5.3 collective-permute-done.6
  155.2 21.3 %mixer_forward.3 = (bf16[4,2,128,512]{3,2,1,0:T(8,128)(2,1)}, f32[4,2,128,512]{3,2,1,0:T(8,128)}, bf16[4,2,4,128,128]{4,3,2,1,0:T(8,128)(2,1)}, bf16[4,2,128,512...) custom-call(s32[4]{0:T(128)} %iota_xor_fusion.refs_0_, f32[4,2,128,2176]{3,2,1,0:T(8,128)} %bitcast.169, ...), custom_call_target="tpu_custom_call" | custom-call | flops 23520000000 | bytes 8000000 | tf_op jit(solution)/shard_map/mixer_forward/pallas_call | solution.py:387
  176.6 5.8 collective-permute-done.8
  189.6 19.9 %collective-permute-done.21 = bf16[256,2048]{1,0:T(8,128)(2,1)S(1)} collective-permute-done((bf16[256,2048]{1,0:T(8,128)(2,1)S(1)}, bf16[256,2048]{1,0:T(8,128)(2,1)S(1)}, u32[]{:S(2)}, u32[]{:S(2)}) %collective-permute-start.21) | collective-permute-done | bytes 1048608 | tf_op jit(solution)/shard_map/ppermute | solution.py:487
  212.9 9.7 %collective-permute-done.22 = bf16[128,2048]{1,0:T(8,128)(2,1)S(1)} collective-permute-done((bf16[128,2048]{1,0:T(8,128)(2,1)S(1)}, bf16[128,2048]{1,0:T(8,128)(2,1)S(1)}, u32[]{:S(2)}, u32[]{:S(2)}) %collective-permute-start.22) | collective-permute-done | bytes 524320 | tf_op jit(solution)/shard_map/ppermute | solution.py:487
  231.6 19.8 %collective-permute-done.11.refs_2_ = bf16[256,2048]{1,0:T(8,128)(2,1)S(1)} collective-permute-done((bf16[256,2048]{1,0:T(8,128)(2,1)S(1)}, bf16[256,2048]{1,0:T(8,128)(2,1)S(1)}, u32[]{:S(2)}, u32[]{:S(2)}) %collective-permute-start.11) | collective-permute-done | bytes 1048608 | tf_op jit(solution)/shard_map/ppermute | solution.py:487
  254.3 6.6 collective-permute-done.16.refs_8_
  260.9 8.7 collective-permute-done.12.refs_3_
  275.1 21.7 %collective-permute-done.25.refs_2_ = bf16[256,2048]{1,0:T(8,128)(2,1)S(1)} collective-permute-done((bf16[256,2048]{1,0:T(8,128)(2,1)S(1)}, bf16[256,2048]{1,0:T(8,128)(2,1)S(1)}, u32[]{:S(2)}, u32[]{:S(2)}) %collective-permute-start.25) | collective-permute-done | bytes 1048608 | tf_op jit(solution)/shard_map/ppermute | solution.py:487
  300.4 18.8 %collective-permute-done.37.refs_7_ = bf16[256,2048]{1,0:T(8,128)(2,1)S(1)} collective-permute-done((bf16[256,2048]{1,0:T(8,128)(2,1)S(1)}, bf16[256,2048]{1,0:T(8,128)(2,1)S(1)}, u32[]{:S(2)}, u32[]{:S(2)}) %collective-permute-start.37) | collective-permute-done | bytes 1048608 | tf_op jit(solution)/shard_map/ppermute | solution.py:487
  323.2 28.3 %ffn_stage.4 = (bf16[2,256,1408]{2,1,0:T(8,128)(2,1)}, bf16[2,256,1408]{2,1,0:T(8,128)(2,1)}, bf16[2,256,1408]{2,1,0:T(8,128)(2,1)}, bf16[2,256,2048]{2,1,0:T(8,...) custom-call(bf16[256,2048]{1,0:T(8,128)(2,1)} %copy-done.42, ...), custom_call_target="tpu_custom_call" | custom-call | flops 29527900160 | bytes 30000000 | tf_op jit(solution)/shard_map/ffn_stage/pallas_call | solution.py:701
  351.4 27.9 %ffn_stage.5 = (bf16[2,256,1408]{2,1,0:T(8,128)(2,1)}, bf16[2,256,1408]{2,1,0:T(8,128)(2,1)}, bf16[2,256,1408]{2,1,0:T(8,128)(2,1)}, bf16[2,256,2048]{2,1,0:T(8,...) custom-call(bf16[256,2048]{1,0:T(8,128)(2,1)} %copy-done.42, ...), custom_call_target="tpu_custom_call", output_to_operand_aliasing={{5}: (13, {}), {6}: (14, {}), {7}: (15, {}), {8}: (16, {}),... | custom-call | flops 29527900160 | bytes 30000000 | tf_op jit(solution)/shard_map/ffn_stage/pallas_call | solution.py:701
  381.7 28.1 %ffn_stage.6 = (bf16[2,256,1408]{2,1,0:T(8,128)(2,1)}, bf16[2,256,1408]{2,1,0:T(8,128)(2,1)}, bf16[2,256,1408]{2,1,0:T(8,128)(2,1)}, bf16[2,256,2048]{2,1,0:T(8,...) custom-call(bf16[256,2048]{1,0:T(8,128)(2,1)} %copy-done.41, ...), custom_call_target="tpu_custom_call" | custom-call | flops 29527900160 | bytes 30000000 | tf_op jit(solution)/shard_map/ffn_stage/pallas_call | solution.py:701
  412.8 28.4 %ffn_stage.7 = (bf16[2,256,1408]{2,1,0:T(8,128)(2,1)}, bf16[2,256,1408]{2,1,0:T(8,128)(2,1)}, bf16[2,256,1408]{2,1,0:T(8,128)(2,1)}, bf16[2,256,2048]{2,1,0:T(8,...) custom-call(bf16[256,2048]{1,0:T(8,128)(2,1)} %copy-done.41, ...), custom_call_target="tpu_custom_call", output_to_operand_aliasing={{5}: (13, {}), {6}: (14, {}), {7}: (15, {}), {8}: (16, {}),... | custom-call | flops 29527900160 | bytes 30000000 | tf_op jit(solution)/shard_map/ffn_stage/pallas_call | solution.py:701
  442.4 2.9 multiply_reduce_fusion.1
  447.6 14.2 %collective-permute-done.41 = bf16[256,2048]{1,0:T(8,128)(2,1)S(1)} collective-permute-done((bf16[256,2048]{1,0:T(8,128)(2,1)S(1)}, bf16[256,2048]{1,0:T(8,128)(2,1)S(1)}, u32[]{:S(2)}, u32[]{:S(2)}) %collective-permute-start.41) | collective-permute-done | bytes 1048608 | tf_op jit(solution)/shard_map/ppermute | solution.py:487
  465.5 6.2 collective-permute-done.42
  474.8 4.1 fusion.1
  480.8 18.5 %weight_gradient.5 = bf16[2048,1408]{1,0:T(8,128)(2,1)} custom-call(bf16[512,2048]{1,0:T(8,128)(2,1)} %bitcast.182, bf16[512,2048]{1,0:T(8,128)(2,1)} %bitcast.184, bf16[512,2048]{1,0:T(8,128)(2,1)} %bitcast.187, bf16[512,2048]{1,0:T(8,128)(2,1)} %bitcast.189, bf16[512,1408]{1,0:T(8,128)(2,1)} %bitcast.200, bf16[512,1408]{1,0:T(8,128)(2,1)} %bitcast.201, ...), custom_call_target="tpu_custom_call" | custom-call | flops 17716740096 | bytes 20000000 | tf_op jit(solution)/shard_map/weight_gradient/pallas_call | solution.py:746
  499.4 2.8 constant_dynamic-update-slice_fusion.19
  506.3 22.0 %collective-permute-done.45 = bf16[256,2048]{1,0:T(8,128)(2,1)S(1)} collective-permute-done((bf16[256,2048]{1,0:T(8,128)(2,1)S(1)}, bf16[256,2048]{1,0:T(8,128)(2,1)S(1)}, u32[]{:S(2)}, u32[]{:S(2)}) %collective-permute-start.45) | collective-permute-done | bytes 1048608 | tf_op jit(solution)/shard_map/ppermute | solution.py:487
  531.9 8.1 collective-permute-done.31
  546.0 18.6 %weight_gradient.6 = bf16[2048,1408]{1,0:T(8,128)(2,1)} custom-call(bf16[512,2048]{1,0:T(8,128)(2,1)} %bitcast.183, bf16[512,2048]{1,0:T(8,128)(2,1)} %bitcast.185, bf16[512,2048]{1,0:T(8,128)(2,1)} %bitcast.188, bf16[512,2048]{1,0:T(8,128)(2,1)} %bitcast.190, bf16[512,1408]{1,0:T(8,128)(2,1)} %bitcast.196, bf16[512,1408]{1,0:T(8,128)(2,1)} %bitcast.197, ...), custom_call_target="tpu_custom_call" | custom-call | flops 17716740096 | bytes 20000000 | tf_op jit(solution)/shard_map/weight_gradient/pallas_call | solution.py:746
  564.7 2.4 constant_dynamic-update-slice_fusion.18
  574.3 5.9 fusion.42
  580.2 46.3 %mixer_backward.2 = (bf16[4,2,128,2176]{3,2,1,0:T(8,128)(2,1)}, f32[16,512]{1,0:T(8,128)}, f32[8,128]{1,0:T(8,128)}, f32[8,512]{1,0:T(8,128)}) custom-call(s32[4]{0:T(128)} %iota_xor_fusion.refs_0_, f32[4,2,128,2176]{3,2,1,0:T(8,128)} %bitcast.173, f32[4,2,128,2176]{3,2,1,0:T(8,128)} %bitcast.174, f32[2,4,128,16]{3,2,1,0:T(8,128)} %bitcast.153, ...), custom_call_target="tpu_custom_call" | custom-call | flops 52800000000 | bytes 12000000 | tf_op jit(solution)/shard_map/mixer_backward/pallas_call | solution.py:440
  626.5 18.7 %weight_gradient.7 = bf16[2048,1408]{1,0:T(8,128)(2,1)} custom-call(bf16[512,2048]{1,0:T(8,128)(2,1)} %bitcast.179, bf16[512,2048]{1,0:T(8,128)(2,1)} %bitcast.180, bf16[512,2048]{1,0:T(8,128)(2,1)} %bitcast.181, bf16[512,2048]{1,0:T(8,128)(2,1)} %bitcast.186, bf16[512,1408]{1,0:T(8,128)(2,1)} %bitcast.193, bf16[512,1408]{1,0:T(8,128)(2,1)} %bitcast.194, ...), custom_call_target="tpu_custom_call" | custom-call | flops 17716740096 | bytes 20000000 | tf_op jit(solution)/shard_map/weight_gradient/pallas_call | solution.py:746
  645.2 14.2 %convolution_convert_fusion.1 = bf16[1024,2048]{1,0:T(8,128)(2,1)S(1)} fusion(bf16[1024,2176]{1,0:T(8,128)(2,1)} %bitcast.175, bf16[2048,2176]{1,0:T(8,128)(2,1)} %concatenate.151), kind=kOutput, calls=%fused_computation.1 | convolution fusion | flops 9128902656 | bytes 17563648 | tf_op jit(solution)/shard_map/dot_general | solution.py:773
  667.2 8.7 weight_gradient.8
  680.1 11.0 %collective-permute-done.48 = bf16[256,2048]{1,0:T(8,128)(2,1)S(1)} collective-permute-done((bf16[256,2048]{1,0:T(8,128)(2,1)}, bf16[256,2048]{1,0:T(8,128)(2,1)S(1)}, u32[]{:S(2)}, u32[]{:S(2)}) %collective-permute-start.48) | collective-permute-done | bytes 1048608 | tf_op jit(solution)/shard_map/ppermute | solution.py:487
  692.1 2.8 add_convert_fusion.9
  696.7 5.6 collective-permute-done.52
  710.7 3.7 collective-permute-done.54
  715.1 3.1 convert_add_fusion.1
  718.2 2.4 convert_element_type.429
  720.6 5.9 fusion.43
  726.5 46.2 %mixer_backward.3 = (bf16[4,2,128,2176]{3,2,1,0:T(8,128)(2,1)}, f32[16,512]{1,0:T(8,128)}, f32[8,128]{1,0:T(8,128)}, f32[8,512]{1,0:T(8,128)}) custom-call(s32[4]{0:T(128)} %iota_xor_fusion.refs_0_, f32[4,2,128,2176]{3,2,1,0:T(8,128)} %bitcast.170, f32[4,2,128,2176]{3,2,1,0:T(8,128)} %bitcast.171, f32[2,4,128,16]{3,2,1,0:T(8,128)} %bitcast.151, ...), custom_call_target="tpu_custom_call" | custom-call | flops 52800000000 | bytes 12000000 | tf_op jit(solution)/shard_map/mixer_backward/pallas_call | solution.py:440
  775.1 14.0 %convolution_convert_fusion = bf16[1024,2048]{1,0:T(8,128)(2,1)S(1)} fusion(bf16[1024,2176]{1,0:T(8,128)(2,1)} %bitcast.177, bf16[2048,2176]{1,0:T(8,128)(2,1)} %concatenate.151), kind=kOutput, calls=%fused_computation | convolution fusion | flops 9128902656 | bytes 17563648 | tf_op jit(solution)/shard_map/dot_general | solution.py:773
  793.3 25.9 %weight_gradient.9 = bf16[2048,2176]{1,0:T(8,128)(2,1)} custom-call(bf16[1024,2048]{1,0:T(8,128)(2,1)} %constant_dynamic-update-slice_fusion.refs_0_, bf16[1024,2048]{1,0:T(8,128)(2,1)} %copy-done.44, bf16[1024,2176]{1,0:T(8,128)(2,1)} %bitcast.176, bf16[1024,2176]{1,0:T(8,128)(2,1)} %bitcast.178), custom_call_target="tpu_custom_call" | custom-call | flops 27380416512 | bytes 20000000 | tf_op jit(solution)/shard_map/weight_gradient/pallas_call | solution.py:746
  821.9 12.5 %collective-permute-done.56 = bf16[256,2048]{1,0:T(8,128)(2,1)S(1)} collective-permute-done((bf16[256,2048]{1,0:T(8,128)(2,1)}, bf16[256,2048]{1,0:T(8,128)(2,1)S(1)}, u32[]{:S(2)}, u32[]{:S(2)}) %collective-permute-start.56) | collective-permute-done | bytes 1048608 | tf_op jit(solution)/shard_map/ppermute | solution.py:487
  841.4 5.0 collective-permute-done.58
  849.9 2.6 collective-permute-start.73
  852.5 6.6 collective-permute-done.60
  859.2 3.3 add_convert_fusion.3
  865.5 2.5 collective-permute-start.74
  868.1 3.0 collective-permute-start.70
  877.5 3.4 fusion.15
  882.7 2.5 convert_element_type.441
  885.2 2.3 collective-permute-start.65
  887.6 2.5 collective-permute-done.65
  891.3 4.3 collective-permute-done.66
  897.2 4.7 fusion.3
  906.4 10.9 %reduce-scatter.10.cloned.1.call-done = bf16[256,2176]{1,0:T(8,128)(2,1)} async-done(((bf16[2048,2176]{1,0:T(8,128)(2,1)}), bf16[256,2176]{1,0:T(8,128)(2,1)}) %reduce-scatter.10.cloned.1.call-update) | async-done | bytes 1114128 | tf_op jit(solution)/shard_map/reduce_scatter | solution.py:911
  919.7 2.6 fusion.34
  (491 shorter events, 186.5 us)
Async XLA Ops:
  7.2 315.9 %all-gather.4.cloned.1.call-start = ((), (), s32[]{:S(2)}) async-start(), calls=%async_computation.5 | async-start | bytes 6488064 | tf_op jit(solution)/shard_map/all_gather | solution.py:827
  8.0 315.2 %all-gather.6.cloned.1.call-start = ((), (), s32[]{:S(2)}) async-start(), calls=%async_computation.6 | async-start | bytes 6488064 | tf_op jit(solution)/shard_map/all_gather | solution.py:828
  8.7 314.5 %all-gather.8.cloned.1.call-start = ((), (), s32[]{:S(2)}) async-start(), calls=%async_computation.7 | async-start | bytes 6488064 | tf_op jit(solution)/shard_map/all_gather | solution.py:829
  12.9 26.5 %collective-permute-start.1 = (bf16[256,2048]{1,0:T(8,128)(2,1)}, bf16[256,2048]{1,0:T(8,128)(2,1)}, u32[]{:S(2)}, u32[]{:S(2)}) collective-permute-start(bf16[256,2048]{1,0:T(8,128)(2,1)} %get-tuple-element.372), channel_id=1, source_target_pairs={{0,2},{1,3},{2,0},{3,1},{4,6},{5,7},{6,4},{7,5},{8,10},{9,11},{10,... | collective-permute-start | bytes 3145736 | tf_op jit(solution)/shard_map/ppermute | solution.py:487
  16.0 27.1 %collective-permute-start = (bf16[256,2048]{1,0:T(8,128)(2,1)}, bf16[256,2048]{1,0:T(8,128)(2,1)}, u32[]{:S(2)}, u32[]{:S(2)}) collective-permute-start(bf16[256,2048]{1,0:T(8,128)(2,1)} %get-tuple-element.372), channel_id=1, source_target_pairs={{0,1},{1,0},{2,3},{3,2},{4,5},{5,4},{6,7},{7,6},{8,9},{9,8},{10,11... | collective-permute-start | bytes 3145736 | tf_op jit(solution)/shard_map/ppermute | solution.py:487
  17.5 700.7 %reduce-scatter.6.cloned.1.call-start = ((), (), s32[]{:S(2)}) async-start(), calls=%async_computation.8 | async-start | bytes 6488064 | tf_op jit(solution)/shard_map/reduce_scatter | solution.py:911
  41.3 30.1 %collective-permute-start.2 = (bf16[128,2048]{1,0:T(8,128)(2,1)}, bf16[128,2048]{1,0:T(8,128)(2,1)}, u32[]{:S(2)}, u32[]{:S(2)}) collective-permute-start(bf16[128,2048]{1,0:T(8,128)(2,1)} %slice.589), channel_id=1, source_target_pairs={{0,1},{1,0},{2,3},{3,2},{4,5},{5,4},{6,7},{7,6},{8,9},{9,8},{10,11... | collective-permute-start | bytes 1572872 | tf_op jit(solution)/shard_map/ppermute | solution.py:487
  44.9 26.5 %collective-permute-start.3 = (bf16[128,2048]{1,0:T(8,128)(2,1)}, bf16[128,2048]{1,0:T(8,128)(2,1)}, u32[]{:S(2)}, u32[]{:S(2)}) collective-permute-start(bf16[128,2048]{1,0:T(8,128)(2,1)} %slice.590), channel_id=1, source_target_pairs={{0,2},{1,3},{2,0},{3,1},{4,6},{5,7},{6,4},{7,5},{8,10},{9,11},{10,... | collective-permute-start | bytes 1572872 | tf_op jit(solution)/shard_map/ppermute | solution.py:487
  71.4 41.4 %collective-permute-start.5 = (bf16[256,2048]{1,0:T(8,128)(2,1)S(1)}, bf16[256,2048]{1,0:T(8,128)(2,1)S(1)}, u32[]{:S(2)}, u32[]{:S(2)}) collective-permute-start(bf16[256,2048]{1,0:T(8,128)(2,1)S(1)} %get-tuple-element.136), channel_id=1, source_target_pairs={{0,2},{1,3},{2,0},{3,1},{4,6},{5,7},{6,4},{7,5},{8,10},{9,11},{10,... | collective-permute-start | bytes 3145736 | tf_op jit(solution)/shard_map/ppermute | solution.py:487
  71.9 42.7 %collective-permute-start.4 = (bf16[256,2048]{1,0:T(8,128)(2,1)S(1)}, bf16[256,2048]{1,0:T(8,128)(2,1)S(1)}, u32[]{:S(2)}, u32[]{:S(2)}) collective-permute-start(bf16[256,2048]{1,0:T(8,128)(2,1)S(1)} %get-tuple-element.136), channel_id=1, source_target_pairs={{0,1},{1,0},{2,3},{3,2},{4,5},{5,4},{6,7},{7,6},{8,9},{9,8},{10,11... | collective-permute-start | bytes 3145736 | tf_op jit(solution)/shard_map/ppermute | solution.py:487
  112.8 14.9 %collective-permute-start.18 = (bf16[128,2048]{1,0:T(8,128)(2,1)S(1)}, bf16[128,2048]{1,0:T(8,128)(2,1)S(1)}, u32[]{:S(2)}, u32[]{:S(2)}) collective-permute-start(bf16[128,2048]{1,0:T(8,128)(2,1)S(1)} %slice.610), channel_id=1, source_target_pairs={{0,1},{1,0},{2,3},{3,2},{4,5},{5,4},{6,7},{7,6},{8,9},{9,8},{10,11... | collective-permute-start | bytes 1572872 | tf_op jit(solution)/shard_map/ppermute | solution.py:487
  114.7 14.9 %collective-permute-start.19 = (bf16[128,2048]{1,0:T(8,128)(2,1)S(1)}, bf16[128,2048]{1,0:T(8,128)(2,1)S(1)}, u32[]{:S(2)}, u32[]{:S(2)}) collective-permute-start(bf16[128,2048]{1,0:T(8,128)(2,1)S(1)} %slice.611), channel_id=1, source_target_pairs={{0,2},{1,3},{2,0},{3,1},{4,6},{5,7},{6,4},{7,5},{8,10},{9,11},{10,... | collective-permute-start | bytes 1572872 | tf_op jit(solution)/shard_map/ppermute | solution.py:487
  118.9 28.5 %collective-permute-start.6 = (bf16[256,2048]{1,0:T(8,128)(2,1)S(1)}, bf16[256,2048]{1,0:T(8,128)(2,1)S(1)}, u32[]{:S(2)}, u32[]{:S(2)}) collective-permute-start(bf16[256,2048]{1,0:T(8,128)(2,1)S(1)} %pad_maximum_fusion.5), channel_id=1, source_target_pairs={{0,1},{1,0},{2,3},{3,2},{4,5},{5,4},{6,7},{7,6},{8,9},{9,8},{10,11... | collective-permute-start | bytes 3145736 | tf_op jit(solution)/shard_map/ppermute | solution.py:487
  119.6 29.7 %collective-permute-start.7 = (bf16[256,2048]{1,0:T(8,128)(2,1)S(1)}, bf16[256,2048]{1,0:T(8,128)(2,1)S(1)}, u32[]{:S(2)}, u32[]{:S(2)}) collective-permute-start(bf16[256,2048]{1,0:T(8,128)(2,1)S(1)} %pad_maximum_fusion.6), channel_id=1, source_target_pairs={{0,2},{1,3},{2,0},{3,1},{4,6},{5,7},{6,4},{7,5},{8,10},{9,11},{10,... | collective-permute-start | bytes 3145736 | tf_op jit(solution)/shard_map/ppermute | solution.py:487
  149.3 36.0 %collective-permute-start.15 = (bf16[256,2048]{1,0:T(8,128)(2,1)S(1)}, bf16[256,2048]{1,0:T(8,128)(2,1)}, u32[]{:S(2)}, u32[]{:S(2)}) collective-permute-start(bf16[256,2048]{1,0:T(8,128)(2,1)S(1)} %copy-done.31), channel_id=1, source_target_pairs={{0,2},{1,3},{2,0},{3,1},{4,6},{5,7},{6,4},{7,5},{8,10},{9,11},{10,... | collective-permute-start | bytes 3145736 | tf_op jit(solution)/shard_map/ppermute | solution.py:487
  150.7 34.6 %collective-permute-start.14 = (bf16[256,2048]{1,0:T(8,128)(2,1)S(1)}, bf16[256,2048]{1,0:T(8,128)(2,1)}, u32[]{:S(2)}, u32[]{:S(2)}) collective-permute-start(bf16[256,2048]{1,0:T(8,128)(2,1)S(1)} %copy-done.31), channel_id=1, source_target_pairs={{0,1},{1,0},{2,3},{3,2},{4,5},{5,4},{6,7},{7,6},{8,9},{9,8},{10,11... | collective-permute-start | bytes 3145736 | tf_op jit(solution)/shard_map/ppermute | solution.py:487
  152.5 29.8 %collective-permute-start.8 = (bf16[128,2048]{1,0:T(8,128)(2,1)}, bf16[128,2048]{1,0:T(8,128)(2,1)}, u32[]{:S(2)}, u32[]{:S(2)}) collective-permute-start(bf16[128,2048]{1,0:T(8,128)(2,1)} %get-tuple-element.362), channel_id=1, source_target_pairs={{0,2},{1,3},{2,0},{3,1},{4,6},{5,7},{6,4},{7,5},{8,10},{9,11},{10,... | collective-permute-start | bytes 1572872 | tf_op jit(solution)/shard_map/ppermute | solution.py:487
  152.8 30.2 %collective-permute-start.9 = (bf16[128,2048]{1,0:T(8,128)(2,1)S(1)}, bf16[128,2048]{1,0:T(8,128)(2,1)}, u32[]{:S(2)}, u32[]{:S(2)}) collective-permute-start(bf16[128,2048]{1,0:T(8,128)(2,1)S(1)} %get-tuple-element.363), channel_id=1, source_target_pairs={{0,1},{1,0},{2,3},{3,2},{4,5},{5,4},{6,7},{7,6},{8,9},{9,8},{10,11... | collective-permute-start | bytes 1572872 | tf_op jit(solution)/shard_map/ppermute | solution.py:487
  188.1 21.4 %collective-permute-start.21 = (bf16[256,2048]{1,0:T(8,128)(2,1)S(1)}, bf16[256,2048]{1,0:T(8,128)(2,1)S(1)}, u32[]{:S(2)}, u32[]{:S(2)}) collective-permute-start(bf16[256,2048]{1,0:T(8,128)(2,1)S(1)} %pad_maximum_fusion.8), channel_id=1, source_target_pairs={{0,2},{1,3},{2,0},{3,1},{4,6},{5,7},{6,4},{7,5},{8,10},{9,11},{10,... | collective-permute-start | bytes 3145736 | tf_op jit(solution)/shard_map/ppermute | solution.py:487
  189.1 22.6 %collective-permute-start.20 = (bf16[256,2048]{1,0:T(8,128)(2,1)S(1)}, bf16[256,2048]{1,0:T(8,128)(2,1)S(1)}, u32[]{:S(2)}, u32[]{:S(2)}) collective-permute-start(bf16[256,2048]{1,0:T(8,128)(2,1)S(1)} %pad_maximum_fusion.7), channel_id=1, source_target_pairs={{0,1},{1,0},{2,3},{3,2},{4,5},{5,4},{6,7},{7,6},{8,9},{9,8},{10,11... | collective-permute-start | bytes 3145736 | tf_op jit(solution)/shard_map/ppermute | solution.py:487
  225.2 26.1 %collective-permute-start.11 = (bf16[256,2048]{1,0:T(8,128)(2,1)S(1)}, bf16[256,2048]{1,0:T(8,128)(2,1)S(1)}, u32[]{:S(2)}, u32[]{:S(2)}) collective-permute-start(bf16[256,2048]{1,0:T(8,128)(2,1)S(1)} %get-tuple-element.396.refs_0_), channel_id=1, source_target_pairs={{0,2},{1,3},{2,0},{3,1},{4,6},{5,7},{6,4},{7,5},{8,10},{9,11},{10,... | collective-permute-start | bytes 3145736 | tf_op jit(solution)/shard_map/ppermute | solution.py:487
  227.1 26.1 %collective-permute-start.10 = (bf16[256,2048]{1,0:T(8,128)(2,1)S(1)}, bf16[256,2048]{1,0:T(8,128)(2,1)S(1)}, u32[]{:S(2)}, u32[]{:S(2)}) collective-permute-start(bf16[256,2048]{1,0:T(8,128)(2,1)S(1)} %get-tuple-element.396.refs_0_), channel_id=1, source_target_pairs={{0,1},{1,0},{2,3},{3,2},{4,5},{5,4},{6,7},{7,6},{8,9},{9,8},{10,11... | collective-permute-start | bytes 3145736 | tf_op jit(solution)/shard_map/ppermute | solution.py:487
  228.5 32.4 %collective-permute-start.16 = (bf16[128,2048]{1,0:T(8,128)(2,1)S(1)}, bf16[128,2048]{1,0:T(8,128)(2,1)S(1)}, u32[]{:S(2)}, u32[]{:S(2)}) collective-permute-start(bf16[128,2048]{1,0:T(8,128)(2,1)S(1)} %slice.608), channel_id=1, source_target_pairs={{0,1},{1,0},{2,3},{3,2},{4,5},{5,4},{6,7},{7,6},{8,9},{9,8},{10,11... | collective-permute-start | bytes 1572872 | tf_op jit(solution)/shard_map/ppermute | solution.py:487
  231.3 29.6 %collective-permute-start.17 = (bf16[128,2048]{1,0:T(8,128)(2,1)S(1)}, bf16[128,2048]{1,0:T(8,128)(2,1)S(1)}, u32[]{:S(2)}, u32[]{:S(2)}) collective-permute-start(bf16[128,2048]{1,0:T(8,128)(2,1)S(1)} %slice.609), channel_id=1, source_target_pairs={{0,2},{1,3},{2,0},{3,1},{4,6},{5,7},{6,4},{7,5},{8,10},{9,11},{10,... | collective-permute-start | bytes 1572872 | tf_op jit(solution)/shard_map/ppermute | solution.py:487
  251.4 18.2 %collective-permute-start.12 = (bf16[128,2048]{1,0:T(8,128)(2,1)S(1)}, bf16[128,2048]{1,0:T(8,128)(2,1)S(1)}, u32[]{:S(2)}, u32[]{:S(2)}) collective-permute-start(bf16[128,2048]{1,0:T(8,128)(2,1)S(1)} %slice.606), channel_id=1, source_target_pairs={{0,1},{1,0},{2,3},{3,2},{4,5},{5,4},{6,7},{7,6},{8,9},{9,8},{10,11... | collective-permute-start | bytes 1572872 | tf_op jit(solution)/shard_map/ppermute | solution.py:487
  253.2 17.4 %collective-permute-start.13 = (bf16[128,2048]{1,0:T(8,128)(2,1)S(1)}, bf16[128,2048]{1,0:T(8,128)(2,1)S(1)}, u32[]{:S(2)}, u32[]{:S(2)}) collective-permute-start(bf16[128,2048]{1,0:T(8,128)(2,1)S(1)} %slice.607), channel_id=1, source_target_pairs={{0,2},{1,3},{2,0},{3,1},{4,6},{5,7},{6,4},{7,5},{8,10},{9,11},{10,... | collective-permute-start | bytes 1572872 | tf_op jit(solution)/shard_map/ppermute | solution.py:487
  270.7 26.1 %collective-permute-start.25 = (bf16[256,2048]{1,0:T(8,128)(2,1)S(1)}, bf16[256,2048]{1,0:T(8,128)(2,1)S(1)}, u32[]{:S(2)}, u32[]{:S(2)}) collective-permute-start(bf16[256,2048]{1,0:T(8,128)(2,1)S(1)} %get-tuple-element.160.refs_0_), channel_id=1, source_target_pairs={{0,2},{1,3},{2,0},{3,1},{4,6},{5,7},{6,4},{7,5},{8,10},{9,11},{10,... | collective-permute-start | bytes 3145736 | tf_op jit(solution)/shard_map/ppermute | solution.py:487
  272.5 26.2 %collective-permute-start.24 = (bf16[256,2048]{1,0:T(8,128)(2,1)S(1)}, bf16[256,2048]{1,0:T(8,128)(2,1)S(1)}, u32[]{:S(2)}, u32[]{:S(2)}) collective-permute-start(bf16[256,2048]{1,0:T(8,128)(2,1)S(1)} %get-tuple-element.160.refs_0_), channel_id=1, source_target_pairs={{0,1},{1,0},{2,3},{3,2},{4,5},{5,4},{6,7},{7,6},{8,9},{9,8},{10,11... | collective-permute-start | bytes 3145736 | tf_op jit(solution)/shard_map/ppermute | solution.py:487
  272.8 46.5 %collective-permute-start.37 = (bf16[256,2048]{1,0:T(8,128)(2,1)S(1)}, bf16[256,2048]{1,0:T(8,128)(2,1)S(1)}, u32[]{:S(2)}, u32[]{:S(2)}) collective-permute-start(bf16[256,2048]{1,0:T(8,128)(2,1)S(1)} %bitcast_convert_fusion.refs_5_), channel_id=1, source_target_pairs={{0,2},{1,3},{2,0},{3,1},{4,6},{5,7},{6,4},{7,5},{8,10},{9,11},{10,... | collective-permute-start | bytes 3145736 | tf_op jit(solution)/shard_map/ppermute | solution.py:487
  273.3 47.8 %collective-permute-start.36 = (bf16[256,2048]{1,0:T(8,128)(2,1)S(1)}, bf16[256,2048]{1,0:T(8,128)(2,1)S(1)}, u32[]{:S(2)}, u32[]{:S(2)}) collective-permute-start(bf16[256,2048]{1,0:T(8,128)(2,1)S(1)} %bitcast_convert_fusion.refs_5_), channel_id=1, source_target_pairs={{0,1},{1,0},{2,3},{3,2},{4,5},{5,4},{6,7},{7,6},{8,9},{9,8},{10,11... | collective-permute-start | bytes 3145736 | tf_op jit(solution)/shard_map/ppermute | solution.py:487
  297.7 83.5 %collective-permute-start.34 = (bf16[128,2048]{1,0:T(8,128)(2,1)}, bf16[128,2048]{1,0:T(8,128)(2,1)}, u32[]{:S(2)}, u32[]{:S(2)}) collective-permute-start(bf16[128,2048]{1,0:T(8,128)(2,1)} %slice.631), channel_id=1, source_target_pairs={{0,1},{1,0},{2,3},{3,2},{4,5},{5,4},{6,7},{7,6},{8,9},{9,8},{10,11... | collective-permute-start | bytes 1572872 | tf_op jit(solution)/shard_map/ppermute | solution.py:487
  299.5 82.2 %collective-permute-start.35 = (bf16[128,2048]{1,0:T(8,128)(2,1)}, bf16[128,2048]{1,0:T(8,128)(2,1)}, u32[]{:S(2)}, u32[]{:S(2)}) collective-permute-start(bf16[128,2048]{1,0:T(8,128)(2,1)} %slice.632), channel_id=1, source_target_pairs={{0,2},{1,3},{2,0},{3,1},{4,6},{5,7},{6,4},{7,5},{8,10},{9,11},{10,... | collective-permute-start | bytes 1572872 | tf_op jit(solution)/shard_map/ppermute | solution.py:487
  320.2 61.5 %collective-permute-start.38 = (bf16[128,2048]{1,0:T(8,128)(2,1)}, bf16[128,2048]{1,0:T(8,128)(2,1)}, u32[]{:S(2)}, u32[]{:S(2)}) collective-permute-start(bf16[128,2048]{1,0:T(8,128)(2,1)} %slice.633), channel_id=1, source_target_pairs={{0,1},{1,0},{2,3},{3,2},{4,5},{5,4},{6,7},{7,6},{8,9},{9,8},{10,11... | collective-permute-start | bytes 1572872 | tf_op jit(solution)/shard_map/ppermute | solution.py:487
  322.2 59.4 %collective-permute-start.39 = (bf16[128,2048]{1,0:T(8,128)(2,1)}, bf16[128,2048]{1,0:T(8,128)(2,1)}, u32[]{:S(2)}, u32[]{:S(2)}) collective-permute-start(bf16[128,2048]{1,0:T(8,128)(2,1)} %slice.634), channel_id=1, source_target_pairs={{0,2},{1,3},{2,0},{3,1},{4,6},{5,7},{6,4},{7,5},{8,10},{9,11},{10,... | collective-permute-start | bytes 1572872 | tf_op jit(solution)/shard_map/ppermute | solution.py:487
  379.4 30.4 %collective-permute-start.26 = (bf16[256,2048]{1,0:T(8,128)(2,1)}, bf16[256,2048]{1,0:T(8,128)(2,1)S(1)}, u32[]{:S(2)}, u32[]{:S(2)}) collective-permute-start(bf16[256,2048]{1,0:T(8,128)(2,1)} %get-tuple-element.156), channel_id=1, source_target_pairs={{0,1},{1,0},{2,3},{3,2},{4,5},{5,4},{6,7},{7,6},{8,9},{9,8},{10,11... | collective-permute-start | bytes 3145736 | tf_op jit(solution)/shard_map/ppermute | solution.py:487
  381.2 28.5 %collective-permute-start.27 = (bf16[256,2048]{1,0:T(8,128)(2,1)}, bf16[256,2048]{1,0:T(8,128)(2,1)S(1)}, u32[]{:S(2)}, u32[]{:S(2)}) collective-permute-start(bf16[256,2048]{1,0:T(8,128)(2,1)} %get-tuple-element.157), channel_id=1, source_target_pairs={{0,2},{1,3},{2,0},{3,1},{4,6},{5,7},{6,4},{7,5},{8,10},{9,11},{10,... | collective-permute-start | bytes 3145736 | tf_op jit(solution)/shard_map/ppermute | solution.py:487
  411.0 31.4 %collective-permute-start.28 = (bf16[128,2048]{1,0:T(8,128)(2,1)}, bf16[128,2048]{1,0:T(8,128)(2,1)}, u32[]{:S(2)}, u32[]{:S(2)}) collective-permute-start(bf16[128,2048]{1,0:T(8,128)(2,1)} %get-tuple-element.380), channel_id=1, source_target_pairs={{0,2},{1,3},{2,0},{3,1},{4,6},{5,7},{6,4},{7,5},{8,10},{9,11},{10,... | collective-permute-start | bytes 1572872 | tf_op jit(solution)/shard_map/ppermute | solution.py:487
  412.6 29.8 %collective-permute-start.29 = (bf16[128,2048]{1,0:T(8,128)(2,1)S(1)}, bf16[128,2048]{1,0:T(8,128)(2,1)}, u32[]{:S(2)}, u32[]{:S(2)}) collective-permute-start(bf16[128,2048]{1,0:T(8,128)(2,1)S(1)} %get-tuple-element.381), channel_id=1, source_target_pairs={{0,1},{1,0},{2,3},{3,2},{4,5},{5,4},{6,7},{7,6},{8,9},{9,8},{10,11... | collective-permute-start | bytes 1572872 | tf_op jit(solution)/shard_map/ppermute | solution.py:487
  445.4 16.4 %collective-permute-start.41 = (bf16[256,2048]{1,0:T(8,128)(2,1)S(1)}, bf16[256,2048]{1,0:T(8,128)(2,1)S(1)}, u32[]{:S(2)}, u32[]{:S(2)}) collective-permute-start(bf16[256,2048]{1,0:T(8,128)(2,1)S(1)} %copy-done.79), channel_id=1, source_target_pairs={{0,2},{1,3},{2,0},{3,1},{4,6},{5,7},{6,4},{7,5},{8,10},{9,11},{10,... | collective-permute-start | bytes 3145736 | tf_op jit(solution)/shard_map/ppermute | solution.py:487
  446.5 15.6 %collective-permute-start.40 = (bf16[256,2048]{1,0:T(8,128)(2,1)S(1)}, bf16[256,2048]{1,0:T(8,128)(2,1)S(1)}, u32[]{:S(2)}, u32[]{:S(2)}) collective-permute-start(bf16[256,2048]{1,0:T(8,128)(2,1)S(1)} %copy-done.78), channel_id=1, source_target_pairs={{0,1},{1,0},{2,3},{3,2},{4,5},{5,4},{6,7},{7,6},{8,9},{9,8},{10,11... | collective-permute-start | bytes 3145736 | tf_op jit(solution)/shard_map/ppermute | solution.py:487
  499.3 273.4 %reduce-scatter.8.cloned.1.call-start = ((), (), s32[]{:S(2)}) async-start(), calls=%async_computation.9 | async-start | bytes 6488064 | tf_op jit(solution)/shard_map/reduce_scatter | solution.py:911
  502.2 26.1 %collective-permute-start.45 = (bf16[256,2048]{1,0:T(8,128)(2,1)S(1)}, bf16[256,2048]{1,0:T(8,128)(2,1)S(1)}, u32[]{:S(2)}, u32[]{:S(2)}) collective-permute-start(bf16[256,2048]{1,0:T(8,128)(2,1)S(1)} %get-tuple-element.329), channel_id=1, source_target_pairs={{0,2},{1,3},{2,0},{3,1},{4,6},{5,7},{6,4},{7,5},{8,10},{9,11},{10,... | collective-permute-start | bytes 3145736 | tf_op jit(solution)/shard_map/ppermute | solution.py:487
  502.8 27.7 %collective-permute-start.44 = (bf16[256,2048]{1,0:T(8,128)(2,1)S(1)}, bf16[256,2048]{1,0:T(8,128)(2,1)S(1)}, u32[]{:S(2)}, u32[]{:S(2)}) collective-permute-start(bf16[256,2048]{1,0:T(8,128)(2,1)S(1)} %get-tuple-element.329), channel_id=1, source_target_pairs={{0,1},{1,0},{2,3},{3,2},{4,5},{5,4},{6,7},{7,6},{8,9},{9,8},{10,11... | collective-permute-start | bytes 3145736 | tf_op jit(solution)/shard_map/ppermute | solution.py:487
  504.1 35.9 %collective-permute-start.31 = (bf16[256,2048]{1,0:T(8,128)(2,1)S(1)}, bf16[256,2048]{1,0:T(8,128)(2,1)S(1)}, u32[]{:S(2)}, u32[]{:S(2)}) collective-permute-start(bf16[256,2048]{1,0:T(8,128)(2,1)S(1)} %copy-done.43), channel_id=1, source_target_pairs={{0,2},{1,3},{2,0},{3,1},{4,6},{5,7},{6,4},{7,5},{8,10},{9,11},{10,... | collective-permute-start | bytes 3145736 | tf_op jit(solution)/shard_map/ppermute | solution.py:487
  505.7 37.1 %collective-permute-start.30 = (bf16[256,2048]{1,0:T(8,128)(2,1)S(1)}, bf16[256,2048]{1,0:T(8,128)(2,1)S(1)}, u32[]{:S(2)}, u32[]{:S(2)}) collective-permute-start(bf16[256,2048]{1,0:T(8,128)(2,1)S(1)} %copy-done.43), channel_id=1, source_target_pairs={{0,1},{1,0},{2,3},{3,2},{4,5},{5,4},{6,7},{7,6},{8,9},{9,8},{10,11... | collective-permute-start | bytes 3145736 | tf_op jit(solution)/shard_map/ppermute | solution.py:487
  529.2 116.0 %collective-permute-start.46 = (bf16[128,2048]{1,0:T(8,128)(2,1)}, bf16[128,2048]{1,0:T(8,128)(2,1)}, u32[]{:S(2)}, u32[]{:S(2)}) collective-permute-start(bf16[128,2048]{1,0:T(8,128)(2,1)} %slice.639), channel_id=1, source_target_pairs={{0,1},{1,0},{2,3},{3,2},{4,5},{5,4},{6,7},{7,6},{8,9},{9,8},{10,11... | collective-permute-start | bytes 1572872 | tf_op jit(solution)/shard_map/ppermute | solution.py:487
  531.4 113.8 %collective-permute-start.47 = (bf16[128,2048]{1,0:T(8,128)(2,1)}, bf16[128,2048]{1,0:T(8,128)(2,1)}, u32[]{:S(2)}, u32[]{:S(2)}) collective-permute-start(bf16[128,2048]{1,0:T(8,128)(2,1)} %slice.640), channel_id=1, source_target_pairs={{0,2},{1,3},{2,0},{3,1},{4,6},{5,7},{6,4},{7,5},{8,10},{9,11},{10,... | collective-permute-start | bytes 1572872 | tf_op jit(solution)/shard_map/ppermute | solution.py:487
  541.8 28.5 %collective-permute-start.32 = (bf16[128,2048]{1,0:T(8,128)(2,1)}, bf16[128,2048]{1,0:T(8,128)(2,1)}, u32[]{:S(2)}, u32[]{:S(2)}) collective-permute-start(bf16[128,2048]{1,0:T(8,128)(2,1)} %slice.629), channel_id=1, source_target_pairs={{0,1},{1,0},{2,3},{3,2},{4,5},{5,4},{6,7},{7,6},{8,9},{9,8},{10,11... | collective-permute-start | bytes 1572872 | tf_op jit(solution)/shard_map/ppermute | solution.py:487
  544.6 27.8 %collective-permute-start.33 = (bf16[128,2048]{1,0:T(8,128)(2,1)}, bf16[128,2048]{1,0:T(8,128)(2,1)}, u32[]{:S(2)}, u32[]{:S(2)}) collective-permute-start(bf16[128,2048]{1,0:T(8,128)(2,1)} %slice.630), channel_id=1, source_target_pairs={{0,2},{1,3},{2,0},{3,1},{4,6},{5,7},{6,4},{7,5},{8,10},{9,11},{10,... | collective-permute-start | bytes 1572872 | tf_op jit(solution)/shard_map/ppermute | solution.py:487
  564.7 306.4 %reduce-scatter.12.cloned.1.call-start = ((), (), s32[]{:S(2)}) async-start(), calls=%async_computation.11 | async-start | bytes 2359296 | tf_op jit(solution)/shard_map/reduce_scatter | solution.py:911
  676.0 206.8 %reduce-scatter.14.cloned.1.call-start = ((), (), s32[]{:S(2)}) async-start(), calls=%async_computation.12 | async-start | bytes 6488064 | tf_op jit(solution)/shard_map/reduce_scatter | solution.py:911
  676.0 15.1 %collective-permute-start.48 = (bf16[256,2048]{1,0:T(8,128)(2,1)}, bf16[256,2048]{1,0:T(8,128)(2,1)S(1)}, u32[]{:S(2)}, u32[]{:S(2)}) collective-permute-start(bf16[256,2048]{1,0:T(8,128)(2,1)} %get-tuple-element.202), channel_id=1, source_target_pairs={{0,1},{1,0},{2,3},{3,2},{4,5},{5,4},{6,7},{7,6},{8,9},{9,8},{10,11... | collective-permute-start | bytes 3145736 | tf_op jit(solution)/shard_map/ppermute | solution.py:487
  676.9 15.0 %collective-permute-start.49 = (bf16[256,2048]{1,0:T(8,128)(2,1)}, bf16[256,2048]{1,0:T(8,128)(2,1)S(1)}, u32[]{:S(2)}, u32[]{:S(2)}) collective-permute-start(bf16[256,2048]{1,0:T(8,128)(2,1)} %get-tuple-element.204), channel_id=1, source_target_pairs={{0,2},{1,3},{2,0},{3,1},{4,6},{5,7},{6,4},{7,5},{8,10},{9,11},{10,... | collective-permute-start | bytes 3145736 | tf_op jit(solution)/shard_map/ppermute | solution.py:487
  677.6 24.7 %collective-permute-start.52 = (bf16[256,2048]{1,0:T(8,128)(2,1)}, bf16[256,2048]{1,0:T(8,128)(2,1)S(1)}, u32[]{:S(2)}, u32[]{:S(2)}) collective-permute-start(bf16[256,2048]{1,0:T(8,128)(2,1)} %pad_maximum_fusion.9), channel_id=1, source_target_pairs={{0,1},{1,0},{2,3},{3,2},{4,5},{5,4},{6,7},{7,6},{8,9},{9,8},{10,11... | collective-permute-start | bytes 3145736 | tf_op jit(solution)/shard_map/ppermute | solution.py:487
  678.6 24.7 %collective-permute-start.53 = (bf16[256,2048]{1,0:T(8,128)(2,1)}, bf16[256,2048]{1,0:T(8,128)(2,1)}, u32[]{:S(2)}, u32[]{:S(2)}) collective-permute-start(bf16[256,2048]{1,0:T(8,128)(2,1)} %pad_maximum_fusion.10), channel_id=1, source_target_pairs={{0,2},{1,3},{2,0},{3,1},{4,6},{5,7},{6,4},{7,5},{8,10},{9,11},{10,... | collective-permute-start | bytes 3145736 | tf_op jit(solution)/shard_map/ppermute | solution.py:487
  696.6 220.7 %reduce-scatter.10.cloned.1.call-start = ((), (), s32[]{:S(2)}) async-start(), calls=%async_computation.10 | async-start | bytes 10027008 | tf_op jit(solution)/shard_map/reduce_scatter | solution.py:911
  819.3 15.1 %collective-permute-start.56 = (bf16[256,2048]{1,0:T(8,128)(2,1)}, bf16[256,2048]{1,0:T(8,128)(2,1)S(1)}, u32[]{:S(2)}, u32[]{:S(2)}) collective-permute-start(bf16[256,2048]{1,0:T(8,128)(2,1)} %get-tuple-element.207), channel_id=1, source_target_pairs={{0,1},{1,0},{2,3},{3,2},{4,5},{5,4},{6,7},{7,6},{8,9},{9,8},{10,11... | collective-permute-start | bytes 3145736 | tf_op jit(solution)/shard_map/ppermute | solution.py:487
  820.3 15.0 %collective-permute-start.57 = (bf16[256,2048]{1,0:T(8,128)(2,1)}, bf16[256,2048]{1,0:T(8,128)(2,1)S(1)}, u32[]{:S(2)}, u32[]{:S(2)}) collective-permute-start(bf16[256,2048]{1,0:T(8,128)(2,1)} %get-tuple-element.209), channel_id=1, source_target_pairs={{0,2},{1,3},{2,0},{3,1},{4,6},{5,7},{6,4},{7,5},{8,10},{9,11},{10,... | collective-permute-start | bytes 3145736 | tf_op jit(solution)/shard_map/ppermute | solution.py:487
  839.7 19.4 %collective-permute-start.60 = (bf16[256,2048]{1,0:T(8,128)(2,1)}, bf16[256,2048]{1,0:T(8,128)(2,1)S(1)}, u32[]{:S(2)}, u32[]{:S(2)}) collective-permute-start(bf16[256,2048]{1,0:T(8,128)(2,1)} %pad_maximum_fusion.11), channel_id=1, source_target_pairs={{0,1},{1,0},{2,3},{3,2},{4,5},{5,4},{6,7},{7,6},{8,9},{9,8},{10,11... | collective-permute-start | bytes 3145736 | tf_op jit(solution)/shard_map/ppermute | solution.py:487
  840.8 18.4 %collective-permute-start.61 = (bf16[256,2048]{1,0:T(8,128)(2,1)S(1)}, bf16[256,2048]{1,0:T(8,128)(2,1)S(1)}, u32[]{:S(2)}, u32[]{:S(2)}) collective-permute-start(bf16[256,2048]{1,0:T(8,128)(2,1)S(1)} %copy-done.33), channel_id=1, source_target_pairs={{0,2},{1,3},{2,0},{3,1},{4,6},{5,7},{6,4},{7,5},{8,10},{9,11},{10,... | collective-permute-start | bytes 3145736 | tf_op jit(solution)/shard_map/ppermute | solution.py:487
  849.9 15.7 %collective-permute-start.73 = (f32[8,128]{1,0:T(8,128)S(1)}, f32[8,128]{1,0:T(8,128)S(1)}, u32[]{:S(2)}, u32[]{:S(2)}) collective-permute-start(f32[8,128]{1,0:T(8,128)S(1)} %add.339), channel_id=1, source_target_pairs={{0,8},{4,12},{8,0},{12,4},{16,24},{20,28},{24,16},{28,20},{1,9},{5... | collective-permute-start | bytes 12296 | tf_op jit(solution)/shard_map/ppermute | solution.py:487
  852.5 15.6 %collective-permute-start.69 = (f32[16,512]{1,0:T(8,128)S(1)}, f32[16,512]{1,0:T(8,128)S(1)}, u32[]{:S(2)}, u32[]{:S(2)}) collective-permute-start(f32[16,512]{1,0:T(8,128)S(1)} %pad_maximum_fusion.13), channel_id=1, source_target_pairs={{0,4},{4,0},{8,12},{12,8},{16,20},{20,16},{24,28},{28,24},{1,5},{5... | collective-permute-start | bytes 98312 | tf_op jit(solution)/shard_map/ppermute | solution.py:487
  862.5 14.9 %collective-permute-start.62 = (bf16[128,2048]{1,0:T(8,128)(2,1)}, bf16[128,2048]{1,0:T(8,128)(2,1)}, u32[]{:S(2)}, u32[]{:S(2)}) collective-permute-start(bf16[128,2048]{1,0:T(8,128)(2,1)} %get-tuple-element.346), channel_id=1, source_target_pairs={{0,2},{1,3},{2,0},{3,1},{4,6},{5,7},{6,4},{7,5},{8,10},{9,11},{10,... | collective-permute-start | bytes 1572872 | tf_op jit(solution)/shard_map/ppermute | solution.py:487
  862.9 14.5 %collective-permute-start.63 = (bf16[128,2048]{1,0:T(8,128)(2,1)}, bf16[128,2048]{1,0:T(8,128)(2,1)}, u32[]{:S(2)}, u32[]{:S(2)}) collective-permute-start(bf16[128,2048]{1,0:T(8,128)(2,1)} %get-tuple-element.347), channel_id=1, source_target_pairs={{0,1},{1,0},{2,3},{3,2},{4,5},{5,4},{6,7},{7,6},{8,9},{9,8},{10,11... | collective-permute-start | bytes 1572872 | tf_op jit(solution)/shard_map/ppermute | solution.py:487
  (112 other events, 1404.4 us)
Sparse Core Ops, SparseCore 0:
  9.7 63.1 all-gather.3
  74.5 59.0 all-gather.5
  135.3 59.0 all-gather.7
  499.5 65.1 reduce-scatter.5
  566.8 63.1 reduce-scatter.7
  676.1 35.3 reduce-scatter.11
  713.8 63.6 reduce-scatter.13
  819.4 97.8 reduce-scatter.9

commit v3 on v2

--- a/solution.py
+++ b/solution.py
@@ -69,14 +69,20 @@
     return log_alpha, beta, decay_sum, growth, tail, keep
 
 
-def conv_of(ext_ref, conv_ref, aux, m, index, head, rows, width):
+def spread_out(columns, index):
+    return jnp.broadcast_to(columns[:, index : index + 1], (columns.shape[0], HD))
+
+
+def conv_of(ext_ref, conv_ref, masks, m, index, head, rows, width):
     lanes = slice(index * width + head * HD, index * width + (head + 1) * HD)
     own = slice(head * HD, (head + 1) * HD)
-    total = ext_ref[m, 8 : 8 + rows, lanes] * conv_ref[4 * index : 4 * index + 1, own]
+    taps = [ext_ref[m, 8 : 8 + rows, lanes]]
     for j in range(1, 4):
-        line = slice(4 * index + j, 4 * index + j + 1)
-        total = total + ext_ref[m, 8 - j : 8 - j + rows, lanes] * conv_ref[line, own] * aux[:, j : j + 1]
-    return total
+        taps.append(ext_ref[m, 8 - j : 8 - j + rows, lanes] * masks[j - 1])
+    total = taps[0] * conv_ref[4 * index : 4 * index + 1, own]
+    for j in range(1, 4):
+        total = total + taps[j] * conv_ref[4 * index + j : 4 * index + j + 1, own]
+    return total, taps
 
 
 def invert_unit_lower(powers, row_ids, col_ids):
@@ -121,31 +127,32 @@
         aux = aux_ref[m, 0]
         small = raw_ref[0, m, :, 4 * width : 4 * width + LANES]
         _, beta, decay_sum, growth, tail, keep = chunk_gates(small, scal_ref, aux, tri)
+        masks = [spread_out(aux, j) for j in range(1, 4)]
         decay_rows = decay_sum.T
         below = (row_ids >= col_ids) & (aux[:, 0:1] == segrow_ref[m, 0, 0:1, :])
         for head in range(heads):
-            query = conv_of(ext_ref, conv_ref, aux, m, 0, head, rows, width)
+            query, _ = conv_of(ext_ref, conv_ref, masks, m, 0, head, rows, width)
             query = query * sigmoid(query)
             query = query * (
                 lax.rsqrt(jnp.sum(query * query, axis=-1, keepdims=True) + 1e-06) * SCALE
             )
-            key = conv_of(ext_ref, conv_ref, aux, m, 1, head, rows, width)
+            key, _ = conv_of(ext_ref, conv_ref, masks, m, 1, head, rows, width)
             key = key * sigmoid(key)
             key = key * lax.rsqrt(jnp.sum(key * key, axis=-1, keepdims=True) + 1e-06)
-            value = conv_of(ext_ref, conv_ref, aux, m, 2, head, rows, width)
+            value, _ = conv_of(ext_ref, conv_ref, masks, m, 2, head, rows, width)
             value = value * sigmoid(value)
-            b_col = beta[:, heads + head : heads + head + 1]
+            b_col = spread_out(beta, heads + head)
             spread = decay_sum[:, head : head + 1] - decay_rows[head : head + 1, :]
             inside = jnp.exp(jnp.where(below, spread, -1e30))
             both = jnp.concatenate([key, query], axis=0).astype(BF)
             dots = mm_nt(both, both[:rows])
             stacked.append(both)
             values.append(value)
-            powers.append(jnp.where(strict, b_col * dots[:rows] * inside, 0.0))
+            powers.append(jnp.where(strict, b_col[:, :rows] * dots[:rows] * inside, 0.0))
             outs.append((dots[rows:] * inside).astype(BF))
             betas.append(b_col)
-            growths.append(growth[:, head : head + 1])
-            tails.append(tail[:, head : head + 1])
+            growths.append(spread_out(growth, head))
+            tails.append(spread_out(tail, head))
             keeps.append(keep[:, head : head + 1])
     inverses = invert_unit_lower(powers, row_ids, col_ids)
     states = [state_ref[m, h] for m, h in chains]
@@ -204,28 +211,27 @@
     line_ids = lax.broadcasted_iota(jnp.int32, (LANES, rows), 0)
     last_row = lax.broadcasted_iota(jnp.int32, (rows, 1), 0) == rows - 1
 
-    def conv_back(m, index, head, aux, d_conv):
+    def conv_back(m, index, head, later, taps, d_conv):
         lanes = slice(index * width + head * HD, index * width + (head + 1) * HD)
         own = slice(head * HD, (head + 1) * HD)
         dext_ref[m, 0:rows, lanes] = d_conv
         total = d_conv * conv_ref[4 * index : 4 * index + 1, own]
-        dconv_ref[4 * index : 4 * index + 1, own] += jnp.sum(
-            d_conv * ext_ref[m, 8 : 8 + rows, lanes], axis=0, keepdims=True
-        )
+        for j in range(4):
+            line = 4 * index + j
+            dconv_ref[8 * line : 8 * line + 8, own] += jnp.sum(
+                (d_conv * taps[j]).reshape(rows // 8, 8, HD), axis=0
+            )
         for j in range(1, 4):
             line = slice(4 * index + j, 4 * index + j + 1)
-            total = total + dext_ref[m, j : j + rows, lanes] * conv_ref[line, own] * aux[:, 7 + j : 8 + j]
-            dconv_ref[line, own] += jnp.sum(
-                d_conv * ext_ref[m, 8 - j : 8 - j + rows, lanes] * aux[:, j : j + 1],
-                axis=0,
-                keepdims=True,
-            )
+            total = total + dext_ref[m, j : j + rows, lanes] * conv_ref[line, own] * later[j - 1]
         draw_ref[0, m, :, lanes] = total.astype(BF)
 
     for m in range(group):
         aux = aux_ref[m, 0]
         small = raw_ref[0, m, :, 4 * width : 4 * width + LANES]
         log_alpha, beta, decay_sum, growth, tail, keep = chunk_gates(small, scal_ref, aux, tri)
+        masks = [spread_out(aux, j) for j in range(1, 4)]
+        later = [spread_out(aux, 7 + j) for j in range(1, 4)]
         decay_rows = decay_sum.T
         below = (row_ids >= col_ids) & (aux[:, 0:1] == segrow_ref[m, 0, 0:1, :])
         d_decay = jnp.zeros((rows, LANES), F32)
@@ -233,9 +239,9 @@
         d_decay_lines = jnp.zeros((LANES, rows), F32)
         everyone = range(heads)
         own_lanes = [slice(h * HD, (h + 1) * HD) for h in everyone]
-        b_cols = [beta[:, heads + h : heads + h + 1] for h in everyone]
-        g_cols = [growth[:, h : h + 1] for h in everyone]
-        t_cols = [tail[:, h : h + 1] for h in everyone]
+        b_cols = [spread_out(beta, heads + h) for h in everyone]
+        g_cols = [spread_out(growth, h) for h in everyone]
+        t_cols = [spread_out(tail, h) for h in everyone]
         keeps = [keep[:, h : h + 1] for h in everyone]
         d_cores, queries, keys, values = [], [], [], []
         for h in everyone:
@@ -259,15 +265,15 @@
             )
             parts = []
             for index in range(3):
-                conv = conv_of(ext_ref, conv_ref, aux, m, index, h, rows, width)
+                conv, taps = conv_of(ext_ref, conv_ref, masks, m, index, h, rows, width)
                 gate = sigmoid(conv)
                 act = conv * gate
                 slope = gate * (1.0 + conv * (1.0 - gate))
                 if index == 2:
-                    parts.append((act, slope))
+                    parts.append((act, slope, taps))
                 else:
                     root = lax.rsqrt(jnp.sum(act * act, axis=-1, keepdims=True) + 1e-06)
-                    parts.append((act * root, slope * root))
+                    parts.append((act * root, slope * root, taps))
             queries.append(parts[0])
             keys.append(parts[1])
             values.append(parts[2])
@@ -304,16 +310,16 @@
             key_dots = dots[h][:rows]
             d_query_dots = d_weights * insides[h]
             power_in = jnp.where(strict, d_power * insides[h], 0.0)
-            d_key_dots = power_in * b_cols[h]
+            d_key_dots = power_in * b_cols[h][:, :rows]
             reach = d_weights * outs[h] + d_key_dots * key_dots
             key_rest = jnp.sum(key * rest_state, axis=-1, keepdims=True)
             d_beta_col = (
                 jnp.sum(power_in * key_dots, axis=-1, keepdims=True)
                 + jnp.sum(d_rests[h] * values[h][0], axis=-1, keepdims=True)
-                - g_cols[h] * key_rest
-            )
-            d_growth = SCALE * jnp.sum(query * core_state, axis=-1, keepdims=True) - b_cols[h] * key_rest
-            tail_part = t_cols[h] * jnp.sum(d_tail_keys[h] * key, axis=-1, keepdims=True)
+                - growth[:, h : h + 1] * key_rest
+            )
+            d_growth = SCALE * jnp.sum(query * core_state, axis=-1, keepdims=True) - beta[:, heads + h : heads + h + 1] * key_rest
+            tail_part = tail[:, h : h + 1] * jnp.sum(d_tail_keys[h] * key, axis=-1, keepdims=True)
             last_part = jnp.sum(tail_part, axis=0, keepdims=True) + keeps[h] * jnp.sum(
                 jnp.sum(d_states[h] * states[h].astype(F32), axis=0, keepdims=True),
                 axis=-1,
@@ -321,7 +327,7 @@
             )
             d_sum_col = (
                 jnp.sum(reach, axis=-1, keepdims=True)
-                + g_cols[h] * d_growth
+                + growth[:, h : h + 1] * d_growth
                 - tail_part
                 + jnp.where(last_row, last_part, 0.0)
             )
@@ -344,14 +350,14 @@
                 jnp.concatenate([query * (SCALE * g_cols[h]), key * scale_rest], axis=0), pairs[h]
             )
             conv_back(
-                m, 0, h, aux,
+                m, 0, h, later, queries[h][2],
                 queries[h][1] * (d_query - query * jnp.sum(query * d_query, axis=-1, keepdims=True)),
             )
             conv_back(
-                m, 1, h, aux,
+                m, 1, h, later, keys[h][2],
                 keys[h][1] * (d_key - key * jnp.sum(key * d_key, axis=-1, keepdims=True)),
             )
-            conv_back(m, 2, h, aux, b_cols[h] * d_rests[h] * values[h][1])
+            conv_back(m, 2, h, later, values[h][2], b_cols[h] * d_rests[h] * values[h][1])
         d_log = mm_exact(upper, d_decay - d_decay_lines.T)
         d_arg = d_log * scal_ref[0:1, :] * sigmoid(small + scal_ref[1:2, :])
         dscal_ref[0:1, :] += jnp.sum(d_log * log_alpha, axis=0, keepdims=True)
@@ -458,7 +464,7 @@
             ],
             out_specs=[
                 pl.BlockSpec((1, group, rows, total), at),
-                whole((16, width)),
+                whole((96, width)),
                 whole((8, LANES)),
                 whole((8, width)),
             ],
@@ -470,7 +476,7 @@
         ),
         out_shape=[
             jax.ShapeDtypeStruct((blocks, group, rows, total), BF),
-            jax.ShapeDtypeStruct((16, width), F32),
+            jax.ShapeDtypeStruct((96, width), F32),
             jax.ShapeDtypeStruct((8, LANES), F32),
             jax.ShapeDtypeStruct((8, width), F32),
         ],
@@ -548,11 +554,12 @@
     return [hop(after(to_x, *earlier), 1), hop(after(to_y, *earlier), 2), keep]
 
 
-def scatter_far(near):
+def scatter_far(near, *earlier):
     if len(near) == 1:
         return near[0].astype(F32)
     in_x, in_y, keep = near
     half = in_x.shape[0] // 2
+    keep = after(keep, *earlier)
     pass_y = (keep[2 * half : 3 * half].astype(F32) + in_x[half:].astype(F32)).astype(BF)
     pass_x = (keep[3 * half :].astype(F32) + in_y[half:].astype(F32)).astype(BF)
     last_y = hop(pass_y, 2).astype(F32)
@@ -562,15 +569,61 @@
     return keep[: 2 * half].astype(F32) + near_sum + last
 
 
-def arranged(product, size):
-    rows = product.shape[0] // size
+def scatter_kernel(size, where, transposed, x_ref, w_ref, *refs):
+    outs, buf, sem = refs[:-2], refs[-2], refs[-1]
+    step = pl.program_id(0)
+    half = x_ref.shape[0] // 2
+    slot = lax.rem(step, 2)
+
+    def stores(block):
+        return [
+            pltpu.make_async_copy(
+                buf.at[block % 2, h * half : (h + 1) * half],
+                outs[where[(block, h)][0]].at[where[(block, h)][1] : where[(block, h)][1] + half],
+                sem.at[block % 2, h],
+            )
+            for h in (0, 1)
+        ]
+
+    for block in range(2, size):
+        @pl.when(step == block)
+        def _(block=block):
+            for copy in stores(block - 2):
+                copy.wait()
+
+    x = x_ref[...]
+    buf[slot] = (mm_nt(x, w_ref[...]) if transposed else mm(x, w_ref[...])).astype(BF)
+    for block in range(size):
+        @pl.when(step == block)
+        def _(block=block):
+            for copy in stores(block):
+                copy.start()
+            if block == size - 1:
+                for earlier in range(max(0, size - 2), size):
+                    for copy in stores(earlier):
+                        copy.wait()
+
+
+def scatter_matmul(values, weight, size, transposed=False):
+    rows = values.shape[0] // size
+    width = weight.shape[0] if transposed else weight.shape[1]
     counts, where = scatter_plan(size, rows)
-    half = rows // 2
-    pieces = [[None] * (count // half) for count in counts]
-    for (block, h), (index, at) in where.items():
-        start = block * rows + h * half
-        pieces[index][at // half] = product[start : start + half]
-    return [jnp.concatenate(item, axis=0).astype(BF) for item in pieces]
+    return list(pl.pallas_call(
+        lambda *refs: scatter_kernel(size, where, transposed, *refs),
+        grid=(size,),
+        in_specs=[
+            pl.BlockSpec((rows, values.shape[1]), lambda i: (i, 0)),
+            pl.BlockSpec(weight.shape, lambda i: (0, 0)),
+        ],
+        out_specs=[pl.BlockSpec(memory_space=pl.ANY)] * len(counts),
+        out_shape=[jax.ShapeDtypeStruct((count, width), BF) for count in counts],
+        scratch_shapes=[pltpu.VMEM((2, rows, width), BF), pltpu.SemaphoreType.DMA((2, 2))],
+        compiler_params=pltpu.CompilerParams(**PARAMS),
+        cost_estimate=pl.CostEstimate(
+            flops=4 * values.size * width, bytes_accessed=15_000_000, transcendentals=0
+        ),
+        name="scatter_matmul",
+    )(values, weight))
 
 
 def ffn_kernel(turns, rows, parts, n_pieces, where, n_out, aliased, *refs):
@@ -730,32 +783,104 @@
     return flat, list(out[5:])
 
 
+def piece_kernel(size, parts, n_pieces, transposed, *refs):
+    pieces, w_ref, out_ref, copy_ref, xbuf, x_sem = refs[:n_pieces], *refs[n_pieces:]
+    step = pl.program_id(0)
+
+    def loads(block):
+        slot = block % 2
+        found, place = [], 0
+        for k, (index, at, count) in enumerate(parts[block]):
+            found.append(
+                pltpu.make_async_copy(
+                    pieces[index].at[at : at + count],
+                    xbuf.at[slot, place : place + count],
+                    x_sem.at[slot, k],
+                )
+            )
+            place += count
+        return found
+
+    for block in range(size):
+        @pl.when(step == block)
+        def _(block=block):
+            if block == 0:
+                for copy in loads(0):
+                    copy.start()
+            if block + 1 < size:
+                for copy in loads(block + 1):
+                    copy.start()
+            for copy in loads(block):
+                copy.wait()
+
+    x = xbuf[lax.rem(step, 2)]
+    copy_ref[0] = x
+    out_ref[0] = mm_nt(x, w_ref[...]) if transposed else mm(x, w_ref[...])
+
+
+def piece_matmul(pieces, weight, size, transposed=False):
+    width = pieces[0].shape[1]
+    rows = pieces[0].shape[0] if size == 4 else pieces[0].shape[0] // size
+    columns = weight.shape[0] if transposed else weight.shape[1]
+    parts = block_parts(size, rows)
+    return pl.pallas_call(
+        lambda *refs: piece_kernel(size, parts, len(pieces), transposed, *refs),
+        grid=(size,),
+        in_specs=[pl.BlockSpec(memory_space=pl.ANY)] * len(pieces)
+        + [pl.BlockSpec(weight.shape, lambda i: (0, 0))],
+        out_specs=[
+            pl.BlockSpec((1, rows, columns), lambda i: (i, 0, 0)),
+            pl.BlockSpec((1, rows, width), lambda i: (i, 0, 0)),
+        ],
+        out_shape=[
+            jax.ShapeDtypeStruct((size, rows, columns), F32),
+            jax.ShapeDtypeStruct((size, rows, width), BF),
+        ],
+        scratch_shapes=[pltpu.VMEM((2, rows, width), BF), pltpu.SemaphoreType.DMA((2, 2))],
+        compiler_params=pltpu.CompilerParams(**PARAMS),
+        cost_estimate=pl.CostEstimate(
+            flops=4 * size * rows * width * columns, bytes_accessed=30_000_000, transcendentals=0
+        ),
+        name="piece_matmul",
+    )(*pieces, weight)
+
+
 def wgrad_kernel(count, *refs):
-    lefts, rights, out_ref = refs[:count], refs[count : 2 * count], refs[2 * count]
+    lefts, rights, rest = refs[:count], refs[count : 2 * count], refs[2 * count :]
     total = mm_tn(lefts[0][...], rights[0][...])
     for left, right in zip(lefts[1:], rights[1:]):
         total = total + mm_tn(left[...], right[...])
-    out_ref[...] = total.astype(BF)
-
-
-def weight_gradient(lefts, rights):
-    depth, wide = lefts[0].shape
+    out_ref = rest[-1]
+    if len(rest) == 1:
+        out_ref[...] = total.astype(BF)
+    else:
+        columns = total.shape[1]
+        out_ref[:, :columns] = total.astype(BF)
+        out_ref[:, columns:] = rest[0][...]
+
+
+def weight_gradient(lefts, rights, beside=None):
+    wide = lefts[0].shape[1]
     columns = rights[0].shape[1]
+    extra = [] if beside is None else [beside]
+    full = columns + sum(item.shape[1] for item in extra)
     tile = 512 if wide % 512 == 0 else wide
     count = len(lefts)
+    depth = sum(left.shape[0] for left in lefts)
     return pl.pallas_call(
         lambda *refs: wgrad_kernel(count, *refs),
         grid=(wide // tile,),
-        in_specs=[pl.BlockSpec((depth, tile), lambda i: (0, i))] * count
-        + [pl.BlockSpec((depth, columns), lambda i: (0, 0))] * count,
-        out_specs=pl.BlockSpec((tile, columns), lambda i: (i, 0)),
-        out_shape=jax.ShapeDtypeStruct((wide, columns), BF),
+        in_specs=[pl.BlockSpec((left.shape[0], tile), lambda i: (0, i)) for left in lefts]
+        + [pl.BlockSpec(right.shape, lambda i: (0, 0)) for right in rights]
+        + [pl.BlockSpec((tile, item.shape[1]), lambda i: (i, 0)) for item in extra],
+        out_specs=pl.BlockSpec((tile, full), lambda i: (i, 0)),
+        out_shape=jax.ShapeDtypeStruct((wide, full), BF),
         compiler_params=pltpu.CompilerParams(**PARAMS),
         cost_estimate=pl.CostEstimate(
-            flops=3 * count * depth * wide * columns, bytes_accessed=20_000_000, transcendentals=0
+            flops=3 * depth * wide * columns, bytes_accessed=20_000_000, transcendentals=0
         ),
         name="weight_gradient",
-    )(*lefts, *rights)
+    )(*lefts, *rights, *extra)
 
 
 def block_places(size):
@@ -842,12 +967,13 @@
     cots = [item.astype(BF) for item in grads]
     in_a1 = gather_near(normed_in[0])
     w_in = jnp.concatenate(
-        [after(w_query, in_a1), w_key, w_value, w_outgate, w_decay, w_beta,
+        [w_query, w_key, w_value, w_outgate, w_decay, w_beta,
          jnp.zeros((width, LANES - 2 * heads), BF)], axis=1
     )
 
-    def project(full):
-        return times(full, w_in).reshape(blocks, group, rows, 4 * own + LANES)
+    def project(pieces):
+        raw, full = piece_matmul(pieces, w_in, blocks)
+        return raw.reshape(blocks, group, rows, 4 * own + LANES), full.reshape(span, width)
 
     def mix(raw, i):
         mixed, *saved = mixer_forward(
@@ -856,7 +982,7 @@
         return mixed.reshape(span, own), saved
 
     def out_of(mixed):
-        return arranged(times(mixed, w_out), blocks)
+        return scatter_matmul(mixed, w_out, blocks)
 
     def middle(i, attn):
         resid = inputs[i] + attn
@@ -865,43 +991,45 @@
 
     in_a2 = gather_far(in_a1)
     in_b1 = gather_near(normed_in[1], in_a2)
-    full_a = joined(in_a1 + in_a2)
-    raw_a = project(full_a)
-    in_b2 = gather_far(in_b1)
-    mixed_a, saved_a = mix(raw_a, 0)
-    attn_a = out_of(after(mixed_a, in_b1))
-    full_b = joined(in_b1 + in_b2)
+    raw_a, full_a = project(in_a1 + in_a2)
+    in_b2 = gather_far(in_b1, raw_a)
+    cot_a1 = gather_near(cots[0], in_b1)
+    mixed_a, saved_a = mix(after(raw_a, in_b1), 0)
+    attn_a = out_of(after(mixed_a, in_b2))
     at_a1 = scatter_near(attn_a)
-    raw_b = project(after(full_b, attn_a))
-    cot_a1 = gather_near(cots[0], at_a1)
+    pieces_b = in_b1 + in_b2
+    raw_b, full_b = project([after(pieces_b[0], attn_a, cot_a1)] + pieces_b[1:])
+    sum_a = scatter_far(at_a1, raw_b)
+    cot_a2 = gather_far(cot_a1, raw_b)
     mixed_b, saved_b = mix(after(raw_b, at_a1), 1)
-    sum_a = scatter_far(at_a1)
-    cot_a2 = gather_far(cot_a1)
-    attn_b = out_of(after(mixed_b, sum_a, cot_a1))
     resid_a, pull_a, mid_a = middle(0, sum_a)
     mid_a1 = gather_near(mid_a)
-    at_b1 = scatter_near(attn_b, cot_a1)
-    mid_a2 = gather_far(mid_a1)
-    sum_b = scatter_far(at_b1)
-    resid_b, pull_b, mid_b = middle(1, sum_b)
-    mid_b1 = gather_near(mid_b, mid_a2, cot_a2)
-    cot_b1 = gather_near(cots[1], mid_a2, cot_a2)
+    attn_b = out_of(after(mixed_b, mid_a, cot_a2))
+    at_b1 = scatter_near(attn_b, mid_a1)
+    mid_a2 = gather_far(mid_a1, attn_b)
 
     ffn_weights = [ffn_gate, ffn_up, ffn_down]
     first_turns = (1, 3) if blocks == 4 else tuple(range(blocks // 2))
     last_turns = tuple(r for r in range(blocks) if r not in first_turns)
     outs = len(scatter_plan(blocks, own_rows)[0])
-    kept_a, begun = ffn_stage(first_turns, mid_a1 + mid_a2, cot_a1 + cot_a2, ffn_weights, blocks)
-    mid_b2 = gather_far(mid_b1)
-    cot_b2 = gather_far(cot_b1)
-    begun = [after(begun[0], mid_b1)] + begun[1:]
+    near_a = mid_a1 + mid_a2
+    near_a[0] = after(near_a[0], at_b1)
+    sum_b = scatter_far(at_b1)
+    cot_b1 = gather_near(cots[1], at_b1)
+    kept_a, begun = ffn_stage(first_turns, near_a, cot_a1 + cot_a2, ffn_weights, blocks)
+    resid_b, pull_b, mid_b = middle(1, sum_b)
+    mid_b1 = gather_near(mid_b, kept_a[0])
+    cot_b2 = gather_far(cot_b1, kept_a[0])
+    begun[0] = after(begun[0], mid_b, cot_b1)
     kept_a2, out_a = ffn_stage(
-        last_turns, mid_a1 + mid_a2, cot_a1 + cot_a2, ffn_weights, blocks, begun
+        last_turns, near_a, cot_a1 + cot_a2, ffn_weights, blocks, begun
     )
-    gm_a1 = scatter_near(out_a[:outs])
+    mid_b2 = gather_far(mid_b1, kept_a2[0], cot_b2)
+    gm_a1 = scatter_near(out_a[:outs], mid_b2)
     near_b = mid_b1 + mid_b2
     near_b[0] = after(near_b[0], out_a[0])
     kept_b, begun = ffn_stage(first_turns, near_b, cot_b1 + cot_b2, ffn_weights, blocks)
+    d_mid_a = scatter_far(gm_a1, kept_b[0])
     begun = [after(begun[0], gm_a1)] + begun[1:]
     kept_b2, out_b = ffn_stage(last_turns, near_b, cot_b1 + cot_b2, ffn_weights, blocks, begun)
     kept = [kept_a, kept_a2, kept_b, kept_b2]
@@ -915,54 +1043,61 @@
         d_resid = grads[i] + d_resid
         return d_resid, d_norm, d_resid.astype(BF)
 
-    d_mid_a = scatter_far(gm_a1)
     gm_b1 = scatter_near(out_b[:outs], d_mid_a)
     d_resid_a, gain_mid_a, low_a = resid_back(0, pull_a, d_mid_a)
+    rg_a1 = gather_near(low_a)
     gates[0] = after(gates[0], low_a)
-    rg_a1 = gather_near(low_a)
     term_gate = weight_gradient(mids, gates)
     grad_gate = share(term_gate)
-    rg_a2 = gather_far(rg_a1)
-    d_mid_b = scatter_far(gm_b1)
+    rg_a2 = gather_far(rg_a1, term_gate)
+    d_mid_b = scatter_far(gm_b1, term_gate)
     ups[0] = after(ups[0], term_gate, rg_a1, gm_b1)
     term_up = weight_gradient(mids, ups)
     grad_up = share(term_up)
-    d_resid_b, gain_mid_b, low_b = resid_back(1, pull_b, d_mid_b)
+    d_resid_b, gain_mid_b, low_b = resid_back(1, pull_b, after(d_mid_b, term_up))
     rg_b1 = gather_near(low_b)
-    rg_b2 = gather_far(rg_b1)
-    full_ra = joined(rg_a1 + rg_a2)
-    full_rb = joined(rg_b1 + rg_b2)
-
-    def back(i, full, raw, saved):
-        d_mixed = contract_cols(full, w_out).reshape(blocks, group, rows, own)
-        return mixer_backward(
+    ff_a1 = scatter_near(out_a[outs:], low_b)
+
+    def to_mixed(pieces):
+        d_mixed, full = piece_matmul(pieces, w_out, blocks, transposed=True)
+        return d_mixed.reshape(blocks, group, rows, own), full.reshape(span, width)
+
+    def mix_back(i, d_mixed, raw, saved):
+        d_raw, *sums = mixer_backward(
             place, raw, of_group(aux, i), of_group(lines, i), conv_rows, scal, gain_row,
             d_mixed, saved,
         )
+        return d_raw.reshape(span, 4 * own + LANES), sums
 
     def in_back(d_raw):
-        return arranged(contract_cols(d_raw, w_in), blocks)
-
-    d_raw_a, *sums_a = back(0, after(full_ra, term_up, low_b), raw_a, saved_a)
-    d_raw_a = d_raw_a.reshape(span, 4 * own + LANES)
-    acts[0] = after(acts[0], d_raw_a, rg_b1)
+        return scatter_matmul(d_raw, w_in, blocks, transposed=True)
+
+    pieces_ra = rg_a1 + rg_a2
+    pieces_ra[0] = after(pieces_ra[0], low_b)
+    d_mixed_a, full_ra = to_mixed(pieces_ra)
+    d_raw_a, sums_a = mix_back(0, d_mixed_a, raw_a, saved_a)
+    rg_b2 = gather_far(rg_b1, d_raw_a)
+    ffn_a = scatter_far(ff_a1, d_raw_a)
+    d_in_a = in_back(after(d_raw_a, ff_a1, rg_b1))
+    gi_a1 = scatter_near(d_in_a)
+    pieces_rb = rg_b1 + rg_b2
+    pieces_rb[0] = after(pieces_rb[0], d_in_a, ffn_a)
+    d_mixed_b, full_rb = to_mixed(pieces_rb)
+    acts[0] = after(acts[0], d_mixed_b)
     term_down = weight_gradient(cot_all, acts)
-    grad_down = share(term_down)
-    d_in_a = in_back(after(d_raw_a, term_down, rg_b2))
-    gi_a1 = scatter_near(d_in_a)
-    ff_a1 = scatter_near(out_a[outs:], d_in_a)
-    term_out = weight_gradient([after(full_ra, d_in_a), full_rb], [mixed_a, mixed_b])
-    grad_out = share(term_out).T
-    d_raw_b, *sums_b = back(1, after(full_rb, term_out, grad_gate), raw_b, saved_b)
-    d_raw_b = d_raw_b.reshape(span, 4 * own + LANES)
-    d_norm_a = scatter_far(gi_a1)
-    ffn_a = scatter_far(ff_a1)
-    ff_b1 = scatter_near(out_b[outs:], d_norm_a, ffn_a)
-    d_in_b = in_back(after(d_raw_b, d_norm_a, ffn_a, grad_up))
-    gi_b1 = scatter_near(d_in_b)
-    term_in = weight_gradient([full_a, full_b], [d_raw_a, after(d_raw_b, d_in_b)])
+    term_out = weight_gradient(
+        [full_ra, full_rb], [after(mixed_a, gi_a1), mixed_b], term_down
+    )
+    shared_out = share(term_out)
+    grad_out, grad_down = shared_out[:, :own].T, shared_out[:, own:]
+    ff_b1 = scatter_near(out_b[outs:], term_out)
+    d_raw_b, sums_b = mix_back(1, after(d_mixed_b, term_out), raw_b, saved_b)
+    term_in = weight_gradient([full_a, full_b], [d_raw_a, after(d_raw_b, ff_b1)])
     grad_in = share(term_in)
-    ffn_b = scatter_far(ff_b1)
+    d_norm_a = scatter_far(gi_a1, term_in)
+    ffn_b = scatter_far(ff_b1, term_in)
+    d_in_b = in_back(after(d_raw_b, term_in))
+    gi_b1 = scatter_near(d_in_b, d_norm_a, ffn_b)
     d_norm_b = scatter_far(gi_b1)
 
     results, input_grads = [], []
@@ -976,10 +1111,11 @@
         gain_in = gain_in + d_gain
     gain_mid = gain_mid_a + gain_mid_b
     small_sums = [left + right for left, right in zip(sums_a, sums_b)]
-    small_sums[0] = after(small_sums[0], d_in_b)
-    wide = jnp.concatenate([small_sums[0][:12], small_sums[2][:4]], axis=0)
-    wide = butterfly(wide, ("dp",))
-    narrow = butterfly(small_sums[1], ("dp",))
+    conv_sum = jnp.sum(small_sums[0].reshape(12, 8, own), axis=1)
+    scal_sum = jnp.pad(small_sums[1][:2, :heads], ((0, 0), (0, own - heads)))
+    wide = jnp.concatenate([conv_sum, small_sums[2][:1], scal_sum, jnp.zeros((1, own), F32)], axis=0)
+    wide = butterfly(after(wide, term_in), ("dp",))
+    narrow = wide[13:15]
     gains = butterfly(jnp.stack([gain_in, gain_mid]), ("dp", "head"))
     return (
         jnp.concatenate(results, axis=0),

time: 935 us -> 818 us (0.87)
  waiting for transfers between devices: 272 us -> 172 us
  Pallas kernels: 337 us -> 424 us
  matrix products: 72.1 us -> 0 us
  local copies, waits for them, and re-layouts: 82.2 us -> 60 us
  other arithmetic: 68.2 us -> 55.1 us
    pallas_call x0 -> x8, Pallas kernels: none -> 93.8 us  [the longest x4 50.2 us: piece_matmul(): pl.pallas_call(lambda *refs: piece_kernel(size, parts, len(pieces), trans...]
    ppermute x75 -> x72, waiting for transfers between devices: 259 us -> 166 us  [hop(): return lax.ppermute(values, axis, [(i, i ^ bit) for i in range(size)])]
    dot_general x8 -> x0, matrix products: 72.1 us -> none  [the longest x4 40 us: contract_cols(): lax.dot_general(left, right, (((1,), (1,)), ((), ())), preferred_element_...]
    unnamed x199 -> x203, local copies, waits for them, and re-layouts: 31.7 us -> 12.1 us
    concatenate x5 -> x2, local copies, waits for them, and re-layouts: 19.4 us -> 14 us  [the longest x1 14 us: on_device(): jnp.concatenate([w_query, w_key, w_value, w_outgate, w_decay, w_beta, jnp...]
    ppermute x75 -> x72, starting transfers between devices: 81.4 us -> 78.6 us  [hop(): return lax.ppermute(values, axis, [(i, i ^ bit) for i in range(size)])]
  transfers between devices with their start and end apart: 83 -> 79, of which waited for: 44 -> 30; matrix products, arithmetic and copies ran while one was open for 21% -> 12% of each run, Pallas kernels for 34% -> 47%
where the time goes in v3:
time: 818 us; the launch traced here: 806 us
  Pallas kernels  424 us (52%)
  waiting for transfers between devices  172 us (21%)
  starting transfers between devices  78.9 us (10%)
  local copies, waits for them, and re-layouts  60 us (7%)
  other arithmetic  55.1 us (7%)
  between operations  16 us (2%)
    ppermute x72, waiting for transfers between devices, hop(): return lax.ppermute(values, axis, [(i, i ^ bit) for i in range(size)])  166 us
    pallas_call x4, Pallas kernels, ffn_stage(): pl.pallas_call(body, grid=(steps,), in_specs=[anywhere] * (first + len(fi...  112 us
    pallas_call x5, Pallas kernels, weight_gradient(): pl.pallas_call(lambda *refs: wgrad_kernel(count, *refs), grid=(wide // ti...  94.3 us
    pallas_call x2, Pallas kernels, mixer_backward(): pl.pallas_call(body, grid_spec=pltpu.PrefetchScalarGridSpec(num_scalar_pr...  83.4 us
    ppermute x72, starting transfers between devices, hop(): return lax.ppermute(values, axis, [(i, i ^ bit) for i in range(size)])  78.6 us
    pallas_call x4, Pallas kernels, piece_matmul(): pl.pallas_call(lambda *refs: piece_kernel(size, parts, len(pieces), trans...  50.2 us
    pallas_call x4, Pallas kernels, scatter_matmul(): pl.pallas_call(lambda *refs: scatter_kernel(size, where, transposed, *ref...  43.6 us
    pallas_call x2, Pallas kernels, mixer_forward(): pl.pallas_call(body, grid_spec=pltpu.PrefetchScalarGridSpec(num_scalar_pr...  40.3 us
  transfers between devices with their start and end apart: 79, of which 30 were waited for; matrix products, arithmetic and copies ran while one was open for 12% of the time, Pallas kernels for 47%

profile of v3, /device:TPU:0, one launch (start us, length us, event | category | flops | bytes accessed | tf_op | source)
XLA Modules:
  0.0 806.2 jit_solution(3144186263800444837)
XLA Ops:
  8.7 2.0 fusion.16
  11.4 1.9 fusion.14
  13.3 3.0 collective-permute-start.1
  23.3 14.0 %concatenate.88.refs_5_.refs_1_ = bf16[2048,2176]{1,0:T(8,128)(2,1)} concatenate(bf16[2048,512]{1,0:T(8,128)(2,1)} %param.29, bf16[2048,512]{1,0:T(8,128)(2,1)} %param.30, bf16[2048,512]{1,0:T(8,128)(2,1)} %param.31, bf16[2048,512]{1,0:T(8,128)(2,1)} %param.32, bf16[2048,4]{1,0:T(8,128)(2,1)S(1)} %copy.106, bf16[2048,4]{1,0:T(8,128)(2,1)S(1)} %copy.107, ...), dimensions={1} | concatenate | bytes 17825792 | tf_op jit(solution)/shard_map/concatenate | solution.py:969
  37.4 3.2 convert_multiply_fusion.2
  45.5 9.6 %collective-permute-done.2.refs_3_ = bf16[128,2048]{1,0:T(8,128)(2,1)S(1)} collective-permute-done((bf16[128,2048]{1,0:T(8,128)(2,1)S(1)}, bf16[128,2048]{1,0:T(8,128)(2,1)S(1)}, u32[]{:S(2)}, u32[]{:S(2)}) %collective-permute-start.2) | collective-permute-done | bytes 524320 | tf_op jit(solution)/shard_map/ppermute | solution.py:493
  55.1 1.6 collective-permute-done.3.refs_4_
  59.6 16.8 %piece_matmul.4 = (f32[4,256,2176]{2,1,0:T(8,128)}, bf16[4,256,2048]{2,1,0:T(8,128)(2,1)}) custom-call(bf16[256,2048]{1,0:T(8,128)(2,1)} %get-tuple-element.437.refs_0_, bf16[256,2048]{1,0:T(8,128)(2,1)} %collective-permute-done.refs_1_, bf16[256,2048]{1,0:T(8,128)(2,1)} %collective-permute-done.1.refs_2_, bf16[128,2048]{1,0:T(8,128)(2,1)} %copy-done.96, ...), custom_call_target="tpu_custom_call" | custom-call | flops 18253611008 | bytes 30000000 | tf_op jit(solution)/shard_map/piece_matmul/pallas_call | solution.py:826
  76.4 4.2 collective-permute-done.4.refs_1_
  87.3 20.2 %mixer_forward.2 = (bf16[4,2,128,512]{3,2,1,0:T(8,128)(2,1)}, f32[4,2,128,512]{3,2,1,0:T(8,128)}, bf16[4,2,4,128,128]{4,3,2,1,0:T(8,128)(2,1)}, bf16[4,2,128,512...) custom-call(s32[4]{0:T(128)} %iota_xor_fusion.refs_0_, f32[4,2,128,2176]{3,2,1,0:T(8,128)} %bitcast.166, ...), custom_call_target="tpu_custom_call" | custom-call | flops 23520000000 | bytes 8000000 | tf_op jit(solution)/shard_map/mixer_forward/pallas_call | solution.py:393
  107.5 7.4 collective-permute-done.6.refs_3_
  115.5 6.1 scatter_matmul.4
  124.6 17.3 %piece_matmul.5 = (f32[4,256,2176]{2,1,0:T(8,128)}, bf16[4,256,2048]{2,1,0:T(8,128)(2,1)}) custom-call(bf16[256,2048]{1,0:T(8,128)(2,1)} %get-tuple-element.192.refs_0_, bf16[256,2048]{1,0:T(8,128)(2,1)} %copy-done.51, bf16[256,2048]{1,0:T(8,128)(2,1)} %copy-done.52, bf16[128,2048]{1,0:T(8,128)(2,1)} %copy-done.95, ...), custom_call_target="tpu_custom_call" | custom-call | flops 18253611008 | bytes 30000000 | tf_op jit(solution)/shard_map/piece_matmul/pallas_call | solution.py:826
  142.9 1.8 collective-permute-done.11
  154.8 6.5 collective-permute-done.12
  162.1 2.0 multiply_reduce_fusion.5
  168.5 20.2 %mixer_forward.3 = (bf16[4,2,128,512]{3,2,1,0:T(8,128)(2,1)}, f32[4,2,128,512]{3,2,1,0:T(8,128)}, bf16[4,2,4,128,128]{4,3,2,1,0:T(8,128)(2,1)}, bf16[4,2,128,512...) custom-call(s32[4]{0:T(128)} %iota_xor_fusion.refs_0_, f32[4,2,128,2176]{3,2,1,0:T(8,128)} %bitcast.163, ...), custom_call_target="tpu_custom_call" | custom-call | flops 23520000000 | bytes 8000000 | tf_op jit(solution)/shard_map/mixer_forward/pallas_call | solution.py:393
  188.8 6.2 scatter_matmul.5
  197.1 19.9 %collective-permute-done.19 = bf16[256,2048]{1,0:T(8,128)(2,1)S(1)} collective-permute-done((bf16[256,2048]{1,0:T(8,128)(2,1)}, bf16[256,2048]{1,0:T(8,128)(2,1)S(1)}, u32[]{:S(2)}, u32[]{:S(2)}) %collective-permute-start.19) | collective-permute-done | bytes 1048608 | tf_op jit(solution)/shard_map/ppermute | solution.py:493
  224.5 9.0 %collective-permute-done.22 = bf16[128,2048]{1,0:T(8,128)(2,1)S(1)} collective-permute-done((bf16[128,2048]{1,0:T(8,128)(2,1)S(1)}, bf16[128,2048]{1,0:T(8,128)(2,1)S(1)}, u32[]{:S(2)}, u32[]{:S(2)}) %collective-permute-start.22) | collective-permute-done | bytes 524320 | tf_op jit(solution)/shard_map/ppermute | solution.py:493
  235.5 20.1 %collective-permute-done.24.refs_6_ = bf16[256,2048]{1,0:T(8,128)(2,1)S(1)} collective-permute-done((bf16[256,2048]{1,0:T(8,128)(2,1)S(1)}, bf16[256,2048]{1,0:T(8,128)(2,1)S(1)}, u32[]{:S(2)}, u32[]{:S(2)}) %collective-permute-start.24) | collective-permute-done | bytes 1048608 | tf_op jit(solution)/shard_map/ppermute | solution.py:493
  257.7 28.1 %ffn_stage.4 = (bf16[2,256,1408]{2,1,0:T(8,128)(2,1)}, bf16[2,256,1408]{2,1,0:T(8,128)(2,1)}, bf16[2,256,1408]{2,1,0:T(8,128)(2,1)}, bf16[2,256,2048]{2,1,0:T(8,...) custom-call(bf16[256,2048]{1,0:T(8,128)(2,1)} %copy-done.30, ...), custom_call_target="tpu_custom_call" | custom-call | flops 29527900160 | bytes 30000000 | tf_op jit(solution)/shard_map/ffn_stage/pallas_call | solution.py:754
  289.9 27.9 %ffn_stage.5 = (bf16[2,256,1408]{2,1,0:T(8,128)(2,1)}, bf16[2,256,1408]{2,1,0:T(8,128)(2,1)}, bf16[2,256,1408]{2,1,0:T(8,128)(2,1)}, bf16[2,256,2048]{2,1,0:T(8,...) custom-call(bf16[256,2048]{1,0:T(8,128)(2,1)} %copy-done.30, ...), custom_call_target="tpu_custom_call", output_to_operand_aliasing={{5}: (13, {}), {6}: (14, {}), {7}: (15, {}), {8}: (16, {}),... | custom-call | flops 29527900160 | bytes 30000000 | tf_op jit(solution)/shard_map/ffn_stage/pallas_call | solution.py:754
  320.7 12.2 %collective-permute-done.31.refs_4_ = bf16[128,2048]{1,0:T(8,128)(2,1)S(1)} collective-permute-done((bf16[128,2048]{1,0:T(8,128)(2,1)S(1)}, bf16[128,2048]{1,0:T(8,128)(2,1)S(1)}, u32[]{:S(2)}, u32[]{:S(2)}) %collective-permute-start.31) | collective-permute-done | bytes 524320 | tf_op jit(solution)/shard_map/ppermute | solution.py:493
  332.9 1.6 collective-permute-done.30.refs_3_
  336.6 28.1 %ffn_stage.6 = (bf16[2,256,1408]{2,1,0:T(8,128)(2,1)}, bf16[2,256,1408]{2,1,0:T(8,128)(2,1)}, bf16[2,256,1408]{2,1,0:T(8,128)(2,1)}, bf16[2,256,2048]{2,1,0:T(8,...) custom-call(bf16[256,2048]{1,0:T(8,128)(2,1)} %copy-done.31, ...), custom_call_target="tpu_custom_call" | custom-call | flops 29527900160 | bytes 30000000 | tf_op jit(solution)/shard_map/ffn_stage/pallas_call | solution.py:754
  367.3 28.4 %ffn_stage.7 = (bf16[2,256,1408]{2,1,0:T(8,128)(2,1)}, bf16[2,256,1408]{2,1,0:T(8,128)(2,1)}, bf16[2,256,1408]{2,1,0:T(8,128)(2,1)}, bf16[2,256,2048]{2,1,0:T(8,...) custom-call(bf16[256,2048]{1,0:T(8,128)(2,1)} %copy-done.31, ...), custom_call_target="tpu_custom_call", output_to_operand_aliasing={{5}: (13, {}), {6}: (14, {}), {7}: (15, {}), {8}: (16, {}),... | custom-call | flops 29527900160 | bytes 30000000 | tf_op jit(solution)/shard_map/ffn_stage/pallas_call | solution.py:754
  396.4 2.7 multiply_reduce_fusion.1
  399.1 2.0 fusion.33
  401.1 18.9 %weight_gradient.5 = bf16[2048,1408]{1,0:T(8,128)(2,1)} custom-call(bf16[512,2048]{1,0:T(8,128)(2,1)} %bitcast.179, bf16[512,2048]{1,0:T(8,128)(2,1)} %bitcast.181, bf16[512,2048]{1,0:T(8,128)(2,1)} %bitcast.183, bf16[512,2048]{1,0:T(8,128)(2,1)} %bitcast.185, bf16[512,1408]{1,0:T(8,128)(2,1)} %bitcast.195, bf16[512,1408]{1,0:T(8,128)(2,1)} %bitcast.196, ...), custom_call_target="tpu_custom_call" | custom-call | flops 17716740096 | bytes 20000000 | tf_op jit(solution)/shard_map/weight_gradient/pallas_call | solution.py:870
  424.2 22.0 %collective-permute-done.40.refs_1_ = bf16[256,2048]{1,0:T(8,128)(2,1)S(1)} collective-permute-done((bf16[256,2048]{1,0:T(8,128)(2,1)S(1)}, bf16[256,2048]{1,0:T(8,128)(2,1)S(1)}, u32[]{:S(2)}, u32[]{:S(2)}) %collective-permute-start.40) | collective-permute-done | bytes 1048608 | tf_op jit(solution)/shard_map/ppermute | solution.py:493
  450.0 10.2 %collective-permute-done.36 = bf16[256,2048]{1,0:T(8,128)(2,1)S(1)} collective-permute-done((bf16[256,2048]{1,0:T(8,128)(2,1)}, bf16[256,2048]{1,0:T(8,128)(2,1)S(1)}, u32[]{:S(2)}, u32[]{:S(2)}) %collective-permute-start.36) | collective-permute-done | bytes 1048608 | tf_op jit(solution)/shard_map/ppermute | solution.py:493
  464.2 18.6 %weight_gradient.6 = bf16[2048,1408]{1,0:T(8,128)(2,1)} custom-call(bf16[512,2048]{1,0:T(8,128)(2,1)} %bitcast.180, bf16[512,2048]{1,0:T(8,128)(2,1)} %bitcast.182, bf16[512,2048]{1,0:T(8,128)(2,1)} %bitcast.184, bf16[512,2048]{1,0:T(8,128)(2,1)} %bitcast.186, bf16[512,1408]{1,0:T(8,128)(2,1)} %bitcast.193, bf16[512,1408]{1,0:T(8,128)(2,1)} %bitcast.194, ...), custom_call_target="tpu_custom_call" | custom-call | flops 17716740096 | bytes 20000000 | tf_op jit(solution)/shard_map/weight_gradient/pallas_call | solution.py:870
  485.2 2.2 convert_add_fusion.4
  489.0 2.0 fusion.31
  495.0 8.2 %piece_matmul.6 = (f32[4,256,512]{2,1,0:T(8,128)}, bf16[4,256,2048]{2,1,0:T(8,128)(2,1)}) custom-call(bf16[256,2048]{1,0:T(8,128)(2,1)} %copy-done.28, bf16[256,2048]{1,0:T(8,128)(2,1)} %copy-done.49, bf16[256,2048]{1,0:T(8,128)(2,1)} %copy-done.50, bf16[128,2048]{1,0:T(8,128)(2,1)} %collective-permute-done.42.refs_3_, ...), custom_call_target="tpu_custom_call" | custom-call | flops 4294967296 | bytes 30000000 | tf_op jit(solution)/shard_map/piece_matmul/pallas_call | solution.py:826
  503.2 41.5 %mixer_backward.2 = (bf16[4,2,128,2176]{3,2,1,0:T(8,128)(2,1)}, f32[96,512]{1,0:T(8,128)}, f32[8,128]{1,0:T(8,128)}, f32[8,512]{1,0:T(8,128)}) custom-call(s32[4]{0:T(128)} %iota_xor_fusion.refs_0_, f32[4,2,128,2176]{3,2,1,0:T(8,128)} %bitcast.167, f32[4,2,128,2176]{3,2,1,0:T(8,128)} %bitcast.168, f32[2,4,128,16]{3,2,1,0:T(8,128)} %bitcast.147, ...), custom_call_target="tpu_custom_call" | custom-call | flops 52800000000 | bytes 12000000 | tf_op jit(solution)/shard_map/mixer_backward/pallas_call | solution.py:446
  544.8 2.0 slice.529
  548.1 1.9 slice.528
  553.9 15.7 %scatter_matmul.6 = (bf16[256,2048]{1,0:T(8,128)(2,1)}, bf16[256,2048]{1,0:T(8,128)(2,1)}, bf16[512,2048]{1,0:T(8,128)(2,1)}) custom-call(bf16[1024,2176]{1,0:T(8,128)(2,1)} %bitcast.169, bf16[2048,2176]{1,0:T(8,128)(2,1)} %concatenate.88.refs_5_.refs_1_), custom_call_target="tpu_custom_call" | custom-call | flops 18253611008 | bytes 15000000 | tf_op jit(solution)/shard_map/scatter_matmul/pallas_call | solution.py:611
  573.1 7.9 piece_matmul.7
  581.0 18.5 %weight_gradient.7.refs_4_ = bf16[2048,1408]{1,0:T(8,128)(2,1)} custom-call(bf16[512,2048]{1,0:T(8,128)(2,1)} %bitcast.175, bf16[512,2048]{1,0:T(8,128)(2,1)} %bitcast.176, bf16[512,2048]{1,0:T(8,128)(2,1)} %bitcast.177, bf16[512,2048]{1,0:T(8,128)(2,1)} %bitcast.178, bf16[512,1408]{1,0:T(8,128)(2,1)} %bitcast.189, bf16[512,1408]{1,0:T(8,128)(2,1)} %bitcast.190, ...), custom_call_target="tpu_custom_call" | custom-call | flops 17716740096 | bytes 20000000 | tf_op jit(solution)/shard_map/weight_gradient/pallas_call | solution.py:870
  599.5 12.0 %weight_gradient.8 = bf16[2048,1920]{1,0:T(8,128)(2,1)} custom-call(bf16[1024,2048]{1,0:T(8,128)(2,1)} %bitcast.136, bf16[1024,2048]{1,0:T(8,128)(2,1)} %bitcast.137, bf16[1024,512]{1,0:T(8,128)(2,1)} %bitcast.143, bf16[1024,512]{1,0:T(8,128)(2,1)} %bitcast.145, bf16[2048,1408]{1,0:T(8,128)(2,1)} %weight_gradient.7.refs_4_), custom_call_target="tpu_custom_call" | custom-call | flops 6442450944 | bytes 20000000 | tf_op jit(solution)/shard_map/weight_gradient/pallas_call | solution.py:870
  614.3 41.9 %mixer_backward.3 = (bf16[4,2,128,2176]{3,2,1,0:T(8,128)(2,1)}, f32[96,512]{1,0:T(8,128)}, f32[8,128]{1,0:T(8,128)}, f32[8,512]{1,0:T(8,128)}) custom-call(s32[4]{0:T(128)} %iota_xor_fusion.refs_0_, f32[4,2,128,2176]{3,2,1,0:T(8,128)} %bitcast.164, f32[4,2,128,2176]{3,2,1,0:T(8,128)} %bitcast.165, f32[2,4,128,16]{3,2,1,0:T(8,128)} %bitcast.149, ...), custom_call_target="tpu_custom_call" | custom-call | flops 52800000000 | bytes 12000000 | tf_op jit(solution)/shard_map/mixer_backward/pallas_call | solution.py:446
  656.2 26.3 %weight_gradient.9 = bf16[2048,2176]{1,0:T(8,128)(2,1)} custom-call(bf16[1024,2048]{1,0:T(8,128)(2,1)} %bitcast.173, bf16[1024,2048]{1,0:T(8,128)(2,1)} %bitcast.174, bf16[1024,2176]{1,0:T(8,128)(2,1)} %bitcast.170, bf16[1024,2176]{1,0:T(8,128)(2,1)} %bitcast.171), custom_call_target="tpu_custom_call" | custom-call | flops 27380416512 | bytes 20000000 | tf_op jit(solution)/shard_map/weight_gradient/pallas_call | solution.py:870
  684.9 2.6 add_convert_fusion.5
  689.9 15.6 %scatter_matmul.7 = (bf16[256,2048]{1,0:T(8,128)(2,1)}, bf16[256,2048]{1,0:T(8,128)(2,1)}, bf16[512,2048]{1,0:T(8,128)(2,1)}) custom-call(bf16[1024,2176]{1,0:T(8,128)(2,1)} %bitcast.172, bf16[2048,2176]{1,0:T(8,128)(2,1)} %concatenate.88.refs_5_.refs_1_), custom_call_target="tpu_custom_call" | custom-call | flops 18253611008 | bytes 15000000 | tf_op jit(solution)/shard_map/scatter_matmul/pallas_call | solution.py:611
  711.1 3.0 convert_add_fusion.1
  714.1 3.5 collective-permute-done.56
  718.4 1.6 add_convert_fusion
  722.6 12.2 %collective-permute-done.61 = bf16[256,2048]{1,0:T(8,128)(2,1)S(1)} collective-permute-done((bf16[256,2048]{1,0:T(8,128)(2,1)S(1)}, bf16[256,2048]{1,0:T(8,128)(2,1)S(1)}, u32[]{:S(2)}, u32[]{:S(2)}) %collective-permute-start.61) | collective-permute-done | bytes 1048608 | tf_op jit(solution)/shard_map/ppermute | solution.py:493
  740.3 2.4 collective-permute-start.70
  742.7 3.5 collective-permute-done.70
  746.2 3.8 collective-permute-start.71
  750.0 3.8 collective-permute-done.71
  757.9 3.1 fusion.15
  763.0 4.1 collective-permute-done.65
  767.2 1.7 collective-permute-start.66
  769.0 3.9 collective-permute-done.66
  773.4 3.6 fusion.3
  781.5 2.3 convert_element_type.429
  783.8 2.3 convert_element_type.430
  789.8 4.4 reduce-scatter.5.cloned.1.call-done
  796.5 2.6 fusion.36
  (467 shorter events, 136.2 us)
Async XLA Ops:
  7.2 250.5 %all-gather.4.cloned.1.call-start = ((), (), s32[]{:S(2)}) async-start(), calls=%async_computation.4 | async-start | bytes 6488064 | tf_op jit(solution)/shard_map/all_gather | solution.py:952
  7.9 249.7 %all-gather.6.cloned.1.call-start = ((), (), s32[]{:S(2)}) async-start(), calls=%async_computation.5 | async-start | bytes 6488064 | tf_op jit(solution)/shard_map/all_gather | solution.py:953
  8.7 249.0 %all-gather.8.cloned.1.call-start = ((), (), s32[]{:S(2)}) async-start(), calls=%async_computation.6 | async-start | bytes 6488064 | tf_op jit(solution)/shard_map/all_gather | solution.py:954
  13.3 27.3 %collective-permute-start.1 = (bf16[256,2048]{1,0:T(8,128)(2,1)}, bf16[256,2048]{1,0:T(8,128)(2,1)}, u32[]{:S(2)}, u32[]{:S(2)}) collective-permute-start(bf16[256,2048]{1,0:T(8,128)(2,1)} %get-tuple-element.437.refs_0_), channel_id=1, source_target_pairs={{0,2},{1,3},{2,0},{3,1},{4,6},{5,7},{6,4},{7,5},{8,10},{9,11},{10,... | collective-permute-start | bytes 3145736 | tf_op jit(solution)/shard_map/ppermute | solution.py:493
  16.3 26.6 %collective-permute-start = (bf16[256,2048]{1,0:T(8,128)(2,1)}, bf16[256,2048]{1,0:T(8,128)(2,1)}, u32[]{:S(2)}, u32[]{:S(2)}) collective-permute-start(bf16[256,2048]{1,0:T(8,128)(2,1)} %get-tuple-element.437.refs_0_), channel_id=1, source_target_pairs={{0,1},{1,0},{2,3},{3,2},{4,5},{5,4},{6,7},{7,6},{8,9},{9,8},{10,11... | collective-permute-start | bytes 3145736 | tf_op jit(solution)/shard_map/ppermute | solution.py:493
  17.8 763.6 %reduce-scatter.9.cloned.1.call-start = ((), (), s32[]{:S(2)}) async-start(), calls=%async_computation.9 | async-start | bytes 6488064 | tf_op jit(solution)/shard_map/reduce_scatter | solution.py:1039
  57.5 23.1 %collective-permute-start.4 = (bf16[256,2048]{1,0:T(8,128)(2,1)S(1)}, bf16[256,2048]{1,0:T(8,128)(2,1)S(1)}, u32[]{:S(2)}, u32[]{:S(2)}) collective-permute-start(bf16[256,2048]{1,0:T(8,128)(2,1)S(1)} %copy-done.40), channel_id=1, source_target_pairs={{0,1},{1,0},{2,3},{3,2},{4,5},{5,4},{6,7},{7,6},{8,9},{9,8},{10,11... | collective-permute-start | bytes 3145736 | tf_op jit(solution)/shard_map/ppermute | solution.py:493
  58.8 23.0 %collective-permute-start.5 = (bf16[256,2048]{1,0:T(8,128)(2,1)S(1)}, bf16[256,2048]{1,0:T(8,128)(2,1)S(1)}, u32[]{:S(2)}, u32[]{:S(2)}) collective-permute-start(bf16[256,2048]{1,0:T(8,128)(2,1)S(1)} %copy-done.40), channel_id=1, source_target_pairs={{0,2},{1,3},{2,0},{3,1},{4,6},{5,7},{6,4},{7,5},{8,10},{9,11},{10,... | collective-permute-start | bytes 3145736 | tf_op jit(solution)/shard_map/ppermute | solution.py:493
  81.8 41.8 %collective-permute-start.8 = (bf16[256,2048]{1,0:T(8,128)(2,1)S(1)}, bf16[256,2048]{1,0:T(8,128)(2,1)S(1)}, u32[]{:S(2)}, u32[]{:S(2)}) collective-permute-start(bf16[256,2048]{1,0:T(8,128)(2,1)S(1)} %bitcast_convert_fusion.1.refs_5_), channel_id=1, source_target_pairs={{0,1},{1,0},{2,3},{3,2},{4,5},{5,4},{6,7},{7,6},{8,9},{9,8},{10,11... | collective-permute-start | bytes 3145736 | tf_op jit(solution)/shard_map/ppermute | solution.py:493
  82.3 41.3 %collective-permute-start.9 = (bf16[256,2048]{1,0:T(8,128)(2,1)S(1)}, bf16[256,2048]{1,0:T(8,128)(2,1)}, u32[]{:S(2)}, u32[]{:S(2)}) collective-permute-start(bf16[256,2048]{1,0:T(8,128)(2,1)S(1)} %bitcast_convert_fusion.1.refs_5_), channel_id=1, source_target_pairs={{0,2},{1,3},{2,0},{3,1},{4,6},{5,7},{6,4},{7,5},{8,10},{9,11},{10,... | collective-permute-start | bytes 3145736 | tf_op jit(solution)/shard_map/ppermute | solution.py:493
  83.4 31.5 %collective-permute-start.6 = (bf16[128,2048]{1,0:T(8,128)(2,1)S(1)}, bf16[128,2048]{1,0:T(8,128)(2,1)S(1)}, u32[]{:S(2)}, u32[]{:S(2)}) collective-permute-start(bf16[128,2048]{1,0:T(8,128)(2,1)S(1)} %slice.494), channel_id=1, source_target_pairs={{0,1},{1,0},{2,3},{3,2},{4,5},{5,4},{6,7},{7,6},{8,9},{9,8},{10,11... | collective-permute-start | bytes 1572872 | tf_op jit(solution)/shard_map/ppermute | solution.py:493
  84.6 30.8 %collective-permute-start.7 = (bf16[128,2048]{1,0:T(8,128)(2,1)S(1)}, bf16[128,2048]{1,0:T(8,128)(2,1)}, u32[]{:S(2)}, u32[]{:S(2)}) collective-permute-start(bf16[128,2048]{1,0:T(8,128)(2,1)S(1)} %slice.495), channel_id=1, source_target_pairs={{0,2},{1,3},{2,0},{3,1},{4,6},{5,7},{6,4},{7,5},{8,10},{9,11},{10,... | collective-permute-start | bytes 1572872 | tf_op jit(solution)/shard_map/ppermute | solution.py:493
  121.6 21.3 %collective-permute-start.10 = (bf16[256,2048]{1,0:T(8,128)(2,1)}, bf16[256,2048]{1,0:T(8,128)(2,1)S(1)}, u32[]{:S(2)}, u32[]{:S(2)}) collective-permute-start(bf16[256,2048]{1,0:T(8,128)(2,1)} %get-tuple-element.189), channel_id=1, source_target_pairs={{0,1},{1,0},{2,3},{3,2},{4,5},{5,4},{6,7},{7,6},{8,9},{9,8},{10,11... | collective-permute-start | bytes 3145736 | tf_op jit(solution)/shard_map/ppermute | solution.py:493
  122.9 21.8 %collective-permute-start.11 = (bf16[256,2048]{1,0:T(8,128)(2,1)}, bf16[256,2048]{1,0:T(8,128)(2,1)S(1)}, u32[]{:S(2)}, u32[]{:S(2)}) collective-permute-start(bf16[256,2048]{1,0:T(8,128)(2,1)} %get-tuple-element.190), channel_id=1, source_target_pairs={{0,2},{1,3},{2,0},{3,1},{4,6},{5,7},{6,4},{7,5},{8,10},{9,11},{10,... | collective-permute-start | bytes 3145736 | tf_op jit(solution)/shard_map/ppermute | solution.py:493
  146.0 15.2 %collective-permute-start.12 = (bf16[128,2048]{1,0:T(8,128)(2,1)}, bf16[128,2048]{1,0:T(8,128)(2,1)}, u32[]{:S(2)}, u32[]{:S(2)}) collective-permute-start(bf16[128,2048]{1,0:T(8,128)(2,1)} %get-tuple-element.455), channel_id=1, source_target_pairs={{0,2},{1,3},{2,0},{3,1},{4,6},{5,7},{6,4},{7,5},{8,10},{9,11},{10,... | collective-permute-start | bytes 1572872 | tf_op jit(solution)/shard_map/ppermute | solution.py:493
  146.9 15.2 %collective-permute-start.13 = (bf16[128,2048]{1,0:T(8,128)(2,1)}, bf16[128,2048]{1,0:T(8,128)(2,1)}, u32[]{:S(2)}, u32[]{:S(2)}) collective-permute-start(bf16[128,2048]{1,0:T(8,128)(2,1)} %get-tuple-element.456), channel_id=1, source_target_pairs={{0,1},{1,0},{2,3},{3,2},{4,5},{5,4},{6,7},{7,6},{8,9},{9,8},{10,11... | collective-permute-start | bytes 1572872 | tf_op jit(solution)/shard_map/ppermute | solution.py:493
  149.8 38.9 %collective-permute-start.15 = (bf16[128,2048]{1,0:T(8,128)(2,1)S(1)}, bf16[128,2048]{1,0:T(8,128)(2,1)S(1)}, u32[]{:S(2)}, u32[]{:S(2)}) collective-permute-start(bf16[128,2048]{1,0:T(8,128)(2,1)S(1)} %slice.503), channel_id=1, source_target_pairs={{0,2},{1,3},{2,0},{3,1},{4,6},{5,7},{6,4},{7,5},{8,10},{9,11},{10,... | collective-permute-start | bytes 1572872 | tf_op jit(solution)/shard_map/ppermute | solution.py:493
  152.5 36.3 %collective-permute-start.14 = (bf16[128,2048]{1,0:T(8,128)(2,1)S(1)}, bf16[128,2048]{1,0:T(8,128)(2,1)}, u32[]{:S(2)}, u32[]{:S(2)}) collective-permute-start(bf16[128,2048]{1,0:T(8,128)(2,1)S(1)} %slice.502), channel_id=1, source_target_pairs={{0,1},{1,0},{2,3},{3,2},{4,5},{5,4},{6,7},{7,6},{8,9},{9,8},{10,11... | collective-permute-start | bytes 1572872 | tf_op jit(solution)/shard_map/ppermute | solution.py:493
  165.8 29.2 %collective-permute-start.16 = (bf16[256,2048]{1,0:T(8,128)(2,1)S(1)}, bf16[256,2048]{1,0:T(8,128)(2,1)S(1)}, u32[]{:S(2)}, u32[]{:S(2)}) collective-permute-start(bf16[256,2048]{1,0:T(8,128)(2,1)S(1)} %multiply_convert_fusion.1.refs_0_), channel_id=1, source_target_pairs={{0,1},{1,0},{2,3},{3,2},{4,5},{5,4},{6,7},{7,6},{8,9},{9,8},{10,11... | collective-permute-start | bytes 3145736 | tf_op jit(solution)/shard_map/ppermute | solution.py:493
  166.4 28.6 %collective-permute-start.17 = (bf16[256,2048]{1,0:T(8,128)(2,1)S(1)}, bf16[256,2048]{1,0:T(8,128)(2,1)S(1)}, u32[]{:S(2)}, u32[]{:S(2)}) collective-permute-start(bf16[256,2048]{1,0:T(8,128)(2,1)S(1)} %multiply_convert_fusion.1.refs_0_), channel_id=1, source_target_pairs={{0,2},{1,3},{2,0},{3,1},{4,6},{5,7},{6,4},{7,5},{8,10},{9,11},{10,... | collective-permute-start | bytes 3145736 | tf_op jit(solution)/shard_map/ppermute | solution.py:493
  195.1 21.9 %collective-permute-start.19 = (bf16[256,2048]{1,0:T(8,128)(2,1)}, bf16[256,2048]{1,0:T(8,128)(2,1)S(1)}, u32[]{:S(2)}, u32[]{:S(2)}) collective-permute-start(bf16[256,2048]{1,0:T(8,128)(2,1)} %get-tuple-element.203), channel_id=1, source_target_pairs={{0,2},{1,3},{2,0},{3,1},{4,6},{5,7},{6,4},{7,5},{8,10},{9,11},{10,... | collective-permute-start | bytes 3145736 | tf_op jit(solution)/shard_map/ppermute | solution.py:493
  195.6 21.4 %collective-permute-start.18 = (bf16[256,2048]{1,0:T(8,128)(2,1)}, bf16[256,2048]{1,0:T(8,128)(2,1)S(1)}, u32[]{:S(2)}, u32[]{:S(2)}) collective-permute-start(bf16[256,2048]{1,0:T(8,128)(2,1)} %get-tuple-element.201), channel_id=1, source_target_pairs={{0,1},{1,0},{2,3},{3,2},{4,5},{5,4},{6,7},{7,6},{8,9},{9,8},{10,11... | collective-permute-start | bytes 3145736 | tf_op jit(solution)/shard_map/ppermute | solution.py:493
  218.6 14.9 %collective-permute-start.22 = (bf16[128,2048]{1,0:T(8,128)(2,1)S(1)}, bf16[128,2048]{1,0:T(8,128)(2,1)S(1)}, u32[]{:S(2)}, u32[]{:S(2)}) collective-permute-start(bf16[128,2048]{1,0:T(8,128)(2,1)S(1)} %get-tuple-element.453), channel_id=1, source_target_pairs={{0,2},{1,3},{2,0},{3,1},{4,6},{5,7},{6,4},{7,5},{8,10},{9,11},{10,... | collective-permute-start | bytes 1572872 | tf_op jit(solution)/shard_map/ppermute | solution.py:493
  220.7 35.1 %collective-permute-start.21 = (bf16[128,2048]{1,0:T(8,128)(2,1)S(1)}, bf16[128,2048]{1,0:T(8,128)(2,1)S(1)}, u32[]{:S(2)}, u32[]{:S(2)}) collective-permute-start(bf16[128,2048]{1,0:T(8,128)(2,1)S(1)} %slice.505), channel_id=1, source_target_pairs={{0,2},{1,3},{2,0},{3,1},{4,6},{5,7},{6,4},{7,5},{8,10},{9,11},{10,... | collective-permute-start | bytes 1572872 | tf_op jit(solution)/shard_map/ppermute | solution.py:493
  222.3 35.4 %collective-permute-start.20 = (bf16[128,2048]{1,0:T(8,128)(2,1)S(1)}, bf16[128,2048]{1,0:T(8,128)(2,1)}, u32[]{:S(2)}, u32[]{:S(2)}) collective-permute-start(bf16[128,2048]{1,0:T(8,128)(2,1)S(1)} %slice.504), channel_id=1, source_target_pairs={{0,1},{1,0},{2,3},{3,2},{4,5},{5,4},{6,7},{7,6},{8,9},{9,8},{10,11... | collective-permute-start | bytes 1572872 | tf_op jit(solution)/shard_map/ppermute | solution.py:493
  223.1 32.5 %collective-permute-start.24 = (bf16[256,2048]{1,0:T(8,128)(2,1)S(1)}, bf16[256,2048]{1,0:T(8,128)(2,1)S(1)}, u32[]{:S(2)}, u32[]{:S(2)}) collective-permute-start(bf16[256,2048]{1,0:T(8,128)(2,1)S(1)} %bitcast_convert_fusion.refs_5_), channel_id=1, source_target_pairs={{0,1},{1,0},{2,3},{3,2},{4,5},{5,4},{6,7},{7,6},{8,9},{9,8},{10,11... | collective-permute-start | bytes 3145736 | tf_op jit(solution)/shard_map/ppermute | solution.py:493
  233.5 22.3 %collective-permute-start.25 = (bf16[256,2048]{1,0:T(8,128)(2,1)S(1)}, bf16[256,2048]{1,0:T(8,128)(2,1)S(1)}, u32[]{:S(2)}, u32[]{:S(2)}) collective-permute-start(bf16[256,2048]{1,0:T(8,128)(2,1)S(1)} %bitcast_convert_fusion.refs_5_), channel_id=1, source_target_pairs={{0,2},{1,3},{2,0},{3,1},{4,6},{5,7},{6,4},{7,5},{8,10},{9,11},{10,... | collective-permute-start | bytes 3145736 | tf_op jit(solution)/shard_map/ppermute | solution.py:493
  285.8 32.0 %collective-permute-start.26 = (bf16[256,2048]{1,0:T(8,128)(2,1)S(1)}, bf16[256,2048]{1,0:T(8,128)(2,1)S(1)}, u32[]{:S(2)}, u32[]{:S(2)}) collective-permute-start(bf16[256,2048]{1,0:T(8,128)(2,1)S(1)} %multiply_convert_fusion.refs_0_), channel_id=1, source_target_pairs={{0,1},{1,0},{2,3},{3,2},{4,5},{5,4},{6,7},{7,6},{8,9},{9,8},{10,11... | collective-permute-start | bytes 3145736 | tf_op jit(solution)/shard_map/ppermute | solution.py:493
  287.3 32.2 %collective-permute-start.27 = (bf16[256,2048]{1,0:T(8,128)(2,1)S(1)}, bf16[256,2048]{1,0:T(8,128)(2,1)S(1)}, u32[]{:S(2)}, u32[]{:S(2)}) collective-permute-start(bf16[256,2048]{1,0:T(8,128)(2,1)S(1)} %multiply_convert_fusion.refs_0_), channel_id=1, source_target_pairs={{0,2},{1,3},{2,0},{3,1},{4,6},{5,7},{6,4},{7,5},{8,10},{9,11},{10,... | collective-permute-start | bytes 3145736 | tf_op jit(solution)/shard_map/ppermute | solution.py:493
  288.4 29.5 %collective-permute-start.29 = (bf16[128,2048]{1,0:T(8,128)(2,1)S(1)}, bf16[128,2048]{1,0:T(8,128)(2,1)S(1)}, u32[]{:S(2)}, u32[]{:S(2)}) collective-permute-start(bf16[128,2048]{1,0:T(8,128)(2,1)S(1)} %slice.512), channel_id=1, source_target_pairs={{0,2},{1,3},{2,0},{3,1},{4,6},{5,7},{6,4},{7,5},{8,10},{9,11},{10,... | collective-permute-start | bytes 1572872 | tf_op jit(solution)/shard_map/ppermute | solution.py:493
  289.3 28.6 %collective-permute-start.28 = (bf16[128,2048]{1,0:T(8,128)(2,1)S(1)}, bf16[128,2048]{1,0:T(8,128)(2,1)S(1)}, u32[]{:S(2)}, u32[]{:S(2)}) collective-permute-start(bf16[128,2048]{1,0:T(8,128)(2,1)S(1)} %slice.511), channel_id=1, source_target_pairs={{0,1},{1,0},{2,3},{3,2},{4,5},{5,4},{6,7},{7,6},{8,9},{9,8},{10,11... | collective-permute-start | bytes 1572872 | tf_op jit(solution)/shard_map/ppermute | solution.py:493
  317.9 14.9 %collective-permute-start.31 = (bf16[128,2048]{1,0:T(8,128)(2,1)S(1)}, bf16[128,2048]{1,0:T(8,128)(2,1)S(1)}, u32[]{:S(2)}, u32[]{:S(2)}) collective-permute-start(bf16[128,2048]{1,0:T(8,128)(2,1)S(1)} %slice.513), channel_id=1, source_target_pairs={{0,2},{1,3},{2,0},{3,1},{4,6},{5,7},{6,4},{7,5},{8,10},{9,11},{10,... | collective-permute-start | bytes 1572872 | tf_op jit(solution)/shard_map/ppermute | solution.py:493
  319.6 14.9 %collective-permute-start.30 = (bf16[128,2048]{1,0:T(8,128)(2,1)S(1)}, bf16[128,2048]{1,0:T(8,128)(2,1)S(1)}, u32[]{:S(2)}, u32[]{:S(2)}) collective-permute-start(bf16[128,2048]{1,0:T(8,128)(2,1)S(1)} %slice.510), channel_id=1, source_target_pairs={{0,1},{1,0},{2,3},{3,2},{4,5},{5,4},{6,7},{7,6},{8,9},{9,8},{10,11... | collective-permute-start | bytes 1572872 | tf_op jit(solution)/shard_map/ppermute | solution.py:493
  334.5 30.2 %collective-permute-start.33 = (bf16[256,2048]{1,0:T(8,128)(2,1)}, bf16[256,2048]{1,0:T(8,128)(2,1)S(1)}, u32[]{:S(2)}, u32[]{:S(2)}) collective-permute-start(bf16[256,2048]{1,0:T(8,128)(2,1)} %get-tuple-element.231), channel_id=1, source_target_pairs={{0,2},{1,3},{2,0},{3,1},{4,6},{5,7},{6,4},{7,5},{8,10},{9,11},{10,... | collective-permute-start | bytes 3145736 | tf_op jit(solution)/shard_map/ppermute | solution.py:493
  335.1 29.6 %collective-permute-start.32 = (bf16[256,2048]{1,0:T(8,128)(2,1)}, bf16[256,2048]{1,0:T(8,128)(2,1)S(1)}, u32[]{:S(2)}, u32[]{:S(2)}) collective-permute-start(bf16[256,2048]{1,0:T(8,128)(2,1)} %get-tuple-element.229), channel_id=1, source_target_pairs={{0,1},{1,0},{2,3},{3,2},{4,5},{5,4},{6,7},{7,6},{8,9},{9,8},{10,11... | collective-permute-start | bytes 3145736 | tf_op jit(solution)/shard_map/ppermute | solution.py:493
  365.1 30.7 %collective-permute-start.34 = (bf16[128,2048]{1,0:T(8,128)(2,1)S(1)}, bf16[128,2048]{1,0:T(8,128)(2,1)S(1)}, u32[]{:S(2)}, u32[]{:S(2)}) collective-permute-start(bf16[128,2048]{1,0:T(8,128)(2,1)S(1)} %get-tuple-element.449), channel_id=1, source_target_pairs={{0,2},{1,3},{2,0},{3,1},{4,6},{5,7},{6,4},{7,5},{8,10},{9,11},{10,... | collective-permute-start | bytes 1572872 | tf_op jit(solution)/shard_map/ppermute | solution.py:493
  366.3 29.5 %collective-permute-start.35 = (bf16[128,2048]{1,0:T(8,128)(2,1)S(1)}, bf16[128,2048]{1,0:T(8,128)(2,1)}, u32[]{:S(2)}, u32[]{:S(2)}) collective-permute-start(bf16[128,2048]{1,0:T(8,128)(2,1)S(1)} %get-tuple-element.450), channel_id=1, source_target_pairs={{0,1},{1,0},{2,3},{3,2},{4,5},{5,4},{6,7},{7,6},{8,9},{9,8},{10,11... | collective-permute-start | bytes 1572872 | tf_op jit(solution)/shard_map/ppermute | solution.py:493
  420.0 363.8 %reduce-scatter.11.cloned.1.call-start = ((), (), s32[]{:S(2)}) async-start(), calls=%async_computation.10 | async-start | bytes 6488064 | tf_op jit(solution)/shard_map/reduce_scatter | solution.py:1039
  420.1 26.2 %collective-permute-start.40 = (bf16[256,2048]{1,0:T(8,128)(2,1)S(1)}, bf16[256,2048]{1,0:T(8,128)(2,1)S(1)}, u32[]{:S(2)}, u32[]{:S(2)}) collective-permute-start(bf16[256,2048]{1,0:T(8,128)(2,1)S(1)} %get-tuple-element.260.refs_0_), channel_id=1, source_target_pairs={{0,1},{1,0},{2,3},{3,2},{4,5},{5,4},{6,7},{7,6},{8,9},{9,8},{10,11... | collective-permute-start | bytes 3145736 | tf_op jit(solution)/shard_map/ppermute | solution.py:493
  421.2 26.5 %collective-permute-start.41 = (bf16[256,2048]{1,0:T(8,128)(2,1)S(1)}, bf16[256,2048]{1,0:T(8,128)(2,1)S(1)}, u32[]{:S(2)}, u32[]{:S(2)}) collective-permute-start(bf16[256,2048]{1,0:T(8,128)(2,1)S(1)} %get-tuple-element.260.refs_0_), channel_id=1, source_target_pairs={{0,2},{1,3},{2,0},{3,1},{4,6},{5,7},{6,4},{7,5},{8,10},{9,11},{10,... | collective-permute-start | bytes 3145736 | tf_op jit(solution)/shard_map/ppermute | solution.py:493
  422.1 38.1 %collective-permute-start.36 = (bf16[256,2048]{1,0:T(8,128)(2,1)}, bf16[256,2048]{1,0:T(8,128)(2,1)S(1)}, u32[]{:S(2)}, u32[]{:S(2)}) collective-permute-start(bf16[256,2048]{1,0:T(8,128)(2,1)} %get-tuple-element.251), channel_id=1, source_target_pairs={{0,1},{1,0},{2,3},{3,2},{4,5},{5,4},{6,7},{7,6},{8,9},{9,8},{10,11... | collective-permute-start | bytes 3145736 | tf_op jit(solution)/shard_map/ppermute | solution.py:493
  422.6 38.4 %collective-permute-start.37 = (bf16[256,2048]{1,0:T(8,128)(2,1)}, bf16[256,2048]{1,0:T(8,128)(2,1)S(1)}, u32[]{:S(2)}, u32[]{:S(2)}) collective-permute-start(bf16[256,2048]{1,0:T(8,128)(2,1)} %get-tuple-element.253), channel_id=1, source_target_pairs={{0,2},{1,3},{2,0},{3,1},{4,6},{5,7},{6,4},{7,5},{8,10},{9,11},{10,... | collective-permute-start | bytes 3145736 | tf_op jit(solution)/shard_map/ppermute | solution.py:493
  447.2 47.1 %collective-permute-start.43 = (bf16[128,2048]{1,0:T(8,128)(2,1)}, bf16[128,2048]{1,0:T(8,128)(2,1)}, u32[]{:S(2)}, u32[]{:S(2)}) collective-permute-start(bf16[128,2048]{1,0:T(8,128)(2,1)} %slice.523), channel_id=1, source_target_pairs={{0,2},{1,3},{2,0},{3,1},{4,6},{5,7},{6,4},{7,5},{8,10},{9,11},{10,... | collective-permute-start | bytes 1572872 | tf_op jit(solution)/shard_map/ppermute | solution.py:493
  448.5 46.5 %collective-permute-start.42 = (bf16[128,2048]{1,0:T(8,128)(2,1)}, bf16[128,2048]{1,0:T(8,128)(2,1)}, u32[]{:S(2)}, u32[]{:S(2)}) collective-permute-start(bf16[128,2048]{1,0:T(8,128)(2,1)} %slice.522), channel_id=1, source_target_pairs={{0,1},{1,0},{2,3},{3,2},{4,5},{5,4},{6,7},{7,6},{8,9},{9,8},{10,11... | collective-permute-start | bytes 1572872 | tf_op jit(solution)/shard_map/ppermute | solution.py:493
  462.5 22.7 %collective-permute-start.38 = (bf16[128,2048]{1,0:T(8,128)(2,1)}, bf16[128,2048]{1,0:T(8,128)(2,1)}, u32[]{:S(2)}, u32[]{:S(2)}) collective-permute-start(bf16[128,2048]{1,0:T(8,128)(2,1)} %get-tuple-element.447), channel_id=1, source_target_pairs={{0,2},{1,3},{2,0},{3,1},{4,6},{5,7},{6,4},{7,5},{8,10},{9,11},{10,... | collective-permute-start | bytes 1572872 | tf_op jit(solution)/shard_map/ppermute | solution.py:493
  463.4 21.8 %collective-permute-start.39 = (bf16[128,2048]{1,0:T(8,128)(2,1)}, bf16[128,2048]{1,0:T(8,128)(2,1)}, u32[]{:S(2)}, u32[]{:S(2)}) collective-permute-start(bf16[128,2048]{1,0:T(8,128)(2,1)} %get-tuple-element.448), channel_id=1, source_target_pairs={{0,1},{1,0},{2,3},{3,2},{4,5},{5,4},{6,7},{7,6},{8,9},{9,8},{10,11... | collective-permute-start | bytes 1572872 | tf_op jit(solution)/shard_map/ppermute | solution.py:493
  482.8 303.3 %reduce-scatter.7.cloned.1.call-start = ((), (), s32[]{:S(2)}) async-start(), calls=%async_computation.8 | async-start | bytes 8847360 | tf_op jit(solution)/shard_map/reduce_scatter | solution.py:1039
  491.0 53.8 %collective-permute-start.48 = (bf16[256,2048]{1,0:T(8,128)(2,1)S(1)}, bf16[256,2048]{1,0:T(8,128)(2,1)}, u32[]{:S(2)}, u32[]{:S(2)}) collective-permute-start(bf16[256,2048]{1,0:T(8,128)(2,1)S(1)} %get-tuple-element.281.refs_0_), channel_id=1, source_target_pairs={{0,1},{1,0},{2,3},{3,2},{4,5},{5,4},{6,7},{7,6},{8,9},{9,8},{10,11... | collective-permute-start | bytes 3145736 | tf_op jit(solution)/shard_map/ppermute | solution.py:493
  492.3 55.8 %collective-permute-start.49 = (bf16[256,2048]{1,0:T(8,128)(2,1)S(1)}, bf16[256,2048]{1,0:T(8,128)(2,1)}, u32[]{:S(2)}, u32[]{:S(2)}) collective-permute-start(bf16[256,2048]{1,0:T(8,128)(2,1)S(1)} %get-tuple-element.281.refs_0_), channel_id=1, source_target_pairs={{0,2},{1,3},{2,0},{3,1},{4,6},{5,7},{6,4},{7,5},{8,10},{9,11},{10,... | collective-permute-start | bytes 3145736 | tf_op jit(solution)/shard_map/ppermute | solution.py:493
  493.4 57.8 %collective-permute-start.45 = (bf16[256,2048]{1,0:T(8,128)(2,1)}, bf16[256,2048]{1,0:T(8,128)(2,1)S(1)}, u32[]{:S(2)}, u32[]{:S(2)}) collective-permute-start(bf16[256,2048]{1,0:T(8,128)(2,1)} %get-tuple-element.273), channel_id=1, source_target_pairs={{0,2},{1,3},{2,0},{3,1},{4,6},{5,7},{6,4},{7,5},{8,10},{9,11},{10,... | collective-permute-start | bytes 3145736 | tf_op jit(solution)/shard_map/ppermute | solution.py:493
  494.3 56.9 %collective-permute-start.44 = (bf16[256,2048]{1,0:T(8,128)(2,1)}, bf16[256,2048]{1,0:T(8,128)(2,1)S(1)}, u32[]{:S(2)}, u32[]{:S(2)}) collective-permute-start(bf16[256,2048]{1,0:T(8,128)(2,1)} %get-tuple-element.271), channel_id=1, source_target_pairs={{0,1},{1,0},{2,3},{3,2},{4,5},{5,4},{6,7},{7,6},{8,9},{9,8},{10,11... | collective-permute-start | bytes 3145736 | tf_op jit(solution)/shard_map/ppermute | solution.py:493
  546.8 26.2 %collective-permute-start.51 = (bf16[128,2048]{1,0:T(8,128)(2,1)}, bf16[128,2048]{1,0:T(8,128)(2,1)}, u32[]{:S(2)}, u32[]{:S(2)}) collective-permute-start(bf16[128,2048]{1,0:T(8,128)(2,1)} %slice.529), channel_id=1, source_target_pairs={{0,2},{1,3},{2,0},{3,1},{4,6},{5,7},{6,4},{7,5},{8,10},{9,11},{10,... | collective-permute-start | bytes 1572872 | tf_op jit(solution)/shard_map/ppermute | solution.py:493
  550.0 23.1 %collective-permute-start.50 = (bf16[128,2048]{1,0:T(8,128)(2,1)}, bf16[128,2048]{1,0:T(8,128)(2,1)}, u32[]{:S(2)}, u32[]{:S(2)}) collective-permute-start(bf16[128,2048]{1,0:T(8,128)(2,1)} %slice.528), channel_id=1, source_target_pairs={{0,1},{1,0},{2,3},{3,2},{4,5},{5,4},{6,7},{7,6},{8,9},{9,8},{10,11... | collective-permute-start | bytes 1572872 | tf_op jit(solution)/shard_map/ppermute | solution.py:493
  552.4 18.7 %collective-permute-start.46 = (bf16[128,2048]{1,0:T(8,128)(2,1)}, bf16[128,2048]{1,0:T(8,128)(2,1)S(1)}, u32[]{:S(2)}, u32[]{:S(2)}) collective-permute-start(bf16[128,2048]{1,0:T(8,128)(2,1)} %get-tuple-element.445), channel_id=1, source_target_pairs={{0,2},{1,3},{2,0},{3,1},{4,6},{5,7},{6,4},{7,5},{8,10},{9,11},{10,... | collective-permute-start | bytes 1572872 | tf_op jit(solution)/shard_map/ppermute | solution.py:493
  553.2 19.3 %collective-permute-start.47 = (bf16[128,2048]{1,0:T(8,128)(2,1)S(1)}, bf16[128,2048]{1,0:T(8,128)(2,1)S(1)}, u32[]{:S(2)}, u32[]{:S(2)}) collective-permute-start(bf16[128,2048]{1,0:T(8,128)(2,1)S(1)} %get-tuple-element.446), channel_id=1, source_target_pairs={{0,1},{1,0},{2,3},{3,2},{4,5},{5,4},{6,7},{7,6},{8,9},{9,8},{10,11... | collective-permute-start | bytes 1572872 | tf_op jit(solution)/shard_map/ppermute | solution.py:493
  569.7 29.8 %collective-permute-start.52 = (bf16[256,2048]{1,0:T(8,128)(2,1)}, bf16[256,2048]{1,0:T(8,128)(2,1)}, u32[]{:S(2)}, u32[]{:S(2)}) collective-permute-start(bf16[256,2048]{1,0:T(8,128)(2,1)} %get-tuple-element.278), channel_id=1, source_target_pairs={{0,1},{1,0},{2,3},{3,2},{4,5},{5,4},{6,7},{7,6},{8,9},{9,8},{10,11... | collective-permute-start | bytes 3145736 | tf_op jit(solution)/shard_map/ppermute | solution.py:493
  571.1 28.4 %collective-permute-start.53 = (bf16[256,2048]{1,0:T(8,128)(2,1)}, bf16[256,2048]{1,0:T(8,128)(2,1)}, u32[]{:S(2)}, u32[]{:S(2)}) collective-permute-start(bf16[256,2048]{1,0:T(8,128)(2,1)} %get-tuple-element.279), channel_id=1, source_target_pairs={{0,2},{1,3},{2,0},{3,1},{4,6},{5,7},{6,4},{7,5},{8,10},{9,11},{10,... | collective-permute-start | bytes 3145736 | tf_op jit(solution)/shard_map/ppermute | solution.py:493
  611.6 182.6 %reduce-scatter.5.cloned.1.call-start = ((), (), s32[]{:S(2)}) async-start(), calls=%async_computation.7 | async-start | bytes 10027008 | tf_op jit(solution)/shard_map/reduce_scatter | solution.py:1039
  612.8 43.5 %collective-permute-start.55 = (bf16[256,2048]{1,0:T(8,128)(2,1)S(1)}, bf16[256,2048]{1,0:T(8,128)(2,1)}, u32[]{:S(2)}, u32[]{:S(2)}) collective-permute-start(bf16[256,2048]{1,0:T(8,128)(2,1)S(1)} %copy-done.88), channel_id=1, source_target_pairs={{0,2},{1,3},{2,0},{3,1},{4,6},{5,7},{6,4},{7,5},{8,10},{9,11},{10,... | collective-permute-start | bytes 3145736 | tf_op jit(solution)/shard_map/ppermute | solution.py:493
  613.5 42.7 %collective-permute-start.54 = (bf16[256,2048]{1,0:T(8,128)(2,1)S(1)}, bf16[256,2048]{1,0:T(8,128)(2,1)}, u32[]{:S(2)}, u32[]{:S(2)}) collective-permute-start(bf16[256,2048]{1,0:T(8,128)(2,1)S(1)} %copy-done.87), channel_id=1, source_target_pairs={{0,1},{1,0},{2,3},{3,2},{4,5},{5,4},{6,7},{7,6},{8,9},{9,8},{10,11... | collective-permute-start | bytes 3145736 | tf_op jit(solution)/shard_map/ppermute | solution.py:493
  687.4 23.6 %collective-permute-start.58 = (bf16[128,2048]{1,0:T(8,128)(2,1)}, bf16[128,2048]{1,0:T(8,128)(2,1)S(1)}, u32[]{:S(2)}, u32[]{:S(2)}) collective-permute-start(bf16[128,2048]{1,0:T(8,128)(2,1)} %get-tuple-element.441), channel_id=1, source_target_pairs={{0,2},{1,3},{2,0},{3,1},{4,6},{5,7},{6,4},{7,5},{8,10},{9,11},{10,... | collective-permute-start | bytes 1572872 | tf_op jit(solution)/shard_map/ppermute | solution.py:493
  688.7 22.4 %collective-permute-start.59 = (bf16[128,2048]{1,0:T(8,128)(2,1)}, bf16[128,2048]{1,0:T(8,128)(2,1)}, u32[]{:S(2)}, u32[]{:S(2)}) collective-permute-start(bf16[128,2048]{1,0:T(8,128)(2,1)} %get-tuple-element.442), channel_id=1, source_target_pairs={{0,1},{1,0},{2,3},{3,2},{4,5},{5,4},{6,7},{7,6},{8,9},{9,8},{10,11... | collective-permute-start | bytes 1572872 | tf_op jit(solution)/shard_map/ppermute | solution.py:493
  737.2 20.5 %collective-permute-start.62 = (bf16[128,2048]{1,0:T(8,128)(2,1)}, bf16[128,2048]{1,0:T(8,128)(2,1)}, u32[]{:S(2)}, u32[]{:S(2)}) collective-permute-start(bf16[128,2048]{1,0:T(8,128)(2,1)} %get-tuple-element.439), channel_id=1, source_target_pairs={{0,2},{1,3},{2,0},{3,1},{4,6},{5,7},{6,4},{7,5},{8,10},{9,11},{10,... | collective-permute-start | bytes 1572872 | tf_op jit(solution)/shard_map/ppermute | solution.py:493
  738.3 19.5 %collective-permute-start.63 = (bf16[128,2048]{1,0:T(8,128)(2,1)}, bf16[128,2048]{1,0:T(8,128)(2,1)}, u32[]{:S(2)}, u32[]{:S(2)}) collective-permute-start(bf16[128,2048]{1,0:T(8,128)(2,1)} %get-tuple-element.440), channel_id=1, source_target_pairs={{0,1},{1,0},{2,3},{3,2},{4,5},{5,4},{6,7},{7,6},{8,9},{9,8},{10,11... | collective-permute-start | bytes 1572872 | tf_op jit(solution)/shard_map/ppermute | solution.py:493
  (114 other events, 1273.2 us)
Sparse Core Ops, SparseCore 0:
  9.7 63.1 all-gather.3
  74.5 59.1 all-gather.5
  135.3 59.0 all-gather.7
  420.1 65.0 reduce-scatter.8
  487.4 63.2 reduce-scatter.10
  611.7 85.0 reduce-scatter.6
  699.1 95.0 reduce-scatter.4

commit v4 on v3

--- a/solution.py
+++ b/solution.py
@@ -521,7 +521,8 @@
     if len(near) == 1:
         return []
     half = near[0].shape[0] // 2
-    return [hop(after(near[2][:half], *earlier), 1), hop(after(near[1][half:], *earlier), 2)]
+    from_x, from_y = after(near[1], *earlier), after(near[2], *earlier)
+    return [hop(from_y[:half], 1), hop(from_x[half:], 2)]
 
 
 def block_parts(size, rows):
@@ -554,16 +555,15 @@
     return [hop(after(to_x, *earlier), 1), hop(after(to_y, *earlier), 2), keep]
 
 
-def scatter_far(near, *earlier):
+def scatter_far(near, *earlier, before_end=()):
     if len(near) == 1:
         return near[0].astype(F32)
-    in_x, in_y, keep = near
+    in_x, in_y, keep = [after(item, *earlier) for item in near]
     half = in_x.shape[0] // 2
-    keep = after(keep, *earlier)
     pass_y = (keep[2 * half : 3 * half].astype(F32) + in_x[half:].astype(F32)).astype(BF)
     pass_x = (keep[3 * half :].astype(F32) + in_y[half:].astype(F32)).astype(BF)
-    last_y = hop(pass_y, 2).astype(F32)
-    last_x = hop(pass_x, 1).astype(F32)
+    last_y = after(hop(pass_y, 2), *before_end).astype(F32)
+    last_x = after(hop(pass_x, 1), *before_end).astype(F32)
     near_sum = jnp.concatenate([in_x[:half], in_y[:half]], axis=0).astype(F32)
     last = jnp.concatenate([last_y, last_x], axis=0)
     return keep[: 2 * half].astype(F32) + near_sum + last
@@ -1014,18 +1014,18 @@
     outs = len(scatter_plan(blocks, own_rows)[0])
     near_a = mid_a1 + mid_a2
     near_a[0] = after(near_a[0], at_b1)
-    sum_b = scatter_far(at_b1)
-    cot_b1 = gather_near(cots[1], at_b1)
+    sum_b = scatter_far(at_b1, mid_a2)
+    cot_b1 = gather_near(cots[1], at_b1, mid_a2)
     kept_a, begun = ffn_stage(first_turns, near_a, cot_a1 + cot_a2, ffn_weights, blocks)
     resid_b, pull_b, mid_b = middle(1, sum_b)
-    mid_b1 = gather_near(mid_b, kept_a[0])
+    mid_b1 = gather_near(mid_b)
     cot_b2 = gather_far(cot_b1, kept_a[0])
-    begun[0] = after(begun[0], mid_b, cot_b1)
+    begun[0] = after(begun[0], mid_b1, cot_b1)
     kept_a2, out_a = ffn_stage(
         last_turns, near_a, cot_a1 + cot_a2, ffn_weights, blocks, begun
     )
-    mid_b2 = gather_far(mid_b1, kept_a2[0], cot_b2)
-    gm_a1 = scatter_near(out_a[:outs], mid_b2)
+    mid_b2 = gather_far(mid_b1, kept_a[0])
+    gm_a1 = scatter_near(out_a[:outs], mid_b2, cot_b2)
     near_b = mid_b1 + mid_b2
     near_b[0] = after(near_b[0], out_a[0])
     kept_b, begun = ffn_stage(first_turns, near_b, cot_b1 + cot_b2, ffn_weights, blocks)
@@ -1049,12 +1049,15 @@
     gates[0] = after(gates[0], low_a)
     term_gate = weight_gradient(mids, gates)
     grad_gate = share(term_gate)
-    rg_a2 = gather_far(rg_a1, term_gate)
-    d_mid_b = scatter_far(gm_b1, term_gate)
-    ups[0] = after(ups[0], term_gate, rg_a1, gm_b1)
+    ups[0] = after(ups[0], term_gate)
     term_up = weight_gradient(mids, ups)
-    grad_up = share(term_up)
-    d_resid_b, gain_mid_b, low_b = resid_back(1, pull_b, after(d_mid_b, term_up))
+    grad_up = share(after(term_up, rg_a1, gm_b1))
+    rg_a2 = gather_far(rg_a1, term_up)
+    d_mid_b = scatter_far(gm_b1, term_up)
+    acts[0] = after(acts[0], term_up, rg_a1, gm_b1)
+    term_down = weight_gradient(cot_all, acts)
+    d_resid_b, gain_mid_b, low_b = resid_back(1, pull_b, after(d_mid_b, term_down, rg_a2))
+    grad_down = share(after(term_down, low_b))
     rg_b1 = gather_near(low_b)
     ff_a1 = scatter_near(out_a[outs:], low_b)
 
@@ -1083,21 +1086,16 @@
     pieces_rb = rg_b1 + rg_b2
     pieces_rb[0] = after(pieces_rb[0], d_in_a, ffn_a)
     d_mixed_b, full_rb = to_mixed(pieces_rb)
-    acts[0] = after(acts[0], d_mixed_b)
-    term_down = weight_gradient(cot_all, acts)
-    term_out = weight_gradient(
-        [full_ra, full_rb], [after(mixed_a, gi_a1), mixed_b], term_down
-    )
-    shared_out = share(term_out)
-    grad_out, grad_down = shared_out[:, :own].T, shared_out[:, own:]
-    ff_b1 = scatter_near(out_b[outs:], term_out)
-    d_raw_b, sums_b = mix_back(1, after(d_mixed_b, term_out), raw_b, saved_b)
-    term_in = weight_gradient([full_a, full_b], [d_raw_a, after(d_raw_b, ff_b1)])
+    term_out = weight_gradient([full_ra, full_rb], [after(mixed_a, d_mixed_b), mixed_b])
+    grad_out = share(term_out).T
+    ff_b1 = scatter_near(out_b[outs:], gi_a1)
+    d_raw_b, sums_b = mix_back(1, after(d_mixed_b, term_out, gi_a1), raw_b, saved_b)
+    term_in = weight_gradient([full_a, full_b], [d_raw_a, after(d_raw_b, ff_b1, grad_gate, grad_up)])
     grad_in = share(term_in)
-    d_norm_a = scatter_far(gi_a1, term_in)
-    ffn_b = scatter_far(ff_b1, term_in)
-    d_in_b = in_back(after(d_raw_b, term_in))
-    gi_b1 = scatter_near(d_in_b, d_norm_a, ffn_b)
+    d_in_b = in_back(after(d_raw_b, term_in, grad_down))
+    d_norm_a = scatter_far(gi_a1, term_out, before_end=[d_raw_b])
+    ffn_b = scatter_far(ff_b1, d_raw_b, before_end=d_in_b[:1])
+    gi_b1 = scatter_near(d_in_b)
     d_norm_b = scatter_far(gi_b1)
 
     results, input_grads = [], []

time: 818 us -> 784 us (0.958)
  waiting for transfers between devices: 172 us -> 131 us
    ppermute x72, waiting for transfers between devices: 166 us -> 126 us  [hop(): return lax.ppermute(values, axis, [(i, i ^ bit) for i in range(size)])]
    slice x17 -> x16, local copies, waits for them, and re-layouts: 12.1 us -> 17 us  [gather_far(): return [hop(from_y[:half], 1), hop(from_x[half:], 2)]]
  transfers between devices with their start and end apart: 79 -> 80, of which waited for: 30 -> 26; matrix products, arithmetic and copies ran while one was open for 12% -> 13% of each run, Pallas kernels for 47% -> 52%
where the time goes in v4:
time: 784 us; the launch traced here: 771 us
  Pallas kernels  423 us (54%)
  waiting for transfers between devices  131 us (17%)
  starting transfers between devices  79.4 us (10%)
  local copies, waits for them, and re-layouts  63.9 us (8%)
  other arithmetic  58.4 us (7%)
  between operations  16.1 us (2%)
    ppermute x72, waiting for transfers between devices, hop(): return lax.ppermute(values, axis, [(i, i ^ bit) for i in range(size)])  126 us
    pallas_call x4, Pallas kernels, ffn_stage(): pl.pallas_call(body, grid=(steps,), in_specs=[anywhere] * (first + len(fi...  113 us
    pallas_call x5, Pallas kernels, weight_gradient(): pl.pallas_call(lambda *refs: wgrad_kernel(count, *refs), grid=(wide // ti...  92.2 us
    pallas_call x2, Pallas kernels, mixer_backward(): pl.pallas_call(body, grid_spec=pltpu.PrefetchScalarGridSpec(num_scalar_pr...  83.1 us
    ppermute x72, starting transfers between devices, hop(): return lax.ppermute(values, axis, [(i, i ^ bit) for i in range(size)])  79.1 us
    pallas_call x4, Pallas kernels, piece_matmul(): pl.pallas_call(lambda *refs: piece_kernel(size, parts, len(pieces), trans...  50.2 us
    pallas_call x4, Pallas kernels, scatter_matmul(): pl.pallas_call(lambda *refs: scatter_kernel(size, where, transposed, *ref...  44 us
    pallas_call x2, Pallas kernels, mixer_forward(): pl.pallas_call(body, grid_spec=pltpu.PrefetchScalarGridSpec(num_scalar_pr...  40.4 us
  transfers between devices with their start and end apart: 80, of which 26 were waited for; matrix products, arithmetic and copies ran while one was open for 13% of the time, Pallas kernels for 52%

profile of v4, /device:TPU:0, one launch (start us, length us, event | category | flops | bytes accessed | tf_op | source)
XLA Modules:
  0.0 771.5 jit_solution(13414911618490076882)
XLA Ops:
  8.7 2.0 fusion.16
  11.3 1.9 fusion.14
  13.2 3.0 collective-permute-start.1
  23.3 14.0 %concatenate.88.refs_5_.refs_1_ = bf16[2048,2176]{1,0:T(8,128)(2,1)} concatenate(bf16[2048,512]{1,0:T(8,128)(2,1)} %param.29, bf16[2048,512]{1,0:T(8,128)(2,1)} %param.30, bf16[2048,512]{1,0:T(8,128)(2,1)} %param.31, bf16[2048,512]{1,0:T(8,128)(2,1)} %param.32, bf16[2048,4]{1,0:T(8,128)(2,1)S(1)} %copy.106, bf16[2048,4]{1,0:T(8,128)(2,1)S(1)} %copy.107, ...), dimensions={1} | concatenate | bytes 17825792 | tf_op jit(solution)/shard_map/concatenate | solution.py:969
  37.3 3.2 convert_multiply_fusion.2
  45.4 9.6 %collective-permute-done.2.refs_3_ = bf16[128,2048]{1,0:T(8,128)(2,1)S(1)} collective-permute-done((bf16[128,2048]{1,0:T(8,128)(2,1)S(1)}, bf16[128,2048]{1,0:T(8,128)(2,1)S(1)}, u32[]{:S(2)}, u32[]{:S(2)}) %collective-permute-start.2) | collective-permute-done | bytes 524320 | tf_op jit(solution)/shard_map/ppermute | solution.py:493
  59.5 16.8 %piece_matmul.4 = (f32[4,256,2176]{2,1,0:T(8,128)}, bf16[4,256,2048]{2,1,0:T(8,128)(2,1)}) custom-call(bf16[256,2048]{1,0:T(8,128)(2,1)} %get-tuple-element.471.refs_0_, bf16[256,2048]{1,0:T(8,128)(2,1)} %collective-permute-done.refs_1_, bf16[256,2048]{1,0:T(8,128)(2,1)} %collective-permute-done.1.refs_2_, bf16[128,2048]{1,0:T(8,128)(2,1)} %copy-done.92, ...), custom_call_target="tpu_custom_call" | custom-call | flops 18253611008 | bytes 30000000 | tf_op jit(solution)/shard_map/piece_matmul/pallas_call | solution.py:826
  76.4 4.2 collective-permute-done.4.refs_1_
  87.2 20.2 %mixer_forward.2 = (bf16[4,2,128,512]{3,2,1,0:T(8,128)(2,1)}, f32[4,2,128,512]{3,2,1,0:T(8,128)}, bf16[4,2,4,128,128]{4,3,2,1,0:T(8,128)(2,1)}, bf16[4,2,128,512...) custom-call(s32[4]{0:T(128)} %iota_xor_fusion.refs_0_, f32[4,2,128,2176]{3,2,1,0:T(8,128)} %bitcast.160, ...), custom_call_target="tpu_custom_call" | custom-call | flops 23520000000 | bytes 8000000 | tf_op jit(solution)/shard_map/mixer_forward/pallas_call | solution.py:393
  107.5 7.3 collective-permute-done.6.refs_3_
  115.4 6.0 scatter_matmul.4
  124.6 17.1 %piece_matmul.5 = (f32[4,256,2176]{2,1,0:T(8,128)}, bf16[4,256,2048]{2,1,0:T(8,128)(2,1)}) custom-call(bf16[256,2048]{1,0:T(8,128)(2,1)} %get-tuple-element.210.refs_0_, bf16[256,2048]{1,0:T(8,128)(2,1)} %copy-done.48, bf16[256,2048]{1,0:T(8,128)(2,1)} %copy-done.49, bf16[128,2048]{1,0:T(8,128)(2,1)} %copy-done.91, ...), custom_call_target="tpu_custom_call" | custom-call | flops 18253611008 | bytes 30000000 | tf_op jit(solution)/shard_map/piece_matmul/pallas_call | solution.py:826
  153.6 6.5 collective-permute-done.12
  161.5 2.0 multiply_reduce_fusion.5
  167.6 20.2 %mixer_forward.3 = (bf16[4,2,128,512]{3,2,1,0:T(8,128)(2,1)}, f32[4,2,128,512]{3,2,1,0:T(8,128)}, bf16[4,2,4,128,128]{4,3,2,1,0:T(8,128)(2,1)}, bf16[4,2,128,512...) custom-call(s32[4]{0:T(128)} %iota_xor_fusion.refs_0_, f32[4,2,128,2176]{3,2,1,0:T(8,128)} %bitcast.157, ...), custom_call_target="tpu_custom_call" | custom-call | flops 23520000000 | bytes 8000000 | tf_op jit(solution)/shard_map/mixer_forward/pallas_call | solution.py:393
  187.8 6.4 scatter_matmul.5
  198.6 30.0 %collective-permute-done.21.refs_4_ = bf16[128,2048]{1,0:T(8,128)(2,1)S(1)} collective-permute-done((bf16[128,2048]{1,0:T(8,128)(2,1)S(1)}, bf16[128,2048]{1,0:T(8,128)(2,1)S(1)}, u32[]{:S(2)}, u32[]{:S(2)}) %collective-permute-start.21) | collective-permute-done | bytes 524320 | tf_op jit(solution)/shard_map/ppermute | solution.py:493
  233.5 10.5 %collective-permute-done.22 = bf16[128,2048]{1,0:T(8,128)(2,1)S(1)} collective-permute-done((bf16[128,2048]{1,0:T(8,128)(2,1)S(1)}, bf16[128,2048]{1,0:T(8,128)(2,1)S(1)}, u32[]{:S(2)}, u32[]{:S(2)}) %collective-permute-start.22) | collective-permute-done | bytes 524320 | tf_op jit(solution)/shard_map/ppermute | solution.py:493
  249.3 28.3 %ffn_stage.4 = (bf16[2,256,1408]{2,1,0:T(8,128)(2,1)}, bf16[2,256,1408]{2,1,0:T(8,128)(2,1)}, bf16[2,256,1408]{2,1,0:T(8,128)(2,1)}, bf16[2,256,2048]{2,1,0:T(8,...) custom-call(bf16[256,2048]{1,0:T(8,128)(2,1)} %copy-done.36, ...), custom_call_target="tpu_custom_call" | custom-call | flops 29527900160 | bytes 30000000 | tf_op jit(solution)/shard_map/ffn_stage/pallas_call | solution.py:754
  282.9 6.2 collective-permute-done.24.refs_1_
  293.9 27.9 %ffn_stage.5 = (bf16[2,256,1408]{2,1,0:T(8,128)(2,1)}, bf16[2,256,1408]{2,1,0:T(8,128)(2,1)}, bf16[2,256,1408]{2,1,0:T(8,128)(2,1)}, bf16[2,256,2048]{2,1,0:T(8,...) custom-call(bf16[256,2048]{1,0:T(8,128)(2,1)} %copy-done.36, ...), custom_call_target="tpu_custom_call", output_to_operand_aliasing={{5}: (13, {}), {6}: (14, {}), {7}: (15, {}), {8}: (16, {}),... | custom-call | flops 29527900160 | bytes 30000000 | tf_op jit(solution)/shard_map/ffn_stage/pallas_call | solution.py:754
  323.6 28.1 %ffn_stage.6 = (bf16[2,256,1408]{2,1,0:T(8,128)(2,1)}, bf16[2,256,1408]{2,1,0:T(8,128)(2,1)}, bf16[2,256,1408]{2,1,0:T(8,128)(2,1)}, bf16[2,256,2048]{2,1,0:T(8,...) custom-call(bf16[256,2048]{1,0:T(8,128)(2,1)} %copy-done.37, ...), custom_call_target="tpu_custom_call" | custom-call | flops 29527900160 | bytes 30000000 | tf_op jit(solution)/shard_map/ffn_stage/pallas_call | solution.py:754
  354.6 28.3 %ffn_stage.7 = (bf16[2,256,1408]{2,1,0:T(8,128)(2,1)}, bf16[2,256,1408]{2,1,0:T(8,128)(2,1)}, bf16[2,256,1408]{2,1,0:T(8,128)(2,1)}, bf16[2,256,2048]{2,1,0:T(8,...) custom-call(bf16[256,2048]{1,0:T(8,128)(2,1)} %copy-done.37, ...), custom_call_target="tpu_custom_call", output_to_operand_aliasing={{5}: (13, {}), {6}: (14, {}), {7}: (15, {}), {8}: (16, {}),... | custom-call | flops 29527900160 | bytes 30000000 | tf_op jit(solution)/shard_map/ffn_stage/pallas_call | solution.py:754
  383.7 2.9 multiply_reduce_fusion.1
  386.6 2.0 fusion.33
  388.6 18.9 %weight_gradient.5 = bf16[2048,1408]{1,0:T(8,128)(2,1)} custom-call(bf16[512,2048]{1,0:T(8,128)(2,1)} %bitcast.173, bf16[512,2048]{1,0:T(8,128)(2,1)} %bitcast.176, bf16[512,2048]{1,0:T(8,128)(2,1)} %bitcast.179, bf16[512,2048]{1,0:T(8,128)(2,1)} %bitcast.181, bf16[512,1408]{1,0:T(8,128)(2,1)} %bitcast.188, bf16[512,1408]{1,0:T(8,128)(2,1)} %bitcast.192, ...), custom_call_target="tpu_custom_call" | custom-call | flops 17716740096 | bytes 20000000 | tf_op jit(solution)/shard_map/weight_gradient/pallas_call | solution.py:870
  411.7 19.1 %weight_gradient.6 = bf16[2048,1408]{1,0:T(8,128)(2,1)} custom-call(bf16[512,2048]{1,0:T(8,128)(2,1)} %bitcast.174, bf16[512,2048]{1,0:T(8,128)(2,1)} %bitcast.177, bf16[512,2048]{1,0:T(8,128)(2,1)} %bitcast.180, bf16[512,2048]{1,0:T(8,128)(2,1)} %bitcast.182, bf16[512,1408]{1,0:T(8,128)(2,1)} %bitcast.187, bf16[512,1408]{1,0:T(8,128)(2,1)} %bitcast.190, ...), custom_call_target="tpu_custom_call" | custom-call | flops 17716740096 | bytes 20000000 | tf_op jit(solution)/shard_map/weight_gradient/pallas_call | solution.py:870
  430.8 2.6 collective-permute-done.41.refs_2_
  433.4 11.6 %collective-permute-done.36 = bf16[256,2048]{1,0:T(8,128)(2,1)} collective-permute-done((bf16[256,2048]{1,0:T(8,128)(2,1)}, bf16[256,2048]{1,0:T(8,128)(2,1)}, u32[]{:S(2)}, u32[]{:S(2)}) %collective-permute-start.36) | collective-permute-done | bytes 1048608 | tf_op jit(solution)/shard_map/ppermute | solution.py:493
  446.1 1.9 slice.435
  448.6 1.9 slice.434
  451.7 2.9 add_convert_fusion.11
  456.8 18.6 %weight_gradient.7 = bf16[2048,1408]{1,0:T(8,128)(2,1)} custom-call(bf16[512,2048]{1,0:T(8,128)(2,1)} %bitcast.171, bf16[512,2048]{1,0:T(8,128)(2,1)} %bitcast.172, bf16[512,2048]{1,0:T(8,128)(2,1)} %bitcast.175, bf16[512,2048]{1,0:T(8,128)(2,1)} %bitcast.178, bf16[512,1408]{1,0:T(8,128)(2,1)} %bitcast.185, bf16[512,1408]{1,0:T(8,128)(2,1)} %bitcast.186, ...), custom_call_target="tpu_custom_call" | custom-call | flops 17716740096 | bytes 20000000 | tf_op jit(solution)/shard_map/weight_gradient/pallas_call | solution.py:870
  481.2 2.0 fusion.31
  487.4 8.3 %piece_matmul.6 = (f32[4,256,512]{2,1,0:T(8,128)}, bf16[4,256,2048]{2,1,0:T(8,128)(2,1)}) custom-call(bf16[256,2048]{1,0:T(8,128)(2,1)} %copy-done.34, bf16[256,2048]{1,0:T(8,128)(2,1)} %collective-permute-done.40.refs_1_, bf16[256,2048]{1,0:T(8,128)(2,1)} %collective-permute-done.41.refs_2_, bf16[128,2048]{1,0:T(8,128)(2,1)} %collective-permute-done.42.refs_3_, ...), custom_call_target="tpu_custom_call" | custom-call | flops 4294967296 | bytes 30000000 | tf_op jit(solution)/shard_map/piece_matmul/pallas_call | solution.py:826
  495.7 41.6 %mixer_backward.2 = (bf16[4,2,128,2176]{3,2,1,0:T(8,128)(2,1)}, f32[96,512]{1,0:T(8,128)}, f32[8,128]{1,0:T(8,128)}, f32[8,512]{1,0:T(8,128)}) custom-call(s32[4]{0:T(128)} %iota_xor_fusion.refs_0_, f32[4,2,128,2176]{3,2,1,0:T(8,128)} %bitcast.161, f32[4,2,128,2176]{3,2,1,0:T(8,128)} %bitcast.162, f32[2,4,128,16]{3,2,1,0:T(8,128)} %bitcast.141, ...), custom_call_target="tpu_custom_call" | custom-call | flops 52800000000 | bytes 12000000 | tf_op jit(solution)/shard_map/mixer_backward/pallas_call | solution.py:446
  537.3 2.0 slice.444
  540.1 1.9 slice.443
  546.9 16.0 %scatter_matmul.6 = (bf16[256,2048]{1,0:T(8,128)(2,1)}, bf16[256,2048]{1,0:T(8,128)(2,1)}, bf16[512,2048]{1,0:T(8,128)(2,1)}) custom-call(bf16[1024,2176]{1,0:T(8,128)(2,1)} %bitcast.163, bf16[2048,2176]{1,0:T(8,128)(2,1)} %concatenate.88.refs_5_.refs_1_), custom_call_target="tpu_custom_call" | custom-call | flops 18253611008 | bytes 15000000 | tf_op jit(solution)/shard_map/scatter_matmul/pallas_call | solution.py:611
  564.7 2.3 collective-permute-done.47
  568.7 8.1 %piece_matmul.7 = (f32[4,256,512]{2,1,0:T(8,128)}, bf16[4,256,2048]{2,1,0:T(8,128)(2,1)}) custom-call(bf16[256,2048]{1,0:T(8,128)(2,1)} %copy-done.35, bf16[256,2048]{1,0:T(8,128)(2,1)} %collective-permute-done.48.refs_1_, bf16[256,2048]{1,0:T(8,128)(2,1)} %collective-permute-done.49.refs_2_, bf16[128,2048]{1,0:T(8,128)(2,1)} %collective-permute-done.50.refs_3_, ...), custom_call_target="tpu_custom_call" | custom-call | flops 4294967296 | bytes 30000000 | tf_op jit(solution)/shard_map/piece_matmul/pallas_call | solution.py:826
  576.8 8.8 %weight_gradient.8 = bf16[2048,512]{1,0:T(8,128)(2,1)} custom-call(bf16[1024,2048]{1,0:T(8,128)(2,1)} %bitcast.169, bf16[1024,2048]{1,0:T(8,128)(2,1)} %bitcast.170, bf16[1024,512]{1,0:T(8,128)(2,1)} %bitcast.198, bf16[1024,512]{1,0:T(8,128)(2,1)} %bitcast.200), custom_call_target="tpu_custom_call" | custom-call | flops 6442450944 | bytes 20000000 | tf_op jit(solution)/shard_map/weight_gradient/pallas_call | solution.py:870
  590.0 41.5 %mixer_backward.3 = (bf16[4,2,128,2176]{3,2,1,0:T(8,128)(2,1)}, f32[96,512]{1,0:T(8,128)}, f32[8,128]{1,0:T(8,128)}, f32[8,512]{1,0:T(8,128)}) custom-call(s32[4]{0:T(128)} %iota_xor_fusion.refs_0_, f32[4,2,128,2176]{3,2,1,0:T(8,128)} %bitcast.158, f32[4,2,128,2176]{3,2,1,0:T(8,128)} %bitcast.159, f32[2,4,128,16]{3,2,1,0:T(8,128)} %bitcast.143, ...), custom_call_target="tpu_custom_call" | custom-call | flops 52800000000 | bytes 12000000 | tf_op jit(solution)/shard_map/mixer_backward/pallas_call | solution.py:446
  631.5 2.3 convert_element_type.406
  633.8 2.3 convert_element_type.407
  636.1 26.8 %weight_gradient.9 = bf16[2048,2176]{1,0:T(8,128)(2,1)} custom-call(bf16[1024,2048]{1,0:T(8,128)(2,1)} %bitcast.167, bf16[1024,2048]{1,0:T(8,128)(2,1)} %bitcast.168, bf16[1024,2176]{1,0:T(8,128)(2,1)} %bitcast.164, bf16[1024,2176]{1,0:T(8,128)(2,1)} %bitcast.165), custom_call_target="tpu_custom_call" | custom-call | flops 27380416512 | bytes 20000000 | tf_op jit(solution)/shard_map/weight_gradient/pallas_call | solution.py:870
  664.5 2.6 add_convert_fusion.5
  669.3 2.4 convert_element_type.408
  671.6 15.6 %scatter_matmul.7 = (bf16[256,2048]{1,0:T(8,128)(2,1)}, bf16[256,2048]{1,0:T(8,128)(2,1)}, bf16[512,2048]{1,0:T(8,128)(2,1)}) custom-call(bf16[1024,2176]{1,0:T(8,128)(2,1)} %bitcast.166, bf16[2048,2176]{1,0:T(8,128)(2,1)} %concatenate.88.refs_5_.refs_1_), custom_call_target="tpu_custom_call" | custom-call | flops 18253611008 | bytes 15000000 | tf_op jit(solution)/shard_map/scatter_matmul/pallas_call | solution.py:611
  692.9 2.4 collective-permute-start.70
  696.4 2.0 collective-permute-done.70
  698.4 1.9 collective-permute-start.71
  702.1 2.2 copy.121
  706.8 11.8 %collective-permute-done.56 = bf16[128,2048]{1,0:T(8,128)(2,1)} collective-permute-done((bf16[128,2048]{1,0:T(8,128)(2,1)}, bf16[128,2048]{1,0:T(8,128)(2,1)}, u32[]{:S(2)}, u32[]{:S(2)}) %collective-permute-start.56) | collective-permute-done | bytes 524320 | tf_op jit(solution)/shard_map/ppermute | solution.py:493
  718.6 1.9 add_convert_fusion.3
  722.9 2.3 add_convert_fusion
  727.7 2.1 collective-permute-done.62
  731.3 3.5 fusion.15
  737.8 3.2 collective-permute-done.65
  741.0 2.4 collective-permute-start.66
  743.4 3.1 collective-permute-done.66
  747.5 4.0 fusion.3
  755.9 3.6 reduce-scatter.12.cloned.1.call-done
  761.8 2.6 fusion.36
  (464 shorter events, 140.0 us)
Async XLA Ops:
  7.2 242.1 %all-gather.4.cloned.1.call-start = ((), (), s32[]{:S(2)}) async-start(), calls=%async_computation.5 | async-start | bytes 6488064 | tf_op jit(solution)/shard_map/all_gather | solution.py:952
  7.9 241.3 %all-gather.6.cloned.1.call-start = ((), (), s32[]{:S(2)}) async-start(), calls=%async_computation.6 | async-start | bytes 6488064 | tf_op jit(solution)/shard_map/all_gather | solution.py:953
  8.7 240.6 %all-gather.8.cloned.1.call-start = ((), (), s32[]{:S(2)}) async-start(), calls=%async_computation.7 | async-start | bytes 6488064 | tf_op jit(solution)/shard_map/all_gather | solution.py:954
  13.2 27.3 %collective-permute-start.1 = (bf16[256,2048]{1,0:T(8,128)(2,1)}, bf16[256,2048]{1,0:T(8,128)(2,1)}, u32[]{:S(2)}, u32[]{:S(2)}) collective-permute-start(bf16[256,2048]{1,0:T(8,128)(2,1)} %get-tuple-element.471.refs_0_), channel_id=1, source_target_pairs={{0,2},{1,3},{2,0},{3,1},{4,6},{5,7},{6,4},{7,5},{8,10},{9,11},{10,... | collective-permute-start | bytes 3145736 | tf_op jit(solution)/shard_map/ppermute | solution.py:493
  16.3 26.6 %collective-permute-start = (bf16[256,2048]{1,0:T(8,128)(2,1)}, bf16[256,2048]{1,0:T(8,128)(2,1)}, u32[]{:S(2)}, u32[]{:S(2)}) collective-permute-start(bf16[256,2048]{1,0:T(8,128)(2,1)} %get-tuple-element.471.refs_0_), channel_id=1, source_target_pairs={{0,1},{1,0},{2,3},{3,2},{4,5},{5,4},{6,7},{7,6},{8,9},{9,8},{10,11... | collective-permute-start | bytes 3145736 | tf_op jit(solution)/shard_map/ppermute | solution.py:493
  17.8 613.7 %reduce-scatter.6.cloned.1.call-start = ((), (), s32[]{:S(2)}) async-start(), calls=%async_computation.8 | async-start | bytes 6488064 | tf_op jit(solution)/shard_map/reduce_scatter | solution.py:1039
  57.5 23.1 %collective-permute-start.4 = (bf16[256,2048]{1,0:T(8,128)(2,1)S(1)}, bf16[256,2048]{1,0:T(8,128)(2,1)S(1)}, u32[]{:S(2)}, u32[]{:S(2)}) collective-permute-start(bf16[256,2048]{1,0:T(8,128)(2,1)S(1)} %copy-done.43), channel_id=1, source_target_pairs={{0,1},{1,0},{2,3},{3,2},{4,5},{5,4},{6,7},{7,6},{8,9},{9,8},{10,11... | collective-permute-start | bytes 3145736 | tf_op jit(solution)/shard_map/ppermute | solution.py:493
  58.8 23.0 %collective-permute-start.5 = (bf16[256,2048]{1,0:T(8,128)(2,1)S(1)}, bf16[256,2048]{1,0:T(8,128)(2,1)S(1)}, u32[]{:S(2)}, u32[]{:S(2)}) collective-permute-start(bf16[256,2048]{1,0:T(8,128)(2,1)S(1)} %copy-done.43), channel_id=1, source_target_pairs={{0,2},{1,3},{2,0},{3,1},{4,6},{5,7},{6,4},{7,5},{8,10},{9,11},{10,... | collective-permute-start | bytes 3145736 | tf_op jit(solution)/shard_map/ppermute | solution.py:493
  81.7 41.9 %collective-permute-start.8 = (bf16[256,2048]{1,0:T(8,128)(2,1)S(1)}, bf16[256,2048]{1,0:T(8,128)(2,1)S(1)}, u32[]{:S(2)}, u32[]{:S(2)}) collective-permute-start(bf16[256,2048]{1,0:T(8,128)(2,1)S(1)} %bitcast_convert_fusion.1.refs_5_), channel_id=1, source_target_pairs={{0,1},{1,0},{2,3},{3,2},{4,5},{5,4},{6,7},{7,6},{8,9},{9,8},{10,11... | collective-permute-start | bytes 3145736 | tf_op jit(solution)/shard_map/ppermute | solution.py:493
  82.3 41.3 %collective-permute-start.9 = (bf16[256,2048]{1,0:T(8,128)(2,1)S(1)}, bf16[256,2048]{1,0:T(8,128)(2,1)}, u32[]{:S(2)}, u32[]{:S(2)}) collective-permute-start(bf16[256,2048]{1,0:T(8,128)(2,1)S(1)} %bitcast_convert_fusion.1.refs_5_), channel_id=1, source_target_pairs={{0,2},{1,3},{2,0},{3,1},{4,6},{5,7},{6,4},{7,5},{8,10},{9,11},{10,... | collective-permute-start | bytes 3145736 | tf_op jit(solution)/shard_map/ppermute | solution.py:493
  83.3 31.5 %collective-permute-start.6 = (bf16[128,2048]{1,0:T(8,128)(2,1)S(1)}, bf16[128,2048]{1,0:T(8,128)(2,1)S(1)}, u32[]{:S(2)}, u32[]{:S(2)}) collective-permute-start(bf16[128,2048]{1,0:T(8,128)(2,1)S(1)} %slice.388), channel_id=1, source_target_pairs={{0,1},{1,0},{2,3},{3,2},{4,5},{5,4},{6,7},{7,6},{8,9},{9,8},{10,11... | collective-permute-start | bytes 1572872 | tf_op jit(solution)/shard_map/ppermute | solution.py:493
  84.7 30.7 %collective-permute-start.7 = (bf16[128,2048]{1,0:T(8,128)(2,1)S(1)}, bf16[128,2048]{1,0:T(8,128)(2,1)}, u32[]{:S(2)}, u32[]{:S(2)}) collective-permute-start(bf16[128,2048]{1,0:T(8,128)(2,1)S(1)} %slice.389), channel_id=1, source_target_pairs={{0,2},{1,3},{2,0},{3,1},{4,6},{5,7},{6,4},{7,5},{8,10},{9,11},{10,... | collective-permute-start | bytes 1572872 | tf_op jit(solution)/shard_map/ppermute | solution.py:493
  121.5 21.7 %collective-permute-start.11 = (bf16[256,2048]{1,0:T(8,128)(2,1)}, bf16[256,2048]{1,0:T(8,128)(2,1)S(1)}, u32[]{:S(2)}, u32[]{:S(2)}) collective-permute-start(bf16[256,2048]{1,0:T(8,128)(2,1)} %get-tuple-element.208), channel_id=1, source_target_pairs={{0,2},{1,3},{2,0},{3,1},{4,6},{5,7},{6,4},{7,5},{8,10},{9,11},{10,... | collective-permute-start | bytes 3145736 | tf_op jit(solution)/shard_map/ppermute | solution.py:493
  122.4 20.8 %collective-permute-start.10 = (bf16[256,2048]{1,0:T(8,128)(2,1)}, bf16[256,2048]{1,0:T(8,128)(2,1)S(1)}, u32[]{:S(2)}, u32[]{:S(2)}) collective-permute-start(bf16[256,2048]{1,0:T(8,128)(2,1)} %get-tuple-element.207), channel_id=1, source_target_pairs={{0,1},{1,0},{2,3},{3,2},{4,5},{5,4},{6,7},{7,6},{8,9},{9,8},{10,11... | collective-permute-start | bytes 3145736 | tf_op jit(solution)/shard_map/ppermute | solution.py:493
  149.7 38.1 %collective-permute-start.15 = (bf16[128,2048]{1,0:T(8,128)(2,1)S(1)}, bf16[128,2048]{1,0:T(8,128)(2,1)S(1)}, u32[]{:S(2)}, u32[]{:S(2)}) collective-permute-start(bf16[128,2048]{1,0:T(8,128)(2,1)S(1)} %slice.404), channel_id=1, source_target_pairs={{0,2},{1,3},{2,0},{3,1},{4,6},{5,7},{6,4},{7,5},{8,10},{9,11},{10,... | collective-permute-start | bytes 1572872 | tf_op jit(solution)/shard_map/ppermute | solution.py:493
  151.6 36.2 %collective-permute-start.14 = (bf16[128,2048]{1,0:T(8,128)(2,1)S(1)}, bf16[128,2048]{1,0:T(8,128)(2,1)S(1)}, u32[]{:S(2)}, u32[]{:S(2)}) collective-permute-start(bf16[128,2048]{1,0:T(8,128)(2,1)S(1)} %slice.403), channel_id=1, source_target_pairs={{0,1},{1,0},{2,3},{3,2},{4,5},{5,4},{6,7},{7,6},{8,9},{9,8},{10,11... | collective-permute-start | bytes 1572872 | tf_op jit(solution)/shard_map/ppermute | solution.py:493
  165.1 29.1 %collective-permute-start.16 = (bf16[256,2048]{1,0:T(8,128)(2,1)S(1)}, bf16[256,2048]{1,0:T(8,128)(2,1)S(1)}, u32[]{:S(2)}, u32[]{:S(2)}) collective-permute-start(bf16[256,2048]{1,0:T(8,128)(2,1)S(1)} %multiply_convert_fusion.1.refs_0_), channel_id=1, source_target_pairs={{0,1},{1,0},{2,3},{3,2},{4,5},{5,4},{6,7},{7,6},{8,9},{9,8},{10,11... | collective-permute-start | bytes 3145736 | tf_op jit(solution)/shard_map/ppermute | solution.py:493
  166.3 28.0 %collective-permute-start.17 = (bf16[256,2048]{1,0:T(8,128)(2,1)S(1)}, bf16[256,2048]{1,0:T(8,128)(2,1)S(1)}, u32[]{:S(2)}, u32[]{:S(2)}) collective-permute-start(bf16[256,2048]{1,0:T(8,128)(2,1)S(1)} %multiply_convert_fusion.1.refs_0_), channel_id=1, source_target_pairs={{0,2},{1,3},{2,0},{3,1},{4,6},{5,7},{6,4},{7,5},{8,10},{9,11},{10,... | collective-permute-start | bytes 3145736 | tf_op jit(solution)/shard_map/ppermute | solution.py:493
  194.3 34.3 %collective-permute-start.19 = (bf16[256,2048]{1,0:T(8,128)(2,1)}, bf16[256,2048]{1,0:T(8,128)(2,1)S(1)}, u32[]{:S(2)}, u32[]{:S(2)}) collective-permute-start(bf16[256,2048]{1,0:T(8,128)(2,1)} %get-tuple-element.223), channel_id=1, source_target_pairs={{0,2},{1,3},{2,0},{3,1},{4,6},{5,7},{6,4},{7,5},{8,10},{9,11},{10,... | collective-permute-start | bytes 3145736 | tf_op jit(solution)/shard_map/ppermute | solution.py:493
  195.7 32.9 %collective-permute-start.18 = (bf16[256,2048]{1,0:T(8,128)(2,1)}, bf16[256,2048]{1,0:T(8,128)(2,1)S(1)}, u32[]{:S(2)}, u32[]{:S(2)}) collective-permute-start(bf16[256,2048]{1,0:T(8,128)(2,1)} %get-tuple-element.221), channel_id=1, source_target_pairs={{0,1},{1,0},{2,3},{3,2},{4,5},{5,4},{6,7},{7,6},{8,9},{9,8},{10,11... | collective-permute-start | bytes 3145736 | tf_op jit(solution)/shard_map/ppermute | solution.py:493
  196.7 32.0 %collective-permute-start.21 = (bf16[128,2048]{1,0:T(8,128)(2,1)S(1)}, bf16[128,2048]{1,0:T(8,128)(2,1)S(1)}, u32[]{:S(2)}, u32[]{:S(2)}) collective-permute-start(bf16[128,2048]{1,0:T(8,128)(2,1)S(1)} %slice.406), channel_id=1, source_target_pairs={{0,2},{1,3},{2,0},{3,1},{4,6},{5,7},{6,4},{7,5},{8,10},{9,11},{10,... | collective-permute-start | bytes 1572872 | tf_op jit(solution)/shard_map/ppermute | solution.py:493
  197.3 31.3 %collective-permute-start.20 = (bf16[128,2048]{1,0:T(8,128)(2,1)S(1)}, bf16[128,2048]{1,0:T(8,128)(2,1)S(1)}, u32[]{:S(2)}, u32[]{:S(2)}) collective-permute-start(bf16[128,2048]{1,0:T(8,128)(2,1)S(1)} %slice.405), channel_id=1, source_target_pairs={{0,1},{1,0},{2,3},{3,2},{4,5},{5,4},{6,7},{7,6},{8,9},{9,8},{10,11... | collective-permute-start | bytes 1572872 | tf_op jit(solution)/shard_map/ppermute | solution.py:493
  231.8 45.8 %collective-permute-start.26 = (bf16[256,2048]{1,0:T(8,128)(2,1)S(1)}, bf16[256,2048]{1,0:T(8,128)(2,1)}, u32[]{:S(2)}, u32[]{:S(2)}) collective-permute-start(bf16[256,2048]{1,0:T(8,128)(2,1)S(1)} %bitcast_convert_fusion.refs_5_), channel_id=1, source_target_pairs={{0,1},{1,0},{2,3},{3,2},{4,5},{5,4},{6,7},{7,6},{8,9},{9,8},{10,11... | collective-permute-start | bytes 3145736 | tf_op jit(solution)/shard_map/ppermute | solution.py:493
  233.1 47.4 %collective-permute-start.27 = (bf16[256,2048]{1,0:T(8,128)(2,1)S(1)}, bf16[256,2048]{1,0:T(8,128)(2,1)}, u32[]{:S(2)}, u32[]{:S(2)}) collective-permute-start(bf16[256,2048]{1,0:T(8,128)(2,1)S(1)} %bitcast_convert_fusion.refs_5_), channel_id=1, source_target_pairs={{0,2},{1,3},{2,0},{3,1},{4,6},{5,7},{6,4},{7,5},{8,10},{9,11},{10,... | collective-permute-start | bytes 3145736 | tf_op jit(solution)/shard_map/ppermute | solution.py:493
  248.1 41.0 %collective-permute-start.24 = (bf16[256,2048]{1,0:T(8,128)(2,1)S(1)}, bf16[256,2048]{1,0:T(8,128)(2,1)}, u32[]{:S(2)}, u32[]{:S(2)}) collective-permute-start(bf16[256,2048]{1,0:T(8,128)(2,1)S(1)} %multiply_convert_fusion.refs_0_), channel_id=1, source_target_pairs={{0,1},{1,0},{2,3},{3,2},{4,5},{5,4},{6,7},{7,6},{8,9},{9,8},{10,11... | collective-permute-start | bytes 3145736 | tf_op jit(solution)/shard_map/ppermute | solution.py:493
  249.0 42.8 %collective-permute-start.25 = (bf16[256,2048]{1,0:T(8,128)(2,1)S(1)}, bf16[256,2048]{1,0:T(8,128)(2,1)}, u32[]{:S(2)}, u32[]{:S(2)}) collective-permute-start(bf16[256,2048]{1,0:T(8,128)(2,1)S(1)} %multiply_convert_fusion.refs_0_), channel_id=1, source_target_pairs={{0,2},{1,3},{2,0},{3,1},{4,6},{5,7},{6,4},{7,5},{8,10},{9,11},{10,... | collective-permute-start | bytes 3145736 | tf_op jit(solution)/shard_map/ppermute | solution.py:493
  278.7 43.1 %collective-permute-start.31 = (bf16[128,2048]{1,0:T(8,128)(2,1)S(1)}, bf16[128,2048]{1,0:T(8,128)(2,1)S(1)}, u32[]{:S(2)}, u32[]{:S(2)}) collective-permute-start(bf16[128,2048]{1,0:T(8,128)(2,1)S(1)} %slice.419), channel_id=1, source_target_pairs={{0,2},{1,3},{2,0},{3,1},{4,6},{5,7},{6,4},{7,5},{8,10},{9,11},{10,... | collective-permute-start | bytes 1572872 | tf_op jit(solution)/shard_map/ppermute | solution.py:493
  281.6 40.2 %collective-permute-start.30 = (bf16[128,2048]{1,0:T(8,128)(2,1)S(1)}, bf16[128,2048]{1,0:T(8,128)(2,1)S(1)}, u32[]{:S(2)}, u32[]{:S(2)}) collective-permute-start(bf16[128,2048]{1,0:T(8,128)(2,1)S(1)} %slice.418), channel_id=1, source_target_pairs={{0,1},{1,0},{2,3},{3,2},{4,5},{5,4},{6,7},{7,6},{8,9},{9,8},{10,11... | collective-permute-start | bytes 1572872 | tf_op jit(solution)/shard_map/ppermute | solution.py:493
  290.2 31.6 %collective-permute-start.29 = (bf16[128,2048]{1,0:T(8,128)(2,1)S(1)}, bf16[128,2048]{1,0:T(8,128)(2,1)S(1)}, u32[]{:S(2)}, u32[]{:S(2)}) collective-permute-start(bf16[128,2048]{1,0:T(8,128)(2,1)S(1)} %slice.417), channel_id=1, source_target_pairs={{0,2},{1,3},{2,0},{3,1},{4,6},{5,7},{6,4},{7,5},{8,10},{9,11},{10,... | collective-permute-start | bytes 1572872 | tf_op jit(solution)/shard_map/ppermute | solution.py:493
  292.8 29.1 %collective-permute-start.28 = (bf16[128,2048]{1,0:T(8,128)(2,1)S(1)}, bf16[128,2048]{1,0:T(8,128)(2,1)S(1)}, u32[]{:S(2)}, u32[]{:S(2)}) collective-permute-start(bf16[128,2048]{1,0:T(8,128)(2,1)S(1)} %slice.416), channel_id=1, source_target_pairs={{0,1},{1,0},{2,3},{3,2},{4,5},{5,4},{6,7},{7,6},{8,9},{9,8},{10,11... | collective-permute-start | bytes 1572872 | tf_op jit(solution)/shard_map/ppermute | solution.py:493
  321.9 29.8 %collective-permute-start.33 = (bf16[256,2048]{1,0:T(8,128)(2,1)}, bf16[256,2048]{1,0:T(8,128)(2,1)S(1)}, u32[]{:S(2)}, u32[]{:S(2)}) collective-permute-start(bf16[256,2048]{1,0:T(8,128)(2,1)} %get-tuple-element.253), channel_id=1, source_target_pairs={{0,2},{1,3},{2,0},{3,1},{4,6},{5,7},{6,4},{7,5},{8,10},{9,11},{10,... | collective-permute-start | bytes 3145736 | tf_op jit(solution)/shard_map/ppermute | solution.py:493
  322.9 28.9 %collective-permute-start.32 = (bf16[256,2048]{1,0:T(8,128)(2,1)}, bf16[256,2048]{1,0:T(8,128)(2,1)S(1)}, u32[]{:S(2)}, u32[]{:S(2)}) collective-permute-start(bf16[256,2048]{1,0:T(8,128)(2,1)} %get-tuple-element.250), channel_id=1, source_target_pairs={{0,1},{1,0},{2,3},{3,2},{4,5},{5,4},{6,7},{7,6},{8,9},{9,8},{10,11... | collective-permute-start | bytes 3145736 | tf_op jit(solution)/shard_map/ppermute | solution.py:493
  352.2 31.0 %collective-permute-start.34 = (bf16[128,2048]{1,0:T(8,128)(2,1)S(1)}, bf16[128,2048]{1,0:T(8,128)(2,1)}, u32[]{:S(2)}, u32[]{:S(2)}) collective-permute-start(bf16[128,2048]{1,0:T(8,128)(2,1)S(1)} %get-tuple-element.483), channel_id=1, source_target_pairs={{0,2},{1,3},{2,0},{3,1},{4,6},{5,7},{6,4},{7,5},{8,10},{9,11},{10,... | collective-permute-start | bytes 1572872 | tf_op jit(solution)/shard_map/ppermute | solution.py:493
  353.6 29.5 %collective-permute-start.35 = (bf16[128,2048]{1,0:T(8,128)(2,1)S(1)}, bf16[128,2048]{1,0:T(8,128)(2,1)}, u32[]{:S(2)}, u32[]{:S(2)}) collective-permute-start(bf16[128,2048]{1,0:T(8,128)(2,1)S(1)} %get-tuple-element.484), channel_id=1, source_target_pairs={{0,1},{1,0},{2,3},{3,2},{4,5},{5,4},{6,7},{7,6},{8,9},{9,8},{10,11... | collective-permute-start | bytes 1572872 | tf_op jit(solution)/shard_map/ppermute | solution.py:493
  407.5 226.3 %reduce-scatter.8.cloned.1.call-start = ((), (), s32[]{:S(2)}) async-start(), calls=%async_computation.9 | async-start | bytes 6488064 | tf_op jit(solution)/shard_map/reduce_scatter | solution.py:1039
  407.5 23.2 %collective-permute-start.40 = (bf16[256,2048]{1,0:T(8,128)(2,1)S(1)}, bf16[256,2048]{1,0:T(8,128)(2,1)}, u32[]{:S(2)}, u32[]{:S(2)}) collective-permute-start(bf16[256,2048]{1,0:T(8,128)(2,1)S(1)} %get-tuple-element.294.refs_0_), channel_id=1, source_target_pairs={{0,1},{1,0},{2,3},{3,2},{4,5},{5,4},{6,7},{7,6},{8,9},{9,8},{10,11... | collective-permute-start | bytes 3145736 | tf_op jit(solution)/shard_map/ppermute | solution.py:493
  408.6 24.7 %collective-permute-start.41 = (bf16[256,2048]{1,0:T(8,128)(2,1)S(1)}, bf16[256,2048]{1,0:T(8,128)(2,1)}, u32[]{:S(2)}, u32[]{:S(2)}) collective-permute-start(bf16[256,2048]{1,0:T(8,128)(2,1)S(1)} %get-tuple-element.294.refs_0_), channel_id=1, source_target_pairs={{0,2},{1,3},{2,0},{3,1},{4,6},{5,7},{6,4},{7,5},{8,10},{9,11},{10,... | collective-permute-start | bytes 3145736 | tf_op jit(solution)/shard_map/ppermute | solution.py:493
  409.2 35.7 %collective-permute-start.36 = (bf16[256,2048]{1,0:T(8,128)(2,1)}, bf16[256,2048]{1,0:T(8,128)(2,1)}, u32[]{:S(2)}, u32[]{:S(2)}) collective-permute-start(bf16[256,2048]{1,0:T(8,128)(2,1)} %get-tuple-element.279), channel_id=1, source_target_pairs={{0,1},{1,0},{2,3},{3,2},{4,5},{5,4},{6,7},{7,6},{8,9},{9,8},{10,11... | collective-permute-start | bytes 3145736 | tf_op jit(solution)/shard_map/ppermute | solution.py:493
  410.5 35.5 %collective-permute-start.37 = (bf16[256,2048]{1,0:T(8,128)(2,1)}, bf16[256,2048]{1,0:T(8,128)(2,1)}, u32[]{:S(2)}, u32[]{:S(2)}) collective-permute-start(bf16[256,2048]{1,0:T(8,128)(2,1)} %get-tuple-element.282), channel_id=1, source_target_pairs={{0,2},{1,3},{2,0},{3,1},{4,6},{5,7},{6,4},{7,5},{8,10},{9,11},{10,... | collective-permute-start | bytes 3145736 | tf_op jit(solution)/shard_map/ppermute | solution.py:493
  446.0 223.2 %reduce-scatter.10.cloned.1.call-start = ((), (), s32[]{:S(2)}) async-start(), calls=%async_computation.10 | async-start | bytes 6488064 | tf_op jit(solution)/shard_map/reduce_scatter | solution.py:1039
  447.9 31.6 %collective-permute-start.43 = (bf16[128,2048]{1,0:T(8,128)(2,1)}, bf16[128,2048]{1,0:T(8,128)(2,1)}, u32[]{:S(2)}, u32[]{:S(2)}) collective-permute-start(bf16[128,2048]{1,0:T(8,128)(2,1)} %slice.435), channel_id=1, source_target_pairs={{0,2},{1,3},{2,0},{3,1},{4,6},{5,7},{6,4},{7,5},{8,10},{9,11},{10,... | collective-permute-start | bytes 1572872 | tf_op jit(solution)/shard_map/ppermute | solution.py:493
  450.5 29.1 %collective-permute-start.42 = (bf16[128,2048]{1,0:T(8,128)(2,1)}, bf16[128,2048]{1,0:T(8,128)(2,1)}, u32[]{:S(2)}, u32[]{:S(2)}) collective-permute-start(bf16[128,2048]{1,0:T(8,128)(2,1)} %slice.434), channel_id=1, source_target_pairs={{0,1},{1,0},{2,3},{3,2},{4,5},{5,4},{6,7},{7,6},{8,9},{9,8},{10,11... | collective-permute-start | bytes 1572872 | tf_op jit(solution)/shard_map/ppermute | solution.py:493
  454.6 23.0 %collective-permute-start.38 = (bf16[128,2048]{1,0:T(8,128)(2,1)}, bf16[128,2048]{1,0:T(8,128)(2,1)S(1)}, u32[]{:S(2)}, u32[]{:S(2)}) collective-permute-start(bf16[128,2048]{1,0:T(8,128)(2,1)} %get-tuple-element.481), channel_id=1, source_target_pairs={{0,2},{1,3},{2,0},{3,1},{4,6},{5,7},{6,4},{7,5},{8,10},{9,11},{10,... | collective-permute-start | bytes 1572872 | tf_op jit(solution)/shard_map/ppermute | solution.py:493
  455.8 21.9 %collective-permute-start.39 = (bf16[128,2048]{1,0:T(8,128)(2,1)}, bf16[128,2048]{1,0:T(8,128)(2,1)S(1)}, u32[]{:S(2)}, u32[]{:S(2)}) collective-permute-start(bf16[128,2048]{1,0:T(8,128)(2,1)} %get-tuple-element.482), channel_id=1, source_target_pairs={{0,1},{1,0},{2,3},{3,2},{4,5},{5,4},{6,7},{7,6},{8,9},{9,8},{10,11... | collective-permute-start | bytes 1572872 | tf_op jit(solution)/shard_map/ppermute | solution.py:493
  483.2 217.1 %reduce-scatter.14.cloned.1.call-start = ((), (), s32[]{:S(2)}) async-start(), calls=%async_computation.12 | async-start | bytes 2359296 | tf_op jit(solution)/shard_map/reduce_scatter | solution.py:1039
  483.3 54.0 %collective-permute-start.48 = (bf16[256,2048]{1,0:T(8,128)(2,1)S(1)}, bf16[256,2048]{1,0:T(8,128)(2,1)}, u32[]{:S(2)}, u32[]{:S(2)}) collective-permute-start(bf16[256,2048]{1,0:T(8,128)(2,1)S(1)} %get-tuple-element.313.refs_0_), channel_id=1, source_target_pairs={{0,1},{1,0},{2,3},{3,2},{4,5},{5,4},{6,7},{7,6},{8,9},{9,8},{10,11... | collective-permute-start | bytes 3145736 | tf_op jit(solution)/shard_map/ppermute | solution.py:493
  484.5 55.6 %collective-permute-start.49 = (bf16[256,2048]{1,0:T(8,128)(2,1)S(1)}, bf16[256,2048]{1,0:T(8,128)(2,1)}, u32[]{:S(2)}, u32[]{:S(2)}) collective-permute-start(bf16[256,2048]{1,0:T(8,128)(2,1)S(1)} %get-tuple-element.313.refs_0_), channel_id=1, source_target_pairs={{0,2},{1,3},{2,0},{3,1},{4,6},{5,7},{6,4},{7,5},{8,10},{9,11},{10,... | collective-permute-start | bytes 3145736 | tf_op jit(solution)/shard_map/ppermute | solution.py:493
  485.4 57.6 %collective-permute-start.45 = (bf16[256,2048]{1,0:T(8,128)(2,1)}, bf16[256,2048]{1,0:T(8,128)(2,1)S(1)}, u32[]{:S(2)}, u32[]{:S(2)}) collective-permute-start(bf16[256,2048]{1,0:T(8,128)(2,1)} %get-tuple-element.306), channel_id=1, source_target_pairs={{0,2},{1,3},{2,0},{3,1},{4,6},{5,7},{6,4},{7,5},{8,10},{9,11},{10,... | collective-permute-start | bytes 3145736 | tf_op jit(solution)/shard_map/ppermute | solution.py:493
  486.5 56.5 %collective-permute-start.44 = (bf16[256,2048]{1,0:T(8,128)(2,1)}, bf16[256,2048]{1,0:T(8,128)(2,1)S(1)}, u32[]{:S(2)}, u32[]{:S(2)}) collective-permute-start(bf16[256,2048]{1,0:T(8,128)(2,1)} %get-tuple-element.303), channel_id=1, source_target_pairs={{0,1},{1,0},{2,3},{3,2},{4,5},{5,4},{6,7},{7,6},{8,9},{9,8},{10,11... | collective-permute-start | bytes 3145736 | tf_op jit(solution)/shard_map/ppermute | solution.py:493
  539.3 29.4 %collective-permute-start.51 = (bf16[128,2048]{1,0:T(8,128)(2,1)}, bf16[128,2048]{1,0:T(8,128)(2,1)}, u32[]{:S(2)}, u32[]{:S(2)}) collective-permute-start(bf16[128,2048]{1,0:T(8,128)(2,1)} %slice.444), channel_id=1, source_target_pairs={{0,2},{1,3},{2,0},{3,1},{4,6},{5,7},{6,4},{7,5},{8,10},{9,11},{10,... | collective-permute-start | bytes 1572872 | tf_op jit(solution)/shard_map/ppermute | solution.py:493
  542.0 26.8 %collective-permute-start.50 = (bf16[128,2048]{1,0:T(8,128)(2,1)}, bf16[128,2048]{1,0:T(8,128)(2,1)}, u32[]{:S(2)}, u32[]{:S(2)}) collective-permute-start(bf16[128,2048]{1,0:T(8,128)(2,1)} %slice.443), channel_id=1, source_target_pairs={{0,1},{1,0},{2,3},{3,2},{4,5},{5,4},{6,7},{7,6},{8,9},{9,8},{10,11... | collective-permute-start | bytes 1572872 | tf_op jit(solution)/shard_map/ppermute | solution.py:493
  544.7 19.4 %collective-permute-start.46 = (bf16[128,2048]{1,0:T(8,128)(2,1)}, bf16[128,2048]{1,0:T(8,128)(2,1)S(1)}, u32[]{:S(2)}, u32[]{:S(2)}) collective-permute-start(bf16[128,2048]{1,0:T(8,128)(2,1)} %get-tuple-element.479), channel_id=1, source_target_pairs={{0,2},{1,3},{2,0},{3,1},{4,6},{5,7},{6,4},{7,5},{8,10},{9,11},{10,... | collective-permute-start | bytes 1572872 | tf_op jit(solution)/shard_map/ppermute | solution.py:493
  546.0 21.1 %collective-permute-start.47 = (bf16[128,2048]{1,0:T(8,128)(2,1)}, bf16[128,2048]{1,0:T(8,128)(2,1)S(1)}, u32[]{:S(2)}, u32[]{:S(2)}) collective-permute-start(bf16[128,2048]{1,0:T(8,128)(2,1)} %get-tuple-element.480), channel_id=1, source_target_pairs={{0,1},{1,0},{2,3},{3,2},{4,5},{5,4},{6,7},{7,6},{8,9},{9,8},{10,11... | collective-permute-start | bytes 1572872 | tf_op jit(solution)/shard_map/ppermute | solution.py:493
  562.9 22.8 %collective-permute-start.52 = (bf16[256,2048]{1,0:T(8,128)(2,1)}, bf16[256,2048]{1,0:T(8,128)(2,1)S(1)}, u32[]{:S(2)}, u32[]{:S(2)}) collective-permute-start(bf16[256,2048]{1,0:T(8,128)(2,1)} %get-tuple-element.310), channel_id=1, source_target_pairs={{0,1},{1,0},{2,3},{3,2},{4,5},{5,4},{6,7},{7,6},{8,9},{9,8},{10,11... | collective-permute-start | bytes 3145736 | tf_op jit(solution)/shard_map/ppermute | solution.py:493
  564.0 21.7 %collective-permute-start.53 = (bf16[256,2048]{1,0:T(8,128)(2,1)}, bf16[256,2048]{1,0:T(8,128)(2,1)}, u32[]{:S(2)}, u32[]{:S(2)}) collective-permute-start(bf16[256,2048]{1,0:T(8,128)(2,1)} %get-tuple-element.311), channel_id=1, source_target_pairs={{0,2},{1,3},{2,0},{3,1},{4,6},{5,7},{6,4},{7,5},{8,10},{9,11},{10,... | collective-permute-start | bytes 3145736 | tf_op jit(solution)/shard_map/ppermute | solution.py:493
  585.7 173.8 %reduce-scatter.12.cloned.1.call-start = ((), (), s32[]{:S(2)}) async-start(), calls=%async_computation.11 | async-start | bytes 10027008 | tf_op jit(solution)/shard_map/reduce_scatter | solution.py:1039
  587.2 48.9 %collective-permute-start.54 = (bf16[256,2048]{1,0:T(8,128)(2,1)S(1)}, bf16[256,2048]{1,0:T(8,128)(2,1)S(1)}, u32[]{:S(2)}, u32[]{:S(2)}) collective-permute-start(bf16[256,2048]{1,0:T(8,128)(2,1)S(1)} %copy-done.82), channel_id=1, source_target_pairs={{0,1},{1,0},{2,3},{3,2},{4,5},{5,4},{6,7},{7,6},{8,9},{9,8},{10,11... | collective-permute-start | bytes 3145736 | tf_op jit(solution)/shard_map/ppermute | solution.py:493
  588.6 47.6 %collective-permute-start.55 = (bf16[256,2048]{1,0:T(8,128)(2,1)}, bf16[256,2048]{1,0:T(8,128)(2,1)S(1)}, u32[]{:S(2)}, u32[]{:S(2)}) collective-permute-start(bf16[256,2048]{1,0:T(8,128)(2,1)} %get-tuple-element.331), channel_id=1, source_target_pairs={{0,2},{1,3},{2,0},{3,1},{4,6},{5,7},{6,4},{7,5},{8,10},{9,11},{10,... | collective-permute-start | bytes 3145736 | tf_op jit(solution)/shard_map/ppermute | solution.py:493
  667.1 24.5 %collective-permute-start.58 = (bf16[128,2048]{1,0:T(8,128)(2,1)}, bf16[128,2048]{1,0:T(8,128)(2,1)S(1)}, u32[]{:S(2)}, u32[]{:S(2)}) collective-permute-start(bf16[128,2048]{1,0:T(8,128)(2,1)} %get-tuple-element.473), channel_id=1, source_target_pairs={{0,2},{1,3},{2,0},{3,1},{4,6},{5,7},{6,4},{7,5},{8,10},{9,11},{10,... | collective-permute-start | bytes 1572872 | tf_op jit(solution)/shard_map/ppermute | solution.py:493
  667.7 25.2 %collective-permute-start.59 = (bf16[128,2048]{1,0:T(8,128)(2,1)}, bf16[128,2048]{1,0:T(8,128)(2,1)S(1)}, u32[]{:S(2)}, u32[]{:S(2)}) collective-permute-start(bf16[128,2048]{1,0:T(8,128)(2,1)} %get-tuple-element.474), channel_id=1, source_target_pairs={{0,1},{1,0},{2,3},{3,2},{4,5},{5,4},{6,7},{7,6},{8,9},{9,8},{10,11... | collective-permute-start | bytes 1572872 | tf_op jit(solution)/shard_map/ppermute | solution.py:493
  687.3 31.4 %collective-permute-start.60 = (bf16[256,2048]{1,0:T(8,128)(2,1)}, bf16[256,2048]{1,0:T(8,128)(2,1)}, u32[]{:S(2)}, u32[]{:S(2)}) collective-permute-start(bf16[256,2048]{1,0:T(8,128)(2,1)} %get-tuple-element.339), channel_id=1, source_target_pairs={{0,1},{1,0},{2,3},{3,2},{4,5},{5,4},{6,7},{7,6},{8,9},{9,8},{10,11... | collective-permute-start | bytes 3145736 | tf_op jit(solution)/shard_map/ppermute | solution.py:493
  688.7 29.9 %collective-permute-start.61 = (bf16[256,2048]{1,0:T(8,128)(2,1)}, bf16[256,2048]{1,0:T(8,128)(2,1)}, u32[]{:S(2)}, u32[]{:S(2)}) collective-permute-start(bf16[256,2048]{1,0:T(8,128)(2,1)} %get-tuple-element.348), channel_id=1, source_target_pairs={{0,2},{1,3},{2,0},{3,1},{4,6},{5,7},{6,4},{7,5},{8,10},{9,11},{10,... | collective-permute-start | bytes 3145736 | tf_op jit(solution)/shard_map/ppermute | solution.py:493
  691.6 27.0 %collective-permute-start.56 = (bf16[128,2048]{1,0:T(8,128)(2,1)}, bf16[128,2048]{1,0:T(8,128)(2,1)}, u32[]{:S(2)}, u32[]{:S(2)}) collective-permute-start(bf16[128,2048]{1,0:T(8,128)(2,1)} %get-tuple-element.477), channel_id=1, source_target_pairs={{0,2},{1,3},{2,0},{3,1},{4,6},{5,7},{6,4},{7,5},{8,10},{9,11},{10,... | collective-permute-start | bytes 1572872 | tf_op jit(solution)/shard_map/ppermute | solution.py:493
  692.2 26.4 %collective-permute-start.57 = (bf16[128,2048]{1,0:T(8,128)(2,1)}, bf16[128,2048]{1,0:T(8,128)(2,1)}, u32[]{:S(2)}, u32[]{:S(2)}) collective-permute-start(bf16[128,2048]{1,0:T(8,128)(2,1)} %get-tuple-element.478), channel_id=1, source_target_pairs={{0,1},{1,0},{2,3},{3,2},{4,5},{5,4},{6,7},{7,6},{8,9},{9,8},{10,11... | collective-permute-start | bytes 1572872 | tf_op jit(solution)/shard_map/ppermute | solution.py:493
  (115 other events, 1154.6 us)
Sparse Core Ops, SparseCore 0:
  9.7 63.1 all-gather.3
  74.5 59.0 all-gather.5
  135.3 59.1 all-gather.7
  407.6 65.1 reduce-scatter.5
  475.0 63.2 reduce-scatter.7
  540.4 63.2 reduce-scatter.9
  605.9 34.1 reduce-scatter.13
  663.1 96.3 reduce-scatter.11
